TPU v7x, 32 devices: a whole 2x2x4 slice. The times are simulated.
32 devices in a mesh: blk: 8 (over y, x, core), tp: 4 (over z).
Axes of the slice: x: 2, y: 2, z: 4, core: 2. Of those that a mesh axis runs over, the one named last changes fastest.
Arguments:
- tokens: bfloat16 [8192, 896], P(('blk', 'tp')), may hold values from -6 to 6
- cotangent: bfloat16 [8192, 896], P(('blk', 'tp')), may hold values from -0.59765625 to 0.59765625
- weights: bfloat16 [8, 608, 3, 896], P('blk', 'tp'), may hold values from -6 to 6
- first_moment: bfloat16 [8, 608, 3, 896], P('blk', 'tp'), may hold values from -0.1796875 to 0.1796875
- second_moment: bfloat16 [8, 608, 3, 896], P('blk', 'tp'), may hold values from 0.0009994507 to 0.0099487305
Outputs:
- averaged: float32 [8, 608, 3, 896], P('blk', 'tp')
All inputs are finite; a program needn't handle non-finite values.
Results may differ from a plain program's by a relative error of at most 0.0003.
Values may be sent and summed in bfloat16 or wider, within the bound.
No kernel may reach another device: no remote copies, remote signals or barrier semaphores. Data moves between devices by JAX's collectives and lax.ppermute only.
A program may use at most 64 MiB of HBM per device.

v0:
```python
import jax
import jax.numpy as jnp
from jax import lax
from jax.sharding import PartitionSpec as P

STEP = 10


def shifted(block, axis, distance):
    devices = range(lax.axis_size(axis))
    route = [((i - distance) % len(devices), i) for i in devices]
    return lax.ppermute(block, axis, route)


def row_terms(xs, grads_out, rows, hidden_scale):
    width_scale = xs.shape[1] ** (-0.5)
    gate = (
        jnp.einsum("td,nd->tn", xs, rows[:, 0, :], preferred_element_type=jnp.float32) * width_scale
    )
    upper = (
        jnp.einsum("td,nd->tn", xs, rows[:, 1, :], preferred_element_type=jnp.float32) * width_scale
    )
    sigma = jax.nn.sigmoid(gate)
    swish = gate * sigma
    hidden = (swish * upper).astype(jnp.bfloat16)
    back = (
        jnp.einsum("td,nd->tn", grads_out, rows[:, 2, :], preferred_element_type=jnp.float32)
        * hidden_scale
    )
    dgate = (back * upper * sigma * (1.0 + gate * (1.0 - sigma))).astype(jnp.bfloat16)
    dupper = (back * swish).astype(jnp.bfloat16)
    grad_gate = jnp.einsum("tn,td->nd", dgate, xs, preferred_element_type=jnp.float32) * width_scale
    grad_upper = (
        jnp.einsum("tn,td->nd", dupper, xs, preferred_element_type=jnp.float32) * width_scale
    )
    grad_down = (
        jnp.einsum("tn,td->nd", hidden, grads_out, preferred_element_type=jnp.float32)
        * hidden_scale
    )
    return jnp.stack([grad_gate, grad_upper, grad_down], axis=1)


def on_device(tokens, cotangent, weights, first_moment, second_moment):
    own_rows = weights[0]
    local_units = own_rows.shape[0]
    hidden_scale = (local_units * lax.axis_size("tp")) ** (-0.5)
    all_tokens, all_cots = (
        lax.all_gather(tokens, "tp", axis=0, tiled=True),
        lax.all_gather(cotangent, "tp", axis=0, tiled=True),
    )
    grads = row_terms(all_tokens, all_cots, own_rows, hidden_scale)
    moment_one = 0.9 * first_moment[0].astype(jnp.float32) + 0.1 * grads
    moment_two = 0.95 * second_moment[0].astype(jnp.float32) + 0.05 * grads * grads
    correct_one = 1.0 - 0.9**STEP
    correct_two = 1.0 - 0.95**STEP
    master = own_rows.astype(jnp.float32)
    step_size = moment_one / correct_one / (jnp.sqrt(moment_two / correct_two) + 1e-08)
    updated = (master - 0.1 * (step_size + 0.1 * master))[None]
    previous = shifted(updated, "blk", 1)
    following = shifted(updated, "blk", -1)
    return (previous + updated + following) / 3.0


def solution(mesh):
    in_specs = (
        P(("blk", "tp"), None),
        P(("blk", "tp"), None),
        P("blk", "tp", None, None),
        P("blk", "tp", None, None),
        P("blk", "tp", None, None),
    )
    out_specs = P("blk", "tp", None, None)
    return jax.shard_map(
        on_device, mesh=mesh, in_specs=in_specs, out_specs=out_specs, check_vma=False
    )
```

profile of v0, /device:TPU:0, one launch (start us, length us, event | category | flops | bytes accessed | tf_op | source)
XLA Modules:
  0.0 148.7 jit_solution(17989361098405296293)
XLA Ops:
  6.5 0.0 all-gather.5.cloned.1.call-start
  6.5 0.7 all-gather.5.cloned.1.call-update
  7.3 0.0 copy-start.1
  7.3 0.0 all-gather.3.cloned.1.call-start
  7.3 0.7 all-gather.3.cloned.1.call-update
  8.0 45.0 %all-gather.5.cloned.1.call-done = bf16[1024,896]{1,0:T(8,128)(2,1)} async-done(((bf16[256,896]{1,0:T(8,128)(2,1)}), bf16[1024,896]{1,0:T(8,128)(2,1)}) %all-gather.5.cloned.1.call-update) | async-done | bytes 1835024 | tf_op jit(solution)/shard_map/all_gather | solution.py:48
  53.1 0.0 copy-start
  53.1 2.5 %convolution_multiply_fusion.1 = f32[1024,152]{0,1:T(8,128)S(1)} fusion(bf16[1024,896]{1,0:T(8,128)(2,1)} %all-gather.5.cloned.1.call-done, bf16[152,3,896]{2,0,1:T(8,128)(2,1)} %bitcast.22), kind=kOutput, calls=%fused_computation.13 | convolution fusion | flops 279076864 | bytes 2729984 | tf_op jit(solution)/shard_map/td,nd->tn/dot_general | solution.py:21
  55.5 0.0 copy-done.1
  55.5 0.0 copy-done
  55.5 1.7 %convolution_multiply_fusion = f32[1024,152]{0,1:T(8,128)} fusion(bf16[1024,896]{1,0:T(8,128)(2,1)S(1)} %copy-done, bf16[152,3,896]{2,0,1:T(8,128)(2,1)S(1)} %bitcast.23), kind=kOutput, calls=%fused_computation.12 | convolution fusion | flops 279076864 | bytes 2729984 | tf_op jit(solution)/shard_map/td,nd->tn/dot_general | solution.py:18
  57.2 37.7 %all-gather.3.cloned.1.call-done = bf16[1024,896]{1,0:T(8,128)(2,1)} async-done(((bf16[256,896]{1,0:T(8,128)(2,1)}), bf16[1024,896]{1,0:T(8,128)(2,1)}) %all-gather.3.cloned.1.call-update) | async-done | bytes 1835024 | tf_op jit(solution)/shard_map/all_gather | solution.py:49
  94.9 0.0 copy-start.2
  94.9 0.0 copy-start.5
  94.9 2.5 %convolution_multiply_fusion.2 = f32[1024,152]{0,1:T(8,128)S(1)} fusion(bf16[1024,896]{1,0:T(8,128)(2,1)} %all-gather.3.cloned.1.call-done, bf16[152,3,896]{2,0,1:T(8,128)(2,1)S(1)} %bitcast.24), kind=kOutput, calls=%fused_computation.14 | convolution fusion | flops 279076864 | bytes 2729984 | tf_op jit(solution)/shard_map/td,nd->tn/dot_general | solution.py:27
  97.4 0.0 copy-done.2
  97.4 0.0 copy-done.5
  97.4 0.6 fusion.7
  98.0 0.6 fusion.8
  98.6 0.0 copy-start.3
  98.6 0.0 copy-start.4
  98.6 0.6 fusion.9
  99.2 0.5 copy-done.3
  99.7 0.2 copy-done.4
  100.0 1.4 convert_subtract_fusion
  101.4 1.9 %collective-permute-start.1 = (f32[1,152,3,896]{3,1,2,0:T(8,128)S(1)}, f32[1,152,3,896]{3,1,2,0:T(8,128)S(1)}, u32[]{:S(2)}, u32[]{:S(2)}) collective-permute-start(f32[1,152,3,896]{3,1,2,0:T(8,128)S(1)} %convert_subtract_fusion), channel_id=1, source_target_pairs={{4,0},{8,4},{12,8},{16,12},{20,16},{24,20},{28,24},{0,28},{5,1},{9... | collective-permute-start | bytes 4902920 | tf_op jit(solution)/shard_map/ppermute | solution.py:12
  103.2 0.0 collective-permute-start
  103.2 35.2 %collective-permute-done.1 = f32[1,152,3,896]{3,1,2,0:T(8,128)S(1)} collective-permute-done((f32[1,152,3,896]{3,1,2,0:T(8,128)S(1)}, f32[1,152,3,896]{3,1,2,0:T(8,128)S(1)}, u32[]{:S(2)}, u32[]{:S(2)}) %collective-permute-start.1) | collective-permute-done | bytes 1634336 | tf_op jit(solution)/shard_map/ppermute | solution.py:12
  138.5 1.9 %collective-permute-done = f32[1,152,3,896]{3,1,2,0:T(8,128)S(1)} collective-permute-done((f32[1,152,3,896]{3,1,2,0:T(8,128)S(1)}, f32[1,152,3,896]{3,1,2,0:T(8,128)S(1)}, u32[]{:S(2)}, u32[]{:S(2)}) %collective-permute-start) | collective-permute-done | bytes 1634336 | tf_op jit(solution)/shard_map/ppermute | solution.py:12
  140.3 1.5 %add_multiply_fusion = f32[1,152,3,896]{3,1,2,0:T(8,128)} fusion(f32[1,152,3,896]{3,1,2,0:T(8,128)S(1)} %collective-permute-done.1, f32[1,152,3,896]{3,1,2,0:T(8,128)S(1)} %collective-permute-done, f32[1,152,3,896]{3,1,2,0:T(8,128)S(1)} %convert_subtract_fusion), kind=kLoop, calls=%fused_computation.11 | loop fusion | flops 1225728 | bytes 6537216 | tf_op jit(solution)/shard_map/div | solution.py:61
Async XLA Ops:
  6.5 46.5 %all-gather.5.cloned.1.call-start = ((), (), s32[]{:S(2)}) async-start(), calls=%async_computation.1 | async-start | bytes 2293760 | tf_op jit(solution)/shard_map/all_gather | solution.py:48
  7.3 48.3 %copy-start.1 = (bf16[1,152,3,896]{3,1,2,0:T(8,128)(2,1)S(1)}, bf16[1,152,3,896]{3,1,2,0:T(8,128)(2,1)}, u32[]{:S(2)}) copy-start(bf16[1,152,3,896]{3,1,2,0:T(8,128)(2,1)} %param.7) | copy-start | bytes 2451460
  7.3 87.7 %all-gather.3.cloned.1.call-start = ((), (), s32[]{:S(2)}) async-start(), calls=%async_computation | async-start | bytes 2293760 | tf_op jit(solution)/shard_map/all_gather | solution.py:49
  53.1 2.5 %copy-start = (bf16[1024,896]{1,0:T(8,128)(2,1)S(1)}, bf16[1024,896]{1,0:T(8,128)(2,1)}, u32[]{:S(2)}) copy-start(bf16[1024,896]{1,0:T(8,128)(2,1)} %all-gather.5.cloned.1.call-done) | copy-start | bytes 5505028
  94.9 2.5 %copy-start.2 = (bf16[1024,896]{1,0:T(8,128)(2,1)S(1)}, bf16[1024,896]{1,0:T(8,128)(2,1)}, u32[]{:S(2)}) copy-start(bf16[1024,896]{1,0:T(8,128)(2,1)} %all-gather.3.cloned.1.call-done) | copy-start | bytes 5505028
  94.9 2.5 %copy-start.5 = (f32[1024,152]{0,1:T(8,128)S(1)}, f32[1024,152]{0,1:T(8,128)}, u32[]{:S(2)}) copy-start(f32[1024,152]{0,1:T(8,128)} %convolution_multiply_fusion) | copy-start | bytes 1867780
  98.6 1.1 copy-start.3
  98.6 1.4 copy-start.4
  101.4 37.1 %collective-permute-start.1 = (f32[1,152,3,896]{3,1,2,0:T(8,128)S(1)}, f32[1,152,3,896]{3,1,2,0:T(8,128)S(1)}, u32[]{:S(2)}, u32[]{:S(2)}) collective-permute-start(f32[1,152,3,896]{3,1,2,0:T(8,128)S(1)} %convert_subtract_fusion), channel_id=1, source_target_pairs={{4,0},{8,4},{12,8},{16,12},{20,16},{24,20},{28,24},{0,28},{5,1},{9... | collective-permute-start | bytes 4902920 | tf_op jit(solution)/shard_map/ppermute | solution.py:12
  103.2 37.1 %collective-permute-start = (f32[1,152,3,896]{3,1,2,0:T(8,128)S(1)}, f32[1,152,3,896]{3,1,2,0:T(8,128)S(1)}, u32[]{:S(2)}, u32[]{:S(2)}) collective-permute-start(f32[1,152,3,896]{3,1,2,0:T(8,128)S(1)} %convert_subtract_fusion), channel_id=1, source_target_pairs={{28,0},{0,4},{4,8},{8,12},{12,16},{16,20},{20,24},{24,28},{29,1},{... | collective-permute-start | bytes 4902920 | tf_op jit(solution)/shard_map/ppermute | solution.py:12
Sparse Core Ops, SparseCore 0:
  8.9 44.0 all-gather.4
  54.6 40.2 all-gather.2
where the time goes:
time: 149 us
  waiting for transfers between devices  121 us (81%)
  between operations  13.5 us (9%)
  matrix products  8.34 us (6%)
  other arithmetic  2.94 us (2%)
  starting transfers between devices  1.91 us (1%)
    all_gather x1, waiting for transfers between devices, on_device(): lax.all_gather(tokens, 'tp', axis=0, tiled=True)  45 us
    all_gather x1, waiting for transfers between devices, on_device(): lax.all_gather(cotangent, 'tp', axis=0, tiled=True)  37.7 us
    ppermute x2, waiting for transfers between devices, shifted(): return lax.ppermute(block, axis, route)  37.1 us
  transfers between devices with their start and end apart: 4, of which 4 were waited for; matrix products, arithmetic and copies ran while one was open for 3% of the time, Pallas kernels for 0%

commit v1 on v0

v1 whole, which is shorter than its diff:
```python
import jax
import jax.numpy as jnp
from jax import lax
from jax.sharding import PartitionSpec as P

STEP = 10
CORRECT_ONE = 1.0 - 0.9**STEP
CORRECT_TWO = 1.0 - 0.95**STEP


def shifted(block, axis, distance):
    count = lax.axis_size(axis)
    return lax.ppermute(block, axis, [((i - distance) % count, i) for i in range(count)])


def adam_step(moment_one, moment_two):
    return moment_one / CORRECT_ONE / (jnp.sqrt(moment_two / CORRECT_TWO) + 1e-08)


def unit_grads(xs, cots, rows, hidden_scale):
    width_scale = xs.shape[1] ** (-0.5)

    def into_units(values, matrix):
        return jnp.einsum("td,nd->nt", values, matrix, preferred_element_type=jnp.float32)

    def over_tokens(terms, values):
        return jnp.einsum("nt,td->nd", terms, values, preferred_element_type=jnp.float32)

    gate = into_units(xs, rows[0]) * width_scale
    upper = into_units(xs, rows[1]) * width_scale
    sigma = jax.nn.sigmoid(gate)
    swish = gate * sigma
    hidden = (swish * upper).astype(jnp.bfloat16)
    back = into_units(cots, rows[2]) * hidden_scale
    dgate = (back * upper * sigma * (1.0 + gate * (1.0 - sigma))).astype(jnp.bfloat16)
    dupper = (back * swish).astype(jnp.bfloat16)
    return (
        over_tokens(dgate, xs) * width_scale,
        over_tokens(dupper, xs) * width_scale,
        over_tokens(hidden, cots) * hidden_scale,
    )


def line_of_four(tokens, cots, rows, hidden_scale):
    inward = [(0, 1), (3, 2)]
    middle = [(1, 2), (2, 1)]
    outward = [(1, 0), (2, 3)]
    units = rows.shape[1]

    def send(block, route):
        return lax.ppermute(block, "tp", route)

    outer_x = send(tokens, inward)
    inner_x = send(tokens, middle)
    outer_g = send(cots, inward)
    inner_g = send(cots, middle)
    far_x = send(outer_x, middle)
    far_g = send(outer_g, middle)
    outer_rows = send(rows, inward)
    both_rows = jnp.concatenate([rows, outer_rows], axis=1)
    near = unit_grads(
        jnp.concatenate([tokens, outer_x, inner_x]),
        jnp.concatenate([cots, outer_g, inner_g]),
        both_rows,
        hidden_scale,
    )
    far = unit_grads(far_x, far_g, both_rows, hidden_scale)
    place = lax.axis_index("tp")
    inside = (place == 1) | (place == 2)
    grads = []
    for k in (2, 1, 0):
        whole = near[k] + far[k]
        arrived = send(whole[units:].astype(jnp.bfloat16), outward)
        grads.append(jnp.where(inside, whole[:units], arrived.astype(jnp.float32)))
    return grads[::-1]


def gathered(tokens, cots, rows, hidden_scale):
    return unit_grads(
        lax.all_gather(tokens, "tp", axis=0, tiled=True),
        lax.all_gather(cots, "tp", axis=0, tiled=True),
        rows,
        hidden_scale,
    )


def on_device(tokens, cotangent, weights, first_moment, second_moment):
    rows = jnp.swapaxes(weights[0], 0, 1)
    hidden_scale = (rows.shape[1] * lax.axis_size("tp")) ** (-0.5)
    moment_one = 0.9 * jnp.swapaxes(first_moment[0], 0, 1).astype(jnp.float32)
    moment_two = 0.95 * jnp.swapaxes(second_moment[0], 0, 1).astype(jnp.float32)
    master = rows.astype(jnp.float32)
    still_step = adam_step(moment_one, moment_two)
    still = master - 0.1 * (still_step + 0.1 * master)
    still_sum = still + shifted(still, "blk", 1) + shifted(still, "blk", -1)
    plan = line_of_four if lax.axis_size("tp") == 4 else gathered
    grads = plan(tokens, cotangent, rows, hidden_scale)
    parts = [None] * 3
    for k in (2, 1, 0):
        step = adam_step(
            moment_one[k] + 0.1 * grads[k], moment_two[k] + 0.05 * grads[k] * grads[k]
        )
        change = 0.1 * (still_step[k] - step)
        sent = change.astype(jnp.bfloat16)
        around = shifted(sent, "blk", 1).astype(jnp.float32) + shifted(sent, "blk", -1).astype(
            jnp.float32
        )
        parts[k] = (still_sum[k] + change + around) / 3.0
    return jnp.swapaxes(jnp.stack(parts), 0, 1)[None]


def solution(mesh):
    in_specs = (
        P(("blk", "tp"), None),
        P(("blk", "tp"), None),
        P("blk", "tp", None, None),
        P("blk", "tp", None, None),
        P("blk", "tp", None, None),
    )
    out_specs = P("blk", "tp", None, None)
    return jax.shard_map(
        on_device, mesh=mesh, in_specs=in_specs, out_specs=out_specs, check_vma=False
    )
```

time: 149 us -> 93.2 us (0.63); the launches traced: 149 us -> 91.4 us
  waiting for transfers between devices: 121 us -> 46.3 us
  starting transfers between devices: 1.91 us -> 27 us
  between operations: 13.5 us -> 0.35 us
  other arithmetic: 2.94 us -> 6.75 us
  local copies, waits for them, and re-layouts: 0.76 us -> 4.47 us
  matrix products: 8.34 us -> 6.45 us
    all_gather x2 -> x0, waiting for transfers between devices: 82.8 us -> none  [the longest x1 45 us: on_device(): lax.all_gather(tokens, 'tp', axis=0, tiled=True)]
    ppermute x2 -> x18, starting transfers between devices: 1.87 us -> 27 us  [the longest x10 19 us: send(): return lax.ppermute(block, 'tp', route)]
    ppermute x2 -> x18, waiting for transfers between devices: 37.1 us -> 46.3 us  [the longest x10 32.4 us: send(): return lax.ppermute(block, 'tp', route)]
    concatenate x0 -> x2, local copies, waits for them, and re-layouts: none -> 2.13 us  [the longest x1 1.07 us: line_of_four(): jnp.concatenate([cots, outer_g, inner_g])]
    dot_general x6 -> x12, matrix products: 8.34 us -> 6.45 us  [the longest x6 3.31 us: over_tokens(): jnp.einsum('nt,td->nd', terms, values, preferred_element_type=jnp.float32)]
  transfers between devices with their start and end apart: 4 -> 18, of which waited for: 4 -> 9; matrix products, arithmetic and copies ran while one was open for 3% -> 17% of each run, Pallas kernels for 0% -> 0%
where the time goes in v1:
time: 93.2 us; the launch traced here: 91.4 us
  waiting for transfers between devices  46.3 us (50%)
  starting transfers between devices  27 us (29%)
  other arithmetic  6.75 us (7%)
  matrix products  6.45 us (7%)
  local copies, waits for them, and re-layouts  4.47 us (5%)
    ppermute x10, waiting for transfers between devices, send(): return lax.ppermute(block, 'tp', route)  32.4 us
    ppermute x10, starting transfers between devices, send(): return lax.ppermute(block, 'tp', route)  19 us
    ppermute x8, waiting for transfers between devices, shifted(): lax.ppermute(block, axis, [((i - distance) % count, i) for i in range(cou...  13.9 us
    ppermute x8, starting transfers between devices, shifted(): lax.ppermute(block, axis, [((i - distance) % count, i) for i in range(cou...  8.08 us
    dot_general x6, matrix products, over_tokens(): jnp.einsum('nt,td->nd', terms, values, preferred_element_type=jnp.float32)  3.31 us
    dot_general x6, matrix products, into_units(): jnp.einsum('td,nd->nt', values, matrix, preferred_element_type=jnp.float32)  3.14 us
    sub x1, other arithmetic, on_device(): still = master - 0.1 * (still_step + 0.1 * master)  2.65 us
    unnamed x14, local copies, waits for them, and re-layouts  2.24 us
  transfers between devices with their start and end apart: 18, of which 9 were waited for; matrix products, arithmetic and copies ran while one was open for 17% of the time, Pallas kernels for 0%

profile of v1, /device:TPU:0, one launch (start us, length us, event | category | flops | bytes accessed | tf_op | source)
XLA Modules:
  0.0 91.4 jit_solution(6629440089962931387)
XLA Ops:
  0.0 5.7 %collective-permute-start.5 = (bf16[256,896]{1,0:T(8,128)(2,1)}, bf16[256,896]{1,0:T(8,128)(2,1)}, u32[]{:S(2)}, u32[]{:S(2)}) collective-permute-start(bf16[256,896]{1,0:T(8,128)(2,1)} %param.5), channel_id=1, source_target_pairs={{0,1},{3,2},{4,5},{7,6},{8,9},{11,10},{12,13},{15,14},{16,17},{19,... | collective-permute-start | bytes 1376264 | tf_op jit(solution)/shard_map/ppermute | solution.py:51
  5.7 1.5 %collective-permute-start.6 = (bf16[256,896]{1,0:T(8,128)(2,1)}, bf16[256,896]{1,0:T(8,128)(2,1)}, u32[]{:S(2)}, u32[]{:S(2)}) collective-permute-start(bf16[256,896]{1,0:T(8,128)(2,1)} %param.5), channel_id=1, source_target_pairs={{1,2},{2,1},{5,6},{6,5},{9,10},{10,9},{13,14},{14,13},{17,18},{18,... | collective-permute-start | bytes 1376264 | tf_op jit(solution)/shard_map/ppermute | solution.py:51
  7.2 3.3 %collective-permute-start.3 = (bf16[256,896]{1,0:T(8,128)(2,1)}, bf16[256,896]{1,0:T(8,128)(2,1)}, u32[]{:S(2)}, u32[]{:S(2)}) collective-permute-start(bf16[256,896]{1,0:T(8,128)(2,1)} %param.6), channel_id=1, source_target_pairs={{0,1},{3,2},{4,5},{7,6},{8,9},{11,10},{12,13},{15,14},{16,17},{19,... | collective-permute-start | bytes 1376264 | tf_op jit(solution)/shard_map/ppermute | solution.py:51
  10.5 1.4 %collective-permute-start.4 = (bf16[256,896]{1,0:T(8,128)(2,1)}, bf16[256,896]{1,0:T(8,128)(2,1)}, u32[]{:S(2)}, u32[]{:S(2)}) collective-permute-start(bf16[256,896]{1,0:T(8,128)(2,1)} %param.6), channel_id=1, source_target_pairs={{1,2},{2,1},{5,6},{6,5},{9,10},{10,9},{13,14},{14,13},{17,18},{18,... | collective-permute-start | bytes 1376264 | tf_op jit(solution)/shard_map/ppermute | solution.py:51
  11.9 1.6 %collective-permute-start.2 = (bf16[3,152,896]{2,1,0:T(8,128)(2,1)}, bf16[3,152,896]{2,1,0:T(8,128)(2,1)S(1)}, u32[]{:S(2)}, u32[]{:S(2)}) collective-permute-start(bf16[3,152,896]{2,1,0:T(8,128)(2,1)} %bitcast.157), channel_id=1, source_target_pairs={{0,1},{3,2},{4,5},{7,6},{8,9},{11,10},{12,13},{15,14},{16,17},{19,... | collective-permute-start | bytes 2451464 | tf_op jit(solution)/shard_map/ppermute | solution.py:51
  13.6 2.6 %convert_subtract_fusion = f32[3,152,896]{2,1,0:T(8,128)S(1)} fusion(bf16[1,152,3,896]{3,1,2,0:T(8,128)(2,1)} %param.7, bf16[1,152,3,896]{3,1,2,0:T(8,128)(2,1)} %param.9, bf16[1,152,3,896]{3,1,2,0:T(8,128)(2,1)} %param.8), kind=kLoop, calls=%fused_computation.4 | loop fusion | flops 4494336 | bytes 4085760 | tf_op jit(solution)/shard_map/sub | solution.py:94
  16.4 0.1 collective-permute-start
  16.4 1.1 %constant_dynamic-update-slice_fusion.4 = bf16[768,896]{1,0:T(8,128)(2,1)S(1)} fusion(bf16[768,896]{1,0:T(8,128)(2,1)S(1)} %constant_dynamic-update-slice_fusion.5, bf16[256,896]{1,0:T(8,128)(2,1)} %collective-permute-done.5), kind=kLoop, calls=%fused_computation.116 | loop fusion | bytes 917504
  17.5 2.7 %collective-permute-start.1 = (f32[3,152,896]{2,1,0:T(8,128)S(1)}, f32[3,152,896]{2,1,0:T(8,128)S(1)}, u32[]{:S(2)}, u32[]{:S(2)}) collective-permute-start(f32[3,152,896]{2,1,0:T(8,128)S(1)} %convert_subtract_fusion), channel_id=1, source_target_pairs={{4,0},{8,4},{12,8},{16,12},{20,16},{24,20},{28,24},{0,28},{5,1},{9... | collective-permute-start | bytes 4902920 | tf_op jit(solution)/shard_map/ppermute | solution.py:13
  20.2 1.1 %constant_dynamic-update-slice_fusion.3 = bf16[768,896]{1,0:T(8,128)(2,1)S(1)} fusion(bf16[768,896]{1,0:T(8,128)(2,1)S(1)} %constant_dynamic-update-slice_fusion.4, bf16[256,896]{1,0:T(8,128)(2,1)} %collective-permute-done.6), kind=kLoop, calls=%fused_computation.115 | loop fusion | bytes 917504 | tf_op jit(solution)/shard_map/concatenate | solution.py:62
  21.3 4.7 %collective-permute-done.3 = bf16[256,896]{1,0:T(8,128)(2,1)} collective-permute-done((bf16[256,896]{1,0:T(8,128)(2,1)}, bf16[256,896]{1,0:T(8,128)(2,1)}, u32[]{:S(2)}, u32[]{:S(2)}) %collective-permute-start.3) | collective-permute-done | bytes 458784 | tf_op jit(solution)/shard_map/ppermute | solution.py:51
  26.0 0.7 collective-permute-start.8
  26.7 1.1 %constant_dynamic-update-slice_fusion.1 = bf16[768,896]{1,0:T(8,128)(2,1)S(1)} fusion(bf16[768,896]{1,0:T(8,128)(2,1)S(1)} %constant_dynamic-update-slice_fusion.2, bf16[256,896]{1,0:T(8,128)(2,1)} %collective-permute-done.3), kind=kLoop, calls=%fused_computation.113 | loop fusion | bytes 917504
  27.7 0.7 collective-permute-start.7
  28.4 1.1 %constant_dynamic-update-slice_fusion = bf16[768,896]{1,0:T(8,128)(2,1)S(1)} fusion(bf16[768,896]{1,0:T(8,128)(2,1)S(1)} %constant_dynamic-update-slice_fusion.1, bf16[256,896]{1,0:T(8,128)(2,1)} %collective-permute-done.4), kind=kLoop, calls=%fused_computation.112 | loop fusion | bytes 917504 | tf_op jit(solution)/shard_map/concatenate | solution.py:63
  29.5 12.8 %collective-permute-done.2 = bf16[3,152,896]{2,1,0:T(8,128)(2,1)S(1)} collective-permute-done((bf16[3,152,896]{2,1,0:T(8,128)(2,1)}, bf16[3,152,896]{2,1,0:T(8,128)(2,1)S(1)}, u32[]{:S(2)}, u32[]{:S(2)}) %collective-permute-start.2) | collective-permute-done | bytes 817184 | tf_op jit(solution)/shard_map/ppermute | solution.py:51
  42.3 0.7 convolution_multiply_fusion
  43.0 0.7 convolution_multiply_fusion.1
  43.7 0.7 convolution_multiply_fusion.2
  44.4 0.8 fusion.58
  45.2 0.7 fusion.56
  46.0 0.7 fusion.57
  46.7 0.4 convolution_multiply_fusion.3
  47.1 0.4 convolution_multiply_fusion.5
  47.4 0.3 fusion.9
  47.8 1.3 %collective-permute-start.12 = (bf16[152,896]{1,0:T(8,128)(2,1)S(1)}, bf16[152,896]{1,0:T(8,128)(2,1)S(1)}, u32[]{:S(2)}, u32[]{:S(2)}) collective-permute-start(bf16[152,896]{1,0:T(8,128)(2,1)S(1)} %slice.239), channel_id=1, source_target_pairs={{1,0},{2,3},{5,4},{6,7},{9,8},{10,11},{13,12},{14,15},{17,16},{18,... | collective-permute-start | bytes 817160 | tf_op jit(solution)/shard_map/ppermute | solution.py:51
  49.1 0.4 convolution_multiply_fusion.4
  49.5 0.3 fusion.8
  49.9 1.4 %collective-permute-start.15 = (bf16[152,896]{1,0:T(8,128)(2,1)S(1)}, bf16[152,896]{1,0:T(8,128)(2,1)S(1)}, u32[]{:S(2)}, u32[]{:S(2)}) collective-permute-start(bf16[152,896]{1,0:T(8,128)(2,1)S(1)} %slice.238), channel_id=1, source_target_pairs={{1,0},{2,3},{5,4},{6,7},{9,8},{10,11},{13,12},{14,15},{17,16},{18,... | collective-permute-start | bytes 817160 | tf_op jit(solution)/shard_map/ppermute | solution.py:51
  51.3 0.4 fusion.10
  51.8 1.3 %collective-permute-start.9 = (bf16[152,896]{1,0:T(8,128)(2,1)S(1)}, bf16[152,896]{1,0:T(8,128)(2,1)S(1)}, u32[]{:S(2)}, u32[]{:S(2)}) collective-permute-start(bf16[152,896]{1,0:T(8,128)(2,1)S(1)} %slice.240), channel_id=1, source_target_pairs={{1,0},{2,3},{5,4},{6,7},{9,8},{10,11},{13,12},{14,15},{17,16},{18,... | collective-permute-start | bytes 817160 | tf_op jit(solution)/shard_map/ppermute | solution.py:51
  53.1 0.9 fusion.3
  54.0 6.1 %collective-permute-done.12 = bf16[152,896]{1,0:T(8,128)(2,1)S(1)} collective-permute-done((bf16[152,896]{1,0:T(8,128)(2,1)S(1)}, bf16[152,896]{1,0:T(8,128)(2,1)S(1)}, u32[]{:S(2)}, u32[]{:S(2)}) %collective-permute-start.12) | collective-permute-done | bytes 272416 | tf_op jit(solution)/shard_map/ppermute | solution.py:51
  60.1 5.8 %collective-permute-done.15 = bf16[152,896]{1,0:T(8,128)(2,1)S(1)} collective-permute-done((bf16[152,896]{1,0:T(8,128)(2,1)S(1)}, bf16[152,896]{1,0:T(8,128)(2,1)S(1)}, u32[]{:S(2)}, u32[]{:S(2)}) %collective-permute-start.15) | collective-permute-done | bytes 272416 | tf_op jit(solution)/shard_map/ppermute | solution.py:51
  65.9 2.9 %collective-permute-done.9 = bf16[152,896]{1,0:T(8,128)(2,1)S(1)} collective-permute-done((bf16[152,896]{1,0:T(8,128)(2,1)S(1)}, bf16[152,896]{1,0:T(8,128)(2,1)S(1)}, u32[]{:S(2)}, u32[]{:S(2)}) %collective-permute-start.9) | collective-permute-done | bytes 272416 | tf_op jit(solution)/shard_map/ppermute | solution.py:51
  68.8 1.2 %fusion.77 = (bf16[152,896]{1,0:T(8,128)(2,1)S(1)}, f32[152,896]{1,0:T(8,128)S(1)}, bf16[152,896]{1,0:T(8,128)(2,1)S(1)}, f32[152,896]{1,0:T(8,128)S(1)}, bf16[1...) fusion(f32[3,152,896]{2,1,0:T(8,128)S(1)} %get-tuple-element.19, bf16[152,896]{1,0:T(8,128)(2,1)S(1)} %collective-permute-done.9, ...), kind=kLoop, calls=%fused_computation.124 | loop fusion | flops 5720064 | bytes 9805825 | tf_op jit(solution)/shard_map/convert_element_type | solution.py:104
  70.0 0.1 collective-permute-start.10
  70.1 2.6 %collective-permute-start.11 = (bf16[152,896]{1,0:T(8,128)(2,1)S(1)}, bf16[152,896]{1,0:T(8,128)(2,1)S(1)}, u32[]{:S(2)}, u32[]{:S(2)}) collective-permute-start(bf16[152,896]{1,0:T(8,128)(2,1)S(1)} %get-tuple-element.5), channel_id=1, source_target_pairs={{4,0},{8,4},{12,8},{16,12},{20,16},{24,20},{28,24},{0,28},{5,1},{9... | collective-permute-start | bytes 817160 | tf_op jit(solution)/shard_map/ppermute | solution.py:13
  72.7 5.2 %collective-permute-done.10 = bf16[152,896]{1,0:T(8,128)(2,1)S(1)} collective-permute-done((bf16[152,896]{1,0:T(8,128)(2,1)S(1)}, bf16[152,896]{1,0:T(8,128)(2,1)S(1)}, u32[]{:S(2)}, u32[]{:S(2)}) %collective-permute-start.10) | collective-permute-done | bytes 272416 | tf_op jit(solution)/shard_map/ppermute | solution.py:13
  77.9 0.5 collective-permute-start.16
  78.4 2.1 %collective-permute-start.17 = (bf16[152,896]{1,0:T(8,128)(2,1)S(1)}, bf16[152,896]{1,0:T(8,128)(2,1)S(1)}, u32[]{:S(2)}, u32[]{:S(2)}) collective-permute-start(bf16[152,896]{1,0:T(8,128)(2,1)S(1)} %get-tuple-element.11), channel_id=1, source_target_pairs={{4,0},{8,4},{12,8},{16,12},{20,16},{24,20},{28,24},{0,28},{5,1},{9... | collective-permute-start | bytes 817160 | tf_op jit(solution)/shard_map/ppermute | solution.py:13
  80.6 0.3 add_add_fusion
  80.9 2.9 %collective-permute-done.13 = bf16[152,896]{1,0:T(8,128)(2,1)S(1)} collective-permute-done((bf16[152,896]{1,0:T(8,128)(2,1)S(1)}, bf16[152,896]{1,0:T(8,128)(2,1)S(1)}, u32[]{:S(2)}, u32[]{:S(2)}) %collective-permute-start.13) | collective-permute-done | bytes 272416 | tf_op jit(solution)/shard_map/ppermute | solution.py:13
  83.7 1.8 %collective-permute-done.14 = bf16[152,896]{1,0:T(8,128)(2,1)S(1)} collective-permute-done((bf16[152,896]{1,0:T(8,128)(2,1)S(1)}, bf16[152,896]{1,0:T(8,128)(2,1)S(1)}, u32[]{:S(2)}, u32[]{:S(2)}) %collective-permute-start.14) | collective-permute-done | bytes 272416 | tf_op jit(solution)/shard_map/ppermute | solution.py:13
  85.6 4.0 %collective-permute-done.16 = bf16[152,896]{1,0:T(8,128)(2,1)S(1)} collective-permute-done((bf16[152,896]{1,0:T(8,128)(2,1)S(1)}, bf16[152,896]{1,0:T(8,128)(2,1)S(1)}, u32[]{:S(2)}, u32[]{:S(2)}) %collective-permute-start.16) | collective-permute-done | bytes 272416 | tf_op jit(solution)/shard_map/ppermute | solution.py:13
  89.6 0.0 collective-permute-done.17
  89.6 0.4 fusion.52
  90.1 1.3 %maximum_bitcast_fusion = f32[1,152,3,896]{3,1,2,0:T(8,128)} fusion(f32[1,152,896]{2,1,0:T(8,128)S(1)} %get-tuple-element.16, f32[1,152,896]{2,1,0:T(8,128)S(1)} %get-tuple-element.17, f32[1,152,896]{2,1,0:T(8,128)S(1)} %get-tuple-element.15), kind=kLoop, calls=%fused_computation.18 | loop fusion | flops 817152 | bytes 3268608 | tf_op jit(solution)/shard_map/broadcast_in_dim | solution.py:109
  (25 shorter events, 0.2 us)
Async XLA Ops:
  0.0 16.4 %collective-permute-start.5 = (bf16[256,896]{1,0:T(8,128)(2,1)}, bf16[256,896]{1,0:T(8,128)(2,1)}, u32[]{:S(2)}, u32[]{:S(2)}) collective-permute-start(bf16[256,896]{1,0:T(8,128)(2,1)} %param.5), channel_id=1, source_target_pairs={{0,1},{3,2},{4,5},{7,6},{8,9},{11,10},{12,13},{15,14},{16,17},{19,... | collective-permute-start | bytes 1376264 | tf_op jit(solution)/shard_map/ppermute | solution.py:51
  5.7 11.8 %collective-permute-start.6 = (bf16[256,896]{1,0:T(8,128)(2,1)}, bf16[256,896]{1,0:T(8,128)(2,1)}, u32[]{:S(2)}, u32[]{:S(2)}) collective-permute-start(bf16[256,896]{1,0:T(8,128)(2,1)} %param.5), channel_id=1, source_target_pairs={{1,2},{2,1},{5,6},{6,5},{9,10},{10,9},{13,14},{14,13},{17,18},{18,... | collective-permute-start | bytes 1376264 | tf_op jit(solution)/shard_map/ppermute | solution.py:51
  7.2 18.8 %collective-permute-start.3 = (bf16[256,896]{1,0:T(8,128)(2,1)}, bf16[256,896]{1,0:T(8,128)(2,1)}, u32[]{:S(2)}, u32[]{:S(2)}) collective-permute-start(bf16[256,896]{1,0:T(8,128)(2,1)} %param.6), channel_id=1, source_target_pairs={{0,1},{3,2},{4,5},{7,6},{8,9},{11,10},{12,13},{15,14},{16,17},{19,... | collective-permute-start | bytes 1376264 | tf_op jit(solution)/shard_map/ppermute | solution.py:51
  10.5 17.2 %collective-permute-start.4 = (bf16[256,896]{1,0:T(8,128)(2,1)}, bf16[256,896]{1,0:T(8,128)(2,1)}, u32[]{:S(2)}, u32[]{:S(2)}) collective-permute-start(bf16[256,896]{1,0:T(8,128)(2,1)} %param.6), channel_id=1, source_target_pairs={{1,2},{2,1},{5,6},{6,5},{9,10},{10,9},{13,14},{14,13},{17,18},{18,... | collective-permute-start | bytes 1376264 | tf_op jit(solution)/shard_map/ppermute | solution.py:51
  11.9 4.3 %copy-start.3 = (bf16[256,896]{1,0:T(8,128)(2,1)S(1)}, bf16[256,896]{1,0:T(8,128)(2,1)}, u32[]{:S(2)}) copy-start(bf16[256,896]{1,0:T(8,128)(2,1)} %param.5) | copy-start | bytes 1376260
  11.9 4.4 %copy-start.4 = (bf16[256,896]{1,0:T(8,128)(2,1)S(1)}, bf16[256,896]{1,0:T(8,128)(2,1)}, u32[]{:S(2)}) copy-start(bf16[256,896]{1,0:T(8,128)(2,1)} %param.6) | copy-start | bytes 1376260
  11.9 30.4 %collective-permute-start.2 = (bf16[3,152,896]{2,1,0:T(8,128)(2,1)}, bf16[3,152,896]{2,1,0:T(8,128)(2,1)S(1)}, u32[]{:S(2)}, u32[]{:S(2)}) collective-permute-start(bf16[3,152,896]{2,1,0:T(8,128)(2,1)} %bitcast.157), channel_id=1, source_target_pairs={{0,1},{3,2},{4,5},{7,6},{8,9},{11,10},{12,13},{15,14},{16,17},{19,... | collective-permute-start | bytes 2451464 | tf_op jit(solution)/shard_map/ppermute | solution.py:51
  16.4 61.5 %collective-permute-start = (f32[3,152,896]{2,1,0:T(8,128)S(1)}, f32[3,152,896]{2,1,0:T(8,128)S(1)}, u32[]{:S(2)}, u32[]{:S(2)}) collective-permute-start(f32[3,152,896]{2,1,0:T(8,128)S(1)} %convert_subtract_fusion), channel_id=1, source_target_pairs={{28,0},{0,4},{4,8},{8,12},{12,16},{16,20},{20,24},{24,28},{29,1},{... | collective-permute-start | bytes 4902920 | tf_op jit(solution)/shard_map/ppermute | solution.py:13
  17.5 24.8 %copy-start = (bf16[1,152,3,896]{3,1,2,0:T(8,128)(2,1)S(1)}, bf16[1,152,3,896]{3,1,2,0:T(8,128)(2,1)}, u32[]{:S(2)}) copy-start(bf16[1,152,3,896]{3,1,2,0:T(8,128)(2,1)} %param.7) | copy-start | bytes 2451460
  17.5 60.9 %collective-permute-start.1 = (f32[3,152,896]{2,1,0:T(8,128)S(1)}, f32[3,152,896]{2,1,0:T(8,128)S(1)}, u32[]{:S(2)}, u32[]{:S(2)}) collective-permute-start(f32[3,152,896]{2,1,0:T(8,128)S(1)} %convert_subtract_fusion), channel_id=1, source_target_pairs={{4,0},{8,4},{12,8},{16,12},{20,16},{24,20},{28,24},{0,28},{5,1},{9... | collective-permute-start | bytes 4902920 | tf_op jit(solution)/shard_map/ppermute | solution.py:13
  26.0 20.7 %collective-permute-start.8 = (bf16[256,896]{1,0:T(8,128)(2,1)}, bf16[256,896]{1,0:T(8,128)(2,1)S(1)}, u32[]{:S(2)}, u32[]{:S(2)}) collective-permute-start(bf16[256,896]{1,0:T(8,128)(2,1)} %collective-permute-done.5), channel_id=1, source_target_pairs={{1,2},{2,1},{5,6},{6,5},{9,10},{10,9},{13,14},{14,13},{17,18},{18,... | collective-permute-start | bytes 1376264 | tf_op jit(solution)/shard_map/ppermute | solution.py:51
  27.7 19.3 %collective-permute-start.7 = (bf16[256,896]{1,0:T(8,128)(2,1)}, bf16[256,896]{1,0:T(8,128)(2,1)S(1)}, u32[]{:S(2)}, u32[]{:S(2)}) collective-permute-start(bf16[256,896]{1,0:T(8,128)(2,1)} %collective-permute-done.3), channel_id=1, source_target_pairs={{1,2},{2,1},{5,6},{6,5},{9,10},{10,9},{13,14},{14,13},{17,18},{18,... | collective-permute-start | bytes 1376264 | tf_op jit(solution)/shard_map/ppermute | solution.py:51
  47.8 12.3 %collective-permute-start.12 = (bf16[152,896]{1,0:T(8,128)(2,1)S(1)}, bf16[152,896]{1,0:T(8,128)(2,1)S(1)}, u32[]{:S(2)}, u32[]{:S(2)}) collective-permute-start(bf16[152,896]{1,0:T(8,128)(2,1)S(1)} %slice.239), channel_id=1, source_target_pairs={{1,0},{2,3},{5,4},{6,7},{9,8},{10,11},{13,12},{14,15},{17,16},{18,... | collective-permute-start | bytes 817160 | tf_op jit(solution)/shard_map/ppermute | solution.py:51
  49.9 3.2 %copy-start.1 = (bf16[1,152,3,896]{3,1,2,0:T(8,128)(2,1)S(1)}, bf16[1,152,3,896]{3,1,2,0:T(8,128)(2,1)}, u32[]{:S(2)}) copy-start(bf16[1,152,3,896]{3,1,2,0:T(8,128)(2,1)} %param.8) | copy-start | bytes 2451460
  49.9 3.2 %copy-start.2 = (bf16[1,152,3,896]{3,1,2,0:T(8,128)(2,1)S(1)}, bf16[1,152,3,896]{3,1,2,0:T(8,128)(2,1)}, u32[]{:S(2)}) copy-start(bf16[1,152,3,896]{3,1,2,0:T(8,128)(2,1)} %param.9) | copy-start | bytes 2451460
  49.9 16.0 %collective-permute-start.15 = (bf16[152,896]{1,0:T(8,128)(2,1)S(1)}, bf16[152,896]{1,0:T(8,128)(2,1)S(1)}, u32[]{:S(2)}, u32[]{:S(2)}) collective-permute-start(bf16[152,896]{1,0:T(8,128)(2,1)S(1)} %slice.238), channel_id=1, source_target_pairs={{1,0},{2,3},{5,4},{6,7},{9,8},{10,11},{13,12},{14,15},{17,16},{18,... | collective-permute-start | bytes 817160 | tf_op jit(solution)/shard_map/ppermute | solution.py:51
  51.8 17.0 %collective-permute-start.9 = (bf16[152,896]{1,0:T(8,128)(2,1)S(1)}, bf16[152,896]{1,0:T(8,128)(2,1)S(1)}, u32[]{:S(2)}, u32[]{:S(2)}) collective-permute-start(bf16[152,896]{1,0:T(8,128)(2,1)S(1)} %slice.240), channel_id=1, source_target_pairs={{1,0},{2,3},{5,4},{6,7},{9,8},{10,11},{13,12},{14,15},{17,16},{18,... | collective-permute-start | bytes 817160 | tf_op jit(solution)/shard_map/ppermute | solution.py:51
  70.0 7.9 %collective-permute-start.10 = (bf16[152,896]{1,0:T(8,128)(2,1)S(1)}, bf16[152,896]{1,0:T(8,128)(2,1)S(1)}, u32[]{:S(2)}, u32[]{:S(2)}) collective-permute-start(bf16[152,896]{1,0:T(8,128)(2,1)S(1)} %get-tuple-element.5), channel_id=1, source_target_pairs={{28,0},{0,4},{4,8},{8,12},{12,16},{16,20},{20,24},{24,28},{29,1},{... | collective-permute-start | bytes 817160 | tf_op jit(solution)/shard_map/ppermute | solution.py:13
  70.1 10.7 %collective-permute-start.11 = (bf16[152,896]{1,0:T(8,128)(2,1)S(1)}, bf16[152,896]{1,0:T(8,128)(2,1)S(1)}, u32[]{:S(2)}, u32[]{:S(2)}) collective-permute-start(bf16[152,896]{1,0:T(8,128)(2,1)S(1)} %get-tuple-element.5), channel_id=1, source_target_pairs={{4,0},{8,4},{12,8},{16,12},{20,16},{24,20},{28,24},{0,28},{5,1},{9... | collective-permute-start | bytes 817160 | tf_op jit(solution)/shard_map/ppermute | solution.py:13
  72.7 11.0 %collective-permute-start.13 = (bf16[152,896]{1,0:T(8,128)(2,1)S(1)}, bf16[152,896]{1,0:T(8,128)(2,1)S(1)}, u32[]{:S(2)}, u32[]{:S(2)}) collective-permute-start(bf16[152,896]{1,0:T(8,128)(2,1)S(1)} %get-tuple-element.13), channel_id=1, source_target_pairs={{28,0},{0,4},{4,8},{8,12},{12,16},{16,20},{20,24},{24,28},{29,1},{... | collective-permute-start | bytes 817160 | tf_op jit(solution)/shard_map/ppermute | solution.py:13
  77.9 7.7 %collective-permute-start.14 = (bf16[152,896]{1,0:T(8,128)(2,1)S(1)}, bf16[152,896]{1,0:T(8,128)(2,1)S(1)}, u32[]{:S(2)}, u32[]{:S(2)}) collective-permute-start(bf16[152,896]{1,0:T(8,128)(2,1)S(1)} %get-tuple-element.13), channel_id=1, source_target_pairs={{4,0},{8,4},{12,8},{16,12},{20,16},{24,20},{28,24},{0,28},{5,1},{9... | collective-permute-start | bytes 817160 | tf_op jit(solution)/shard_map/ppermute | solution.py:13
  77.9 11.7 %collective-permute-start.16 = (bf16[152,896]{1,0:T(8,128)(2,1)S(1)}, bf16[152,896]{1,0:T(8,128)(2,1)S(1)}, u32[]{:S(2)}, u32[]{:S(2)}) collective-permute-start(bf16[152,896]{1,0:T(8,128)(2,1)S(1)} %get-tuple-element.11), channel_id=1, source_target_pairs={{28,0},{0,4},{4,8},{8,12},{12,16},{16,20},{20,24},{24,28},{29,1},{... | collective-permute-start | bytes 817160 | tf_op jit(solution)/shard_map/ppermute | solution.py:13
  78.4 11.2 %collective-permute-start.17 = (bf16[152,896]{1,0:T(8,128)(2,1)S(1)}, bf16[152,896]{1,0:T(8,128)(2,1)S(1)}, u32[]{:S(2)}, u32[]{:S(2)}) collective-permute-start(bf16[152,896]{1,0:T(8,128)(2,1)S(1)} %get-tuple-element.11), channel_id=1, source_target_pairs={{4,0},{8,4},{12,8},{16,12},{20,16},{24,20},{28,24},{0,28},{5,1},{9... | collective-permute-start | bytes 817160 | tf_op jit(solution)/shard_map/ppermute | solution.py:13

commit v2 on v0

v2 whole, which is shorter than its diff:
```python
import functools

import jax
import jax.numpy as jnp
from jax import lax
from jax.experimental import pallas as pl
from jax.experimental.pallas import tpu as pltpu
from jax.sharding import PartitionSpec as P

STEP = 10
CORRECT_ONE = 1.0 - 0.9**STEP
CORRECT_TWO = 1.0 - 0.95**STEP
HALF = jnp.bfloat16
FULL = jnp.float32
ORDER = (2, 1, 0)


def shifted(block, axis, distance):
    count = lax.axis_size(axis)
    return lax.ppermute(block, axis, [((i - distance) % count, i) for i in range(count)])


def adam_step(moment_one, moment_two):
    return moment_one / CORRECT_ONE / (jnp.sqrt(moment_two / CORRECT_TWO) + 1e-08)


def into_units(matrix, values):
    return lax.dot_general(matrix, values, (((1,), (1,)), ((), ())), preferred_element_type=FULL)


def over_tokens(terms, values):
    return lax.dot_general(terms, values, (((1,), (0,)), ((), ())), preferred_element_type=FULL)


def forward_terms(xs, gate_rows, upper_rows):
    scale = xs.shape[1] ** (-0.5)
    gate = into_units(gate_rows, xs) * scale
    upper = into_units(upper_rows, xs) * scale
    sigma = 1.0 / (1.0 + jnp.exp(-gate))
    swish = gate * sigma
    return (swish * upper).astype(HALF), swish, upper * sigma * (1.0 + gate * (1.0 - sigma))


def backward_terms(cots, down_rows, swish, slope, scale):
    back = into_units(down_rows, cots) * scale
    return (back * slope).astype(HALF), (back * swish).astype(HALF)


def unit_grads(xs, cots, rows, scale):
    hidden, swish, slope = forward_terms(xs, rows[0], rows[1])
    dgate, dupper = backward_terms(cots, rows[2], swish, slope, scale)
    width_scale = xs.shape[1] ** (-0.5)
    return jnp.stack(
        [
            over_tokens(dgate, xs) * width_scale,
            over_tokens(dupper, xs) * width_scale,
            over_tokens(hidden, cots) * scale,
        ]
    )


def call(kernel, outs, ins, after=(), flops=0, name=None):
    count = len(ins)

    def body(*refs):
        kernel(*refs[:count], *refs[count + len(after) :])

    return pl.pallas_call(
        body,
        out_shape=outs,
        in_specs=[pl.BlockSpec(memory_space=pltpu.VMEM)] * count
        + [pl.BlockSpec(memory_space=pl.ANY)] * len(after),
        out_specs=[pl.BlockSpec(memory_space=pltpu.VMEM)] * len(outs),
        cost_estimate=pl.CostEstimate(flops=flops, bytes_accessed=0, transcendentals=0),
        compiler_params=pltpu.CompilerParams(vmem_limit_bytes=32 * 2**20),
        name=name,
    )(*ins, *after)


def array(shape, dtype):
    return jax.ShapeDtypeStruct(shape, dtype)


def near_forward(own_x, pair_x, inner_x, rows, hidden, swish, slope):
    size = own_x.shape[0]
    for i, xs in enumerate((own_x, pair_x, inner_x)):
        place = pl.ds(i * size, size)
        hidden[:, place], swish[:, place], slope[:, place] = forward_terms(
            xs[...], rows[0], rows[1]
        )


def near_backward(
    own_x, pair_x, inner_x, own_g, pair_g, inner_g, rows, hidden, swish, slope, grads, *, scale
):
    size, width = own_x.shape
    totals = [0.0, 0.0, 0.0]
    for i, (xs, cots) in enumerate(((own_x, own_g), (pair_x, pair_g), (inner_x, inner_g))):
        place = pl.ds(i * size, size)
        dgate, dupper = backward_terms(
            cots[...], rows[2], swish[:, place], slope[:, place], scale
        )
        totals[0] += over_tokens(dgate, xs[...])
        totals[1] += over_tokens(dupper, xs[...])
        totals[2] += over_tokens(hidden[:, place], cots[...])
    for k in range(3):
        grads[k] = totals[k] * (scale if k == 2 else width ** (-0.5))


def ahead_forward(
    inner_x, far_x, inner_g, rows, pair_rows,
    far_hidden, far_swish, far_slope, hidden, swish, slope, dgate, dupper, *, scale
):
    size = inner_x.shape[0]
    first, second = pl.ds(0, size), pl.ds(size, size)
    hidden[:, first], near_swish, near_slope = forward_terms(
        inner_x[...], pair_rows[0], pair_rows[1]
    )
    dgate[...], dupper[...] = backward_terms(
        inner_g[...], pair_rows[2], near_swish, near_slope, scale
    )
    hidden[:, second], swish[...], slope[...] = forward_terms(
        far_x[...], pair_rows[0], pair_rows[1]
    )
    far_hidden[...], far_swish[...], far_slope[...] = forward_terms(far_x[...], rows[0], rows[1])


def pair_down(inner_g, far_g, hidden, sent, *, scale):
    size = inner_g.shape[0]
    total = over_tokens(hidden[:, :size], inner_g[...])
    total += over_tokens(hidden[:, size:], far_g[...])
    sent[...] = (total * scale).astype(HALF)


def pair_others(
    inner_x, far_x, far_g, pair_rows, swish, slope, dgate, dupper, sent_gate, sent_upper, *, scale
):
    width_scale = inner_x.shape[1] ** (-0.5)
    far_dgate, far_dupper = backward_terms(far_g[...], pair_rows[2], swish[...], slope[...], scale)
    total = over_tokens(dupper[...], inner_x[...]) + over_tokens(far_dupper, far_x[...])
    sent_upper[...] = (total * width_scale).astype(HALF)
    total = over_tokens(dgate[...], inner_x[...]) + over_tokens(far_dgate, far_x[...])
    sent_gate[...] = (total * width_scale).astype(HALF)


def far_backward(far_x, far_g, rows, hidden, swish, slope, near, grads, *, scale):
    width_scale = far_x.shape[1] ** (-0.5)
    dgate, dupper = backward_terms(far_g[...], rows[2], swish[...], slope[...], scale)
    grads[0] = near[0] + over_tokens(dgate, far_x[...]) * width_scale
    grads[1] = near[1] + over_tokens(dupper, far_x[...]) * width_scale
    grads[2] = near[2] + over_tokens(hidden[...], far_g[...]) * scale


def line_of_four(tokens, cots, rows, scale, still):
    pairs = [(0, 1), (1, 0), (2, 3), (3, 2)]
    middle = [(1, 2), (2, 1)]
    units, width = rows.shape[1:]
    size = tokens.shape[0]

    def send(block, route):
        return lax.ppermute(block, "tp", route)

    inner_x = send(tokens, middle)
    pair_x = send(tokens, pairs)
    inner_g = send(cots, middle)
    pair_g = send(cots, pairs)
    pair_rows = send(rows, pairs)
    far_x = send(pair_x, middle)
    far_g = send(pair_g, middle)
    work = 20_000_000_000
    near_terms = call(
        near_forward,
        [array((units, 3 * size), t) for t in (HALF, FULL, FULL)],
        (tokens, pair_x, inner_x, rows),
        after=(still,),
        flops=work,
        name="near_forward",
    )
    near = call(
        functools.partial(near_backward, scale=scale),
        [array((3, units, width), FULL)],
        (tokens, pair_x, inner_x, cots, pair_g, inner_g, rows, *near_terms),
        flops=work,
        name="near_backward",
    )[0]
    ahead = call(
        functools.partial(ahead_forward, scale=scale),
        [array((units, size), t) for t in (HALF, FULL, FULL)]
        + [array((units, 2 * size), HALF)]
        + [array((units, size), t) for t in (FULL, FULL, HALF, HALF)],
        (inner_x, far_x, inner_g, rows, pair_rows),
        after=(near,),
        name="ahead_forward",
    )
    far_terms, (hidden, swish, slope, dgate, dupper) = ahead[:3], ahead[3:]
    sent_down = call(
        functools.partial(pair_down, scale=scale),
        [array((units, width), HALF)],
        (inner_g, far_g, hidden),
        name="pair_down",
    )[0]
    sent_gate, sent_upper = call(
        functools.partial(pair_others, scale=scale),
        [array((units, width), HALF)] * 2,
        (inner_x, far_x, far_g, pair_rows, swish, slope, dgate, dupper),
        after=(sent_down,),
        name="pair_others",
    )
    grads = call(
        functools.partial(far_backward, scale=scale),
        [array((3, units, width), FULL)],
        (far_x, far_g, rows, *far_terms, near),
        after=(sent_gate,),
        name="far_backward",
    )[0]
    return grads, [send(v, pairs) for v in (sent_gate, sent_upper, sent_down)]


def gathered(tokens, cots, rows, scale):
    return unit_grads(
        lax.all_gather(tokens, "tp", axis=0, tiled=True),
        lax.all_gather(cots, "tp", axis=0, tiled=True),
        rows,
        scale,
    )


def still_kernel(rows, first, second, still):
    for k in range(3):
        master = rows[k].astype(FULL)
        step = adam_step(0.9 * first[k].astype(FULL), 0.95 * second[k].astype(FULL))
        still[k] = master - 0.1 * (step + 0.1 * master)


def base_kernel(still, before, after, base):
    base[...] = (still[...] + before[...] + after[...]) / 3.0


def change_kernel(grads, first, second, *rest, parts):
    *came, change, sent = rest
    grad = grads[0]
    for part in came[:parts]:
        grad = grad + part[...].astype(FULL)
    moment_one = 0.9 * first[0].astype(FULL)
    moment_two = 0.95 * second[0].astype(FULL)
    step = adam_step(moment_one + 0.1 * grad, moment_two + 0.05 * grad * grad)
    total = 0.1 * (adam_step(moment_one, moment_two) - step)
    change[...] = total
    sent[...] = total.astype(HALF)


def change_of(k, grads, first, second, came, after):
    units, width = grads.shape[1:]
    slab = pl.BlockSpec((1, units, width), lambda i: (k, 0, 0))
    whole = pl.BlockSpec((units, width), lambda i: (0, 0))
    return pl.pallas_call(
        functools.partial(change_kernel, parts=len(came)),
        grid=(1,),
        out_shape=[array((units, width), FULL), array((units, width), HALF)],
        in_specs=[slab] * 3 + [whole] * len(came) + [pl.BlockSpec(memory_space=pl.ANY)] * len(after),
        out_specs=[whole] * 2,
        cost_estimate=pl.CostEstimate(flops=0, bytes_accessed=0, transcendentals=0),
        compiler_params=pltpu.CompilerParams(vmem_limit_bytes=32 * 2**20),
        name=f"change_{k}",
    )(grads, first, second, *came, *after)


def finish_kernel(base, change, before, after, *rest):
    out = rest[-1]
    out[0] = base[0] + (change[...] + before[...].astype(FULL) + after[...].astype(FULL)) / 3.0


def finish(k, base, change, before, following, after):
    units, width = base.shape[1:]
    slab = pl.BlockSpec((1, units, width), lambda i: (k, 0, 0))
    whole = pl.BlockSpec((units, width), lambda i: (0, 0))
    return pl.pallas_call(
        finish_kernel,
        grid=(1,),
        out_shape=array(base.shape, FULL),
        in_specs=[slab] + [whole] * 3 + [pl.BlockSpec(memory_space=pl.ANY)] * len(after),
        out_specs=slab,
        input_output_aliases={0: 0},
        cost_estimate=pl.CostEstimate(flops=0, bytes_accessed=0, transcendentals=0),
        compiler_params=pltpu.CompilerParams(vmem_limit_bytes=32 * 2**20),
        name=f"finish_{k}",
    )(base, change, before, following, *after)


def on_device(tokens, cotangent, weights, first_moment, second_moment):
    rows, first, second = (
        jnp.swapaxes(v[0], 0, 1) for v in (weights, first_moment, second_moment)
    )
    slab = array(rows.shape, FULL)
    scale = (rows.shape[1] * lax.axis_size("tp")) ** (-0.5)
    still = call(still_kernel, [slab], (rows, first, second), name="still")[0]
    still_before, still_after = shifted(still, "blk", 1), shifted(still, "blk", -1)
    if lax.axis_size("tp") == 4:
        grads, came = line_of_four(tokens, cotangent, rows, scale, still)
        came = [[v] for v in came]
    else:
        grads, came = gathered(tokens, cotangent, rows, scale), [[]] * 3
    base = call(
        base_kernel, [slab], (still, still_before, still_after), after=(grads,), name="base"
    )[0]
    changes, last = [], (base,)
    for k in ORDER:
        change, sent = change_of(k, grads, first, second, came[k], last)
        changes.append((k, change, shifted(sent, "blk", 1), shifted(sent, "blk", -1)))
        last = (sent,)
    out = base
    for k, change, before, following in changes:
        out = finish(k, out, change, before, following, last)
        last = ()
    return jnp.swapaxes(out, 0, 1)[None]


def solution(mesh):
    in_specs = (
        P(("blk", "tp"), None),
        P(("blk", "tp"), None),
        P("blk", "tp", None, None),
        P("blk", "tp", None, None),
        P("blk", "tp", None, None),
    )
    out_specs = P("blk", "tp", None, None)
    return jax.shard_map(
        on_device, mesh=mesh, in_specs=in_specs, out_specs=out_specs, check_vma=False
    )
```

time: 149 us -> 85.3 us (0.57)
  waiting for transfers between devices: 121 us -> 38.4 us
  starting transfers between devices: 1.91 us -> 24.4 us
  Pallas kernels: 0 us -> 16.9 us
  between operations: 13.5 us -> 0.19 us
  matrix products: 8.34 us -> 0 us
  local copies, waits for them, and re-layouts: 0.76 us -> 4.89 us
  other arithmetic: 2.94 us -> 0 us
    all_gather x2 -> x0, waiting for transfers between devices: 82.8 us -> none  [the longest x1 45 us: on_device(): lax.all_gather(tokens, 'tp', axis=0, tiled=True)]
    ppermute x2 -> x18, starting transfers between devices: 1.87 us -> 24.4 us  [the longest x10 20.4 us: send(): return lax.ppermute(block, 'tp', route)]
    pallas_call x0 -> x14, Pallas kernels: none -> 16.9 us  [the longest x8 8.94 us: call(): pl.pallas_call(body, out_shape=outs, in_specs=[pl.BlockSpec(memory_space=...]
    dot_general x6 -> x0, matrix products: 8.34 us -> none  [the longest x1 2.47 us: row_terms(): jnp.einsum('td,nd->tn', grads_out, rows[:, 2, :], preferred_element_type=...]
    unnamed x12 -> x18, local copies, waits for them, and re-layouts: 0.76 us -> 4.89 us
    div x1 -> x0, other arithmetic: 1.55 us -> none  [on_device(): return (previous + updated + following) / 3.0]
    ppermute x2 -> x18, waiting for transfers between devices: 37.1 us -> 38.4 us  [the longest x10 28.9 us: send(): return lax.ppermute(block, 'tp', route)]
  transfers between devices with their start and end apart: 4 -> 18, of which waited for: 4 -> 10; matrix products, arithmetic and copies ran while one was open for 3% -> 0% of each run, Pallas kernels for 0% -> 18%
where the time goes in v2:
time: 85.3 us; the launch traced here: 84.8 us
  waiting for transfers between devices  38.4 us (45%)
  starting transfers between devices  24.4 us (29%)
  Pallas kernels  16.9 us (20%)
  local copies, waits for them, and re-layouts  4.89 us (6%)
    ppermute x10, waiting for transfers between devices, send(): return lax.ppermute(block, 'tp', route)  28.9 us
    ppermute x10, starting transfers between devices, send(): return lax.ppermute(block, 'tp', route)  20.4 us
    ppermute x8, waiting for transfers between devices, shifted(): lax.ppermute(block, axis, [((i - distance) % count, i) for i in range(cou...  9.46 us
    pallas_call x8, Pallas kernels, call(): pl.pallas_call(body, out_shape=outs, in_specs=[pl.BlockSpec(memory_space=...  8.94 us
    pallas_call x3, Pallas kernels, finish(): pl.pallas_call(finish_kernel, grid=(1,), out_shape=array(base.shape, FULL...  5.94 us
    unnamed x18, local copies, waits for them, and re-layouts  4.89 us
    ppermute x8, starting transfers between devices, shifted(): lax.ppermute(block, axis, [((i - distance) % count, i) for i in range(cou...  4.08 us
    pallas_call x3, Pallas kernels, change_of(): pl.pallas_call(functools.partial(change_kernel, parts=len(came)), grid=(1...  2.02 us
  transfers between devices with their start and end apart: 18, of which 10 were waited for; matrix products, arithmetic and copies ran while one was open for 0% of the time, Pallas kernels for 18%

profile of v2, /device:TPU:0, one launch (start us, length us, event | category | flops | bytes accessed | tf_op | source)
XLA Modules:
  0.0 84.8 jit_solution(15092854947949987974)
XLA Ops:
  0.0 0.7 collective-permute-start.6
  0.7 5.9 %collective-permute-start.2 = (bf16[256,896]{1,0:T(8,128)(2,1)}, bf16[256,896]{1,0:T(8,128)(2,1)S(1)}, u32[]{:S(2)}, u32[]{:S(2)}) collective-permute-start(bf16[256,896]{1,0:T(8,128)(2,1)} %refs_0_.3), channel_id=1, source_target_pairs={{0,1},{1,0},{2,3},{3,2},{4,5},{5,4},{6,7},{7,6},{8,9},{9,8},{10,11... | collective-permute-start | bytes 1376264 | tf_op jit(solution)/shard_map/ppermute | solution.py:161
  6.6 0.1 collective-permute-start.4
  6.6 0.7 collective-permute-start.7
  7.3 3.7 %collective-permute-start.8 = (bf16[3,152,896]{2,1,0:T(8,128)(2,1)}, bf16[3,152,896]{2,1,0:T(8,128)(2,1)S(1)}, u32[]{:S(2)}, u32[]{:S(2)}) collective-permute-start(bf16[3,152,896]{2,1,0:T(8,128)(2,1)} %bitcast.20), channel_id=1, source_target_pairs={{0,1},{1,0},{2,3},{3,2},{4,5},{5,4},{6,7},{7,6},{8,9},{9,8},{10,11... | collective-permute-start | bytes 2451464 | tf_op jit(solution)/shard_map/ppermute | solution.py:161
  11.0 1.1 %copy-done.1 = bf16[1,152,3,896]{3,1,2,0:T(8,128)(2,1)S(1)} copy-done((bf16[1,152,3,896]{3,1,2,0:T(8,128)(2,1)S(1)}, bf16[1,152,3,896]{3,1,2,0:T(8,128)(2,1)}, u32[]{:S(2)}) %copy-start.1) | copy-done | bytes 817176
  12.2 1.1 %copy-done.3 = bf16[1,152,3,896]{3,1,2,0:T(8,128)(2,1)S(1)} copy-done((bf16[1,152,3,896]{3,1,2,0:T(8,128)(2,1)S(1)}, bf16[1,152,3,896]{3,1,2,0:T(8,128)(2,1)}, u32[]{:S(2)}) %copy-start.3) | copy-done | bytes 817176
  13.3 1.1 %copy-done.5 = bf16[1,152,3,896]{3,1,2,0:T(8,128)(2,1)S(1)} copy-done((bf16[1,152,3,896]{3,1,2,0:T(8,128)(2,1)S(1)}, bf16[1,152,3,896]{3,1,2,0:T(8,128)(2,1)}, u32[]{:S(2)}) %copy-start.5) | copy-done | bytes 817176
  14.5 1.1 %still.1.refs_4_.refs_0_ = f32[3,152,896]{2,1,0:T(8,128)S(1)} custom-call(bf16[3,152,896]{2,1,0:T(8,128)(2,1)S(1)} %bitcast.21, bf16[3,152,896]{2,1,0:T(8,128)(2,1)S(1)} %bitcast.12, bf16[3,152,896]{2,1,0:T(8,128)(2,1)S(1)} %bitcast.16), custom_call_target="tpu_custom_call" | custom-call | tf_op jit(solution)/shard_map/still/pallas_call | solution.py:68
  15.6 0.0 copy-start.8
  15.6 0.5 collective-permute-start.1
  16.1 2.0 %collective-permute-done.2.refs_1_ = bf16[256,896]{1,0:T(8,128)(2,1)S(1)} collective-permute-done((bf16[256,896]{1,0:T(8,128)(2,1)}, bf16[256,896]{1,0:T(8,128)(2,1)S(1)}, u32[]{:S(2)}, u32[]{:S(2)}) %collective-permute-start.2) | collective-permute-done | bytes 458784 | tf_op jit(solution)/shard_map/ppermute | solution.py:161
  18.2 1.1 %near_forward.1 = (bf16[152,768]{1,0:T(8,128)(2,1)S(1)}, f32[152,768]{1,0:T(8,128)S(1)}, f32[152,768]{1,0:T(8,128)S(1)}) custom-call(bf16[256,896]{1,0:T(8,128)(2,1)S(1)} %copy-done.7, bf16[256,896]{1,0:T(8,128)(2,1)S(1)} %collective-permute-done.2.refs_1_, bf16[256,896]{1,0:T(8,128)(2,1)S(1)} %collective-permute-done.6.refs_2_.refs_0_, ...), custom_call_target="tpu_custom_call" | custom-call | flops 20000000000 | tf_op jit(solution)/shard_map/near_forward/pallas_call | solution.py:68
  19.3 8.7 %collective-permute-done.4.refs_4_ = bf16[256,896]{1,0:T(8,128)(2,1)S(1)} collective-permute-done((bf16[256,896]{1,0:T(8,128)(2,1)}, bf16[256,896]{1,0:T(8,128)(2,1)S(1)}, u32[]{:S(2)}, u32[]{:S(2)}) %collective-permute-start.4) | collective-permute-done | bytes 458784 | tf_op jit(solution)/shard_map/ppermute | solution.py:161
  28.0 0.7 collective-permute-start.3
  28.7 0.7 collective-permute-start.5
  29.4 1.8 %near_backward.1.refs_5_.refs_6_ = f32[3,152,896]{2,1,0:T(8,128)S(1)} custom-call(bf16[256,896]{1,0:T(8,128)(2,1)S(1)} %copy-done.7, bf16[256,896]{1,0:T(8,128)(2,1)S(1)} %collective-permute-done.2.refs_1_, bf16[256,896]{1,0:T(8,128)(2,1)S(1)} %collective-permute-done.6.refs_2_.refs_0_, bf16[256,896]{1,0:T(8,128)(2,1)S(1)} %copy-done.8, ...), custom_call_target="tpu_custom_call" | custom-call | flops 20000000000 | tf_op jit(solution)/shard_map/near_backward/pallas_call | solution.py:68
  31.2 13.1 %collective-permute-done.8.refs_4_.refs_3_ = bf16[3,152,896]{2,1,0:T(8,128)(2,1)S(1)} collective-permute-done((bf16[3,152,896]{2,1,0:T(8,128)(2,1)}, bf16[3,152,896]{2,1,0:T(8,128)(2,1)S(1)}, u32[]{:S(2)}, u32[]{:S(2)}) %collective-permute-start.8) | collective-permute-done | bytes 817184 | tf_op jit(solution)/shard_map/ppermute | solution.py:161
  44.4 1.2 %ahead_forward.1 = (bf16[152,256]{1,0:T(8,128)(2,1)S(1)}, f32[152,256]{1,0:T(8,128)S(1)}, f32[152,256]{1,0:T(8,128)S(1)}, bf16[152,512]{1,0:T(8,128)(2,1)S(1)}, ...) custom-call(bf16[256,896]{1,0:T(8,128)(2,1)S(1)} %collective-permute, ...), custom_call_target="tpu_custom_call" | custom-call | tf_op jit(solution)/shard_map/ahead_forward/pallas_call | solution.py:68
  45.5 0.3 pair_down.1.refs_8_
  45.9 0.0 copy-start.6
  45.9 5.9 %collective-permute-start.9 = (bf16[152,896]{1,0:T(8,128)(2,1)S(1)}, bf16[152,896]{1,0:T(8,128)(2,1)S(1)}, u32[]{:S(2)}, u32[]{:S(2)}) collective-permute-start(bf16[152,896]{1,0:T(8,128)(2,1)S(1)} %pair_down.1.refs_8_), channel_id=1, source_target_pairs={{0,1},{1,0},{2,3},{3,2},{4,5},{5,4},{6,7},{7,6},{8,9},{9,8},{10,11... | collective-permute-start | bytes 817160 | tf_op jit(solution)/shard_map/ppermute | solution.py:161
  51.8 1.0 %pair_others.1 = (bf16[152,896]{1,0:T(8,128)(2,1)S(1)}, bf16[152,896]{1,0:T(8,128)(2,1)S(1)}) custom-call(bf16[256,896]{1,0:T(8,128)(2,1)S(1)} %collective-permute-done.6.refs_2_.refs_0_, bf16[256,896]{1,0:T(8,128)(2,1)S(1)} %collective-permute-done.3.refs_1_.refs_0_, bf16[256,896]{1,0:T(8,128)(2,1)S(1)} %collective-permute-done.5.refs_1_.refs_2_, ...), custom_call_target="tpu_custom_call" | custom-call | tf_op jit(solution)/shard_map/pair_others/pallas_call | solution.py:68
  52.8 0.1 collective-permute-start.13
  52.9 2.0 %collective-permute-start.12 = (bf16[152,896]{1,0:T(8,128)(2,1)S(1)}, bf16[152,896]{1,0:T(8,128)(2,1)S(1)}, u32[]{:S(2)}, u32[]{:S(2)}) collective-permute-start(bf16[152,896]{1,0:T(8,128)(2,1)S(1)} %get-tuple-element.35.refs_7_), channel_id=1, source_target_pairs={{0,1},{1,0},{2,3},{3,2},{4,5},{5,4},{6,7},{7,6},{8,9},{9,8},{10,11... | collective-permute-start | bytes 817160 | tf_op jit(solution)/shard_map/ppermute | solution.py:161
  54.9 0.9 %far_backward.1.refs_3_.grads = f32[3,152,896]{2,1,0:T(8,128)S(1)} custom-call(bf16[256,896]{1,0:T(8,128)(2,1)S(1)} %collective-permute-done.3.refs_1_.refs_0_, bf16[256,896]{1,0:T(8,128)(2,1)S(1)} %collective-permute-done.5.refs_1_.refs_2_, bf16[3,152,896]{2,1,0:T(8,128)(2,1)S(1)} %bitcast.25, bf16[152,256]{1,0:T(8,128)(2,1)S(1)} %get-tuple-element.27.refs_3_, ...), custom_call_target="tpu_custom_call" | custom-call | tf_op jit(solution)/shard_map/far_backward/pallas_call | solution.py:68
  55.8 0.0 copy-start.2
  55.8 1.5 %base.1.rest_1_ = f32[3,152,896]{2,1,0:T(8,128)} custom-call(f32[3,152,896]{2,1,0:T(8,128)S(1)} %still.1.refs_4_.refs_0_, f32[3,152,896]{2,1,0:T(8,128)S(1)} %collective-permute-done.refs_1_, f32[3,152,896]{2,1,0:T(8,128)S(1)} %collective-permute-done.1.refs_2_, f32[3,152,896]{2,1,0:T(8,128)S(1)} %far_backward.1.refs_3_.grads), custom_call_target="tpu_custom_call" | custom-call | tf_op jit(solution)/shard_map/base/pallas_call | solution.py:68
  57.3 1.9 %collective-permute-done.9.rest_0_ = bf16[152,896]{1,0:T(8,128)(2,1)S(1)} collective-permute-done((bf16[152,896]{1,0:T(8,128)(2,1)S(1)}, bf16[152,896]{1,0:T(8,128)(2,1)S(1)}, u32[]{:S(2)}, u32[]{:S(2)}) %collective-permute-start.9) | collective-permute-done | bytes 272416 | tf_op jit(solution)/shard_map/ppermute | solution.py:161
  59.3 1.4 %copy-done = f32[3,152,896]{2,1,0:T(8,128)S(1)} copy-done((f32[3,152,896]{2,1,0:T(8,128)S(1)}, f32[3,152,896]{2,1,0:T(8,128)}, u32[]{:S(2)}) %copy-start) | copy-done | bytes 1634328
  60.7 0.7 change_2.1
  61.4 0.1 collective-permute-start.11
  61.4 0.5 collective-permute-start.10
  61.9 1.6 %collective-permute-done.13.rest_0_ = bf16[152,896]{1,0:T(8,128)(2,1)S(1)} collective-permute-done((bf16[152,896]{1,0:T(8,128)(2,1)S(1)}, bf16[152,896]{1,0:T(8,128)(2,1)S(1)}, u32[]{:S(2)}, u32[]{:S(2)}) %collective-permute-start.13) | collective-permute-done | bytes 272416 | tf_op jit(solution)/shard_map/ppermute | solution.py:161
  63.5 0.7 change_1.1
  64.2 0.7 collective-permute-start.15
  64.9 1.6 %collective-permute-done.12.rest_0_ = bf16[152,896]{1,0:T(8,128)(2,1)S(1)} collective-permute-done((bf16[152,896]{1,0:T(8,128)(2,1)S(1)}, bf16[152,896]{1,0:T(8,128)(2,1)S(1)}, u32[]{:S(2)}, u32[]{:S(2)}) %collective-permute-start.12) | collective-permute-done | bytes 272416 | tf_op jit(solution)/shard_map/ppermute | solution.py:161
  66.4 0.7 change_0.1
  67.1 1.1 %collective-permute-start.17 = (bf16[152,896]{1,0:T(8,128)(2,1)S(1)}, bf16[152,896]{1,0:T(8,128)(2,1)S(1)}, u32[]{:S(2)}, u32[]{:S(2)}) collective-permute-start(bf16[152,896]{1,0:T(8,128)(2,1)S(1)} %get-tuple-element.40.rest_0_), channel_id=1, source_target_pairs={{4,0},{8,4},{12,8},{16,12},{20,16},{24,20},{28,24},{0,28},{5,1},{9... | collective-permute-start | bytes 817160 | tf_op jit(solution)/shard_map/ppermute | solution.py:20
  68.2 1.2 %collective-permute-start.16 = (bf16[152,896]{1,0:T(8,128)(2,1)S(1)}, bf16[152,896]{1,0:T(8,128)(2,1)S(1)}, u32[]{:S(2)}, u32[]{:S(2)}) collective-permute-start(bf16[152,896]{1,0:T(8,128)(2,1)S(1)} %get-tuple-element.40.rest_0_), channel_id=1, source_target_pairs={{28,0},{0,4},{4,8},{8,12},{12,16},{16,20},{20,24},{24,28},{29,1},{... | collective-permute-start | bytes 817160 | tf_op jit(solution)/shard_map/ppermute | solution.py:20
  69.4 1.7 %collective-permute-done.10.before = bf16[152,896]{1,0:T(8,128)(2,1)S(1)} collective-permute-done((bf16[152,896]{1,0:T(8,128)(2,1)S(1)}, bf16[152,896]{1,0:T(8,128)(2,1)S(1)}, u32[]{:S(2)}, u32[]{:S(2)}) %collective-permute-start.10) | collective-permute-done | bytes 272416 | tf_op jit(solution)/shard_map/ppermute | solution.py:20
  71.2 2.0 %finish_2.1.base = f32[3,152,896]{2,1,0:T(8,128)} custom-call(f32[3,152,896]{2,1,0:T(8,128)} %base.1.rest_1_, f32[152,896]{1,0:T(8,128)S(1)} %get-tuple-element.36.change, bf16[152,896]{1,0:T(8,128)(2,1)S(1)} %collective-permute-done.10.before, bf16[152,896]{1,0:T(8,128)(2,1)S(1)} %collective-permute-done.11.after, ...), custom_call_target="tpu_custom_call", output_to_operand_aliasing={{}: (0, {})} | custom-call | tf_op jit(solution)/shard_map/finish_2/pallas_call | solution.py:277
  73.1 0.1 collective-permute-done.15.after
  73.2 3.8 %collective-permute-done.14.before = bf16[152,896]{1,0:T(8,128)(2,1)S(1)} collective-permute-done((bf16[152,896]{1,0:T(8,128)(2,1)S(1)}, bf16[152,896]{1,0:T(8,128)(2,1)S(1)}, u32[]{:S(2)}, u32[]{:S(2)}) %collective-permute-start.14) | collective-permute-done | bytes 272416 | tf_op jit(solution)/shard_map/ppermute | solution.py:20
  77.0 2.0 %finish_1.1.base = f32[3,152,896]{2,1,0:T(8,128)} custom-call(f32[3,152,896]{2,1,0:T(8,128)} %finish_2.1.base, f32[152,896]{1,0:T(8,128)S(1)} %get-tuple-element.41.change, bf16[152,896]{1,0:T(8,128)(2,1)S(1)} %collective-permute-done.14.before, bf16[152,896]{1,0:T(8,128)(2,1)S(1)} %collective-permute-done.15.after), custom_call_target="tpu_custom_call", output_to_operand_aliasing={{}: (0, {})} | custom-call | tf_op jit(solution)/shard_map/finish_1/pallas_call | solution.py:277
  79.0 0.1 collective-permute-done.17.after
  79.0 3.8 %collective-permute-done.16.before = bf16[152,896]{1,0:T(8,128)(2,1)S(1)} collective-permute-done((bf16[152,896]{1,0:T(8,128)(2,1)S(1)}, bf16[152,896]{1,0:T(8,128)(2,1)S(1)}, u32[]{:S(2)}, u32[]{:S(2)}) %collective-permute-start.16) | collective-permute-done | bytes 272416 | tf_op jit(solution)/shard_map/ppermute | solution.py:20
  82.8 2.0 %finish_0.1 = f32[3,152,896]{2,1,0:T(8,128)} custom-call(f32[3,152,896]{2,1,0:T(8,128)} %finish_1.1.base, f32[152,896]{1,0:T(8,128)S(1)} %get-tuple-element.42.change, bf16[152,896]{1,0:T(8,128)(2,1)S(1)} %collective-permute-done.16.before, bf16[152,896]{1,0:T(8,128)(2,1)S(1)} %collective-permute-done.17.after), custom_call_target="tpu_custom_call", output_to_operand_aliasing={{}: (0, {})} | custom-call | tf_op jit(solution)/shard_map/finish_0/pallas_call | solution.py:277
  (20 shorter events, 0.0 us)
Async XLA Ops:
  0.0 15.6 %collective-permute-start.6 = (bf16[256,896]{1,0:T(8,128)(2,1)}, bf16[256,896]{1,0:T(8,128)(2,1)S(1)}, u32[]{:S(2)}, u32[]{:S(2)}) collective-permute-start(bf16[256,896]{1,0:T(8,128)(2,1)} %refs_0_.3), channel_id=1, source_target_pairs={{1,2},{2,1},{5,6},{6,5},{9,10},{10,9},{13,14},{14,13},{17,18},{18,... | collective-permute-start | bytes 1376264 | tf_op jit(solution)/shard_map/ppermute | solution.py:161
  0.7 17.5 %collective-permute-start.2 = (bf16[256,896]{1,0:T(8,128)(2,1)}, bf16[256,896]{1,0:T(8,128)(2,1)S(1)}, u32[]{:S(2)}, u32[]{:S(2)}) collective-permute-start(bf16[256,896]{1,0:T(8,128)(2,1)} %refs_0_.3), channel_id=1, source_target_pairs={{0,1},{1,0},{2,3},{3,2},{4,5},{5,4},{6,7},{7,6},{8,9},{9,8},{10,11... | collective-permute-start | bytes 1376264 | tf_op jit(solution)/shard_map/ppermute | solution.py:161
  6.6 21.4 %collective-permute-start.4 = (bf16[256,896]{1,0:T(8,128)(2,1)}, bf16[256,896]{1,0:T(8,128)(2,1)S(1)}, u32[]{:S(2)}, u32[]{:S(2)}) collective-permute-start(bf16[256,896]{1,0:T(8,128)(2,1)} %refs_3_.1), channel_id=1, source_target_pairs={{0,1},{1,0},{2,3},{3,2},{4,5},{5,4},{6,7},{7,6},{8,9},{9,8},{10,11... | collective-permute-start | bytes 1376264 | tf_op jit(solution)/shard_map/ppermute | solution.py:161
  6.6 22.0 %collective-permute-start.7 = (bf16[256,896]{1,0:T(8,128)(2,1)}, bf16[256,896]{1,0:T(8,128)(2,1)S(1)}, u32[]{:S(2)}, u32[]{:S(2)}) collective-permute-start(bf16[256,896]{1,0:T(8,128)(2,1)} %refs_3_.1), channel_id=1, source_target_pairs={{1,2},{2,1},{5,6},{6,5},{9,10},{10,9},{13,14},{14,13},{17,18},{18,... | collective-permute-start | bytes 1376264 | tf_op jit(solution)/shard_map/ppermute | solution.py:161
  7.3 37.0 %collective-permute-start.8 = (bf16[3,152,896]{2,1,0:T(8,128)(2,1)}, bf16[3,152,896]{2,1,0:T(8,128)(2,1)S(1)}, u32[]{:S(2)}, u32[]{:S(2)}) collective-permute-start(bf16[3,152,896]{2,1,0:T(8,128)(2,1)} %bitcast.20), channel_id=1, source_target_pairs={{0,1},{1,0},{2,3},{3,2},{4,5},{5,4},{6,7},{7,6},{8,9},{9,8},{10,11... | collective-permute-start | bytes 2451464 | tf_op jit(solution)/shard_map/ppermute | solution.py:161
  11.0 1.1 %copy-start.1 = (bf16[1,152,3,896]{3,1,2,0:T(8,128)(2,1)S(1)}, bf16[1,152,3,896]{3,1,2,0:T(8,128)(2,1)}, u32[]{:S(2)}) copy-start(bf16[1,152,3,896]{3,1,2,0:T(8,128)(2,1)} %param.8) | copy-start | bytes 2451460
  12.2 1.1 %copy-start.3 = (bf16[1,152,3,896]{3,1,2,0:T(8,128)(2,1)S(1)}, bf16[1,152,3,896]{3,1,2,0:T(8,128)(2,1)}, u32[]{:S(2)}) copy-start(bf16[1,152,3,896]{3,1,2,0:T(8,128)(2,1)} %param.9) | copy-start | bytes 2451460
  13.3 1.1 %copy-start.5 = (bf16[1,152,3,896]{3,1,2,0:T(8,128)(2,1)S(1)}, bf16[1,152,3,896]{3,1,2,0:T(8,128)(2,1)}, u32[]{:S(2)}) copy-start(bf16[1,152,3,896]{3,1,2,0:T(8,128)(2,1)} %param.7) | copy-start | bytes 2451460
  14.5 3.7 %copy-start.7 = (bf16[256,896]{1,0:T(8,128)(2,1)S(1)}, bf16[256,896]{1,0:T(8,128)(2,1)}, u32[]{:S(2)}) copy-start(bf16[256,896]{1,0:T(8,128)(2,1)} %refs_0_.3) | copy-start | bytes 1376260
  15.6 13.8 %copy-start.8 = (bf16[256,896]{1,0:T(8,128)(2,1)S(1)}, bf16[256,896]{1,0:T(8,128)(2,1)}, u32[]{:S(2)}) copy-start(bf16[256,896]{1,0:T(8,128)(2,1)} %refs_3_.1) | copy-start | bytes 1376260
  15.6 40.2 %collective-permute-start.1 = (f32[3,152,896]{2,1,0:T(8,128)S(1)}, f32[3,152,896]{2,1,0:T(8,128)S(1)}, u32[]{:S(2)}, u32[]{:S(2)}) collective-permute-start(f32[3,152,896]{2,1,0:T(8,128)S(1)} %still.1.refs_4_.refs_0_), channel_id=1, source_target_pairs={{4,0},{8,4},{12,8},{16,12},{20,16},{24,20},{28,24},{0,28},{5,1},{9... | collective-permute-start | bytes 4902920 | tf_op jit(solution)/shard_map/ppermute | solution.py:20
  18.2 37.7 %collective-permute-start = (f32[3,152,896]{2,1,0:T(8,128)S(1)}, f32[3,152,896]{2,1,0:T(8,128)S(1)}, u32[]{:S(2)}, u32[]{:S(2)}) collective-permute-start(f32[3,152,896]{2,1,0:T(8,128)S(1)} %still.1.refs_4_.refs_0_), channel_id=1, source_target_pairs={{28,0},{0,4},{4,8},{8,12},{12,16},{16,20},{20,24},{24,28},{29,1},{... | collective-permute-start | bytes 4902920 | tf_op jit(solution)/shard_map/ppermute | solution.py:20
  28.0 16.4 %collective-permute-start.3 = (bf16[256,896]{1,0:T(8,128)(2,1)S(1)}, bf16[256,896]{1,0:T(8,128)(2,1)S(1)}, u32[]{:S(2)}, u32[]{:S(2)}) collective-permute-start(bf16[256,896]{1,0:T(8,128)(2,1)S(1)} %collective-permute-done.2.refs_1_), channel_id=1, source_target_pairs={{1,2},{2,1},{5,6},{6,5},{9,10},{10,9},{13,14},{14,13},{17,18},{18,... | collective-permute-start | bytes 1376264 | tf_op jit(solution)/shard_map/ppermute | solution.py:161
  28.7 16.8 %collective-permute-start.5 = (bf16[256,896]{1,0:T(8,128)(2,1)S(1)}, bf16[256,896]{1,0:T(8,128)(2,1)S(1)}, u32[]{:S(2)}, u32[]{:S(2)}) collective-permute-start(bf16[256,896]{1,0:T(8,128)(2,1)S(1)} %collective-permute-done.4.refs_4_), channel_id=1, source_target_pairs={{1,2},{2,1},{5,6},{6,5},{9,10},{10,9},{13,14},{14,13},{17,18},{18,... | collective-permute-start | bytes 1376264 | tf_op jit(solution)/shard_map/ppermute | solution.py:161
  45.9 9.0 %copy-start.6 = (bf16[1,152,3,896]{3,1,2,0:T(8,128)(2,1)S(1)}, bf16[1,152,3,896]{3,1,2,0:T(8,128)(2,1)}, u32[]{:S(2)}) copy-start(bf16[1,152,3,896]{3,1,2,0:T(8,128)(2,1)} %param.7) | copy-start | bytes 2451460
  45.9 13.3 %collective-permute-start.9 = (bf16[152,896]{1,0:T(8,128)(2,1)S(1)}, bf16[152,896]{1,0:T(8,128)(2,1)S(1)}, u32[]{:S(2)}, u32[]{:S(2)}) collective-permute-start(bf16[152,896]{1,0:T(8,128)(2,1)S(1)} %pair_down.1.refs_8_), channel_id=1, source_target_pairs={{0,1},{1,0},{2,3},{3,2},{4,5},{5,4},{6,7},{7,6},{8,9},{9,8},{10,11... | collective-permute-start | bytes 817160 | tf_op jit(solution)/shard_map/ppermute | solution.py:161
  52.8 10.7 %collective-permute-start.13 = (bf16[152,896]{1,0:T(8,128)(2,1)S(1)}, bf16[152,896]{1,0:T(8,128)(2,1)S(1)}, u32[]{:S(2)}, u32[]{:S(2)}) collective-permute-start(bf16[152,896]{1,0:T(8,128)(2,1)S(1)} %get-tuple-element.38), channel_id=1, source_target_pairs={{0,1},{1,0},{2,3},{3,2},{4,5},{5,4},{6,7},{7,6},{8,9},{9,8},{10,11... | collective-permute-start | bytes 817160 | tf_op jit(solution)/shard_map/ppermute | solution.py:161
  52.9 13.5 %collective-permute-start.12 = (bf16[152,896]{1,0:T(8,128)(2,1)S(1)}, bf16[152,896]{1,0:T(8,128)(2,1)S(1)}, u32[]{:S(2)}, u32[]{:S(2)}) collective-permute-start(bf16[152,896]{1,0:T(8,128)(2,1)S(1)} %get-tuple-element.35.refs_7_), channel_id=1, source_target_pairs={{0,1},{1,0},{2,3},{3,2},{4,5},{5,4},{6,7},{7,6},{8,9},{9,8},{10,11... | collective-permute-start | bytes 817160 | tf_op jit(solution)/shard_map/ppermute | solution.py:161
  55.8 3.4 %copy-start.2 = (bf16[1,152,3,896]{3,1,2,0:T(8,128)(2,1)S(1)}, bf16[1,152,3,896]{3,1,2,0:T(8,128)(2,1)}, u32[]{:S(2)}) copy-start(bf16[1,152,3,896]{3,1,2,0:T(8,128)(2,1)} %param.8) | copy-start | bytes 2451460
  55.8 3.4 %copy-start.4 = (bf16[1,152,3,896]{3,1,2,0:T(8,128)(2,1)S(1)}, bf16[1,152,3,896]{3,1,2,0:T(8,128)(2,1)}, u32[]{:S(2)}) copy-start(bf16[1,152,3,896]{3,1,2,0:T(8,128)(2,1)} %param.9) | copy-start | bytes 2451460
  59.2 1.4 %copy-start = (f32[3,152,896]{2,1,0:T(8,128)S(1)}, f32[3,152,896]{2,1,0:T(8,128)}, u32[]{:S(2)}) copy-start(f32[3,152,896]{2,1,0:T(8,128)} %base.1.rest_1_) | copy-start | bytes 4902916
  61.4 6.9 %collective-permute-start.11 = (bf16[152,896]{1,0:T(8,128)(2,1)S(1)}, bf16[152,896]{1,0:T(8,128)(2,1)S(1)}, u32[]{:S(2)}, u32[]{:S(2)}) collective-permute-start(bf16[152,896]{1,0:T(8,128)(2,1)S(1)} %get-tuple-element.37.rest_1_), channel_id=1, source_target_pairs={{4,0},{8,4},{12,8},{16,12},{20,16},{24,20},{28,24},{0,28},{5,1},{9... | collective-permute-start | bytes 817160 | tf_op jit(solution)/shard_map/ppermute | solution.py:20
  61.4 9.7 %collective-permute-start.10 = (bf16[152,896]{1,0:T(8,128)(2,1)S(1)}, bf16[152,896]{1,0:T(8,128)(2,1)S(1)}, u32[]{:S(2)}, u32[]{:S(2)}) collective-permute-start(bf16[152,896]{1,0:T(8,128)(2,1)S(1)} %get-tuple-element.37.rest_1_), channel_id=1, source_target_pairs={{28,0},{0,4},{4,8},{8,12},{12,16},{16,20},{20,24},{24,28},{29,1},{... | collective-permute-start | bytes 817160 | tf_op jit(solution)/shard_map/ppermute | solution.py:20
  64.2 9.0 %collective-permute-start.15 = (bf16[152,896]{1,0:T(8,128)(2,1)S(1)}, bf16[152,896]{1,0:T(8,128)(2,1)S(1)}, u32[]{:S(2)}, u32[]{:S(2)}) collective-permute-start(bf16[152,896]{1,0:T(8,128)(2,1)S(1)} %get-tuple-element.39.rest_1_), channel_id=1, source_target_pairs={{4,0},{8,4},{12,8},{16,12},{20,16},{24,20},{28,24},{0,28},{5,1},{9... | collective-permute-start | bytes 817160 | tf_op jit(solution)/shard_map/ppermute | solution.py:20
  64.9 12.1 %collective-permute-start.14 = (bf16[152,896]{1,0:T(8,128)(2,1)S(1)}, bf16[152,896]{1,0:T(8,128)(2,1)S(1)}, u32[]{:S(2)}, u32[]{:S(2)}) collective-permute-start(bf16[152,896]{1,0:T(8,128)(2,1)S(1)} %get-tuple-element.39.rest_1_), channel_id=1, source_target_pairs={{28,0},{0,4},{4,8},{8,12},{12,16},{16,20},{20,24},{24,28},{29,1},{... | collective-permute-start | bytes 817160 | tf_op jit(solution)/shard_map/ppermute | solution.py:20
  67.1 11.9 %collective-permute-start.17 = (bf16[152,896]{1,0:T(8,128)(2,1)S(1)}, bf16[152,896]{1,0:T(8,128)(2,1)S(1)}, u32[]{:S(2)}, u32[]{:S(2)}) collective-permute-start(bf16[152,896]{1,0:T(8,128)(2,1)S(1)} %get-tuple-element.40.rest_0_), channel_id=1, source_target_pairs={{4,0},{8,4},{12,8},{16,12},{20,16},{24,20},{28,24},{0,28},{5,1},{9... | collective-permute-start | bytes 817160 | tf_op jit(solution)/shard_map/ppermute | solution.py:20
  68.2 14.6 %collective-permute-start.16 = (bf16[152,896]{1,0:T(8,128)(2,1)S(1)}, bf16[152,896]{1,0:T(8,128)(2,1)S(1)}, u32[]{:S(2)}, u32[]{:S(2)}) collective-permute-start(bf16[152,896]{1,0:T(8,128)(2,1)S(1)} %get-tuple-element.40.rest_0_), channel_id=1, source_target_pairs={{28,0},{0,4},{4,8},{8,12},{12,16},{16,20},{20,24},{24,28},{29,1},{... | collective-permute-start | bytes 817160 | tf_op jit(solution)/shard_map/ppermute | solution.py:20

commit v3 on v2

v3 whole, which is shorter than its diff:
```python
import functools

import jax
import jax.numpy as jnp
from jax import lax
from jax.experimental import pallas as pl
from jax.experimental.pallas import tpu as pltpu
from jax.sharding import PartitionSpec as P

STEP = 10
CORRECT_ONE = 1.0 - 0.9**STEP
CORRECT_TWO = 1.0 - 0.95**STEP
HALF = jnp.bfloat16
FULL = jnp.float32
ORDER = (2, 1, 0)


def shifted(block, axis, distance):
    count = lax.axis_size(axis)
    return lax.ppermute(block, axis, [((i - distance) % count, i) for i in range(count)])


def adam_step(moment_one, moment_two):
    return moment_one / CORRECT_ONE / (jnp.sqrt(moment_two / CORRECT_TWO) + 1e-08)


def into_units(matrix, values):
    return lax.dot_general(matrix, values, (((1,), (1,)), ((), ())), preferred_element_type=FULL)


def over_tokens(terms, values):
    return lax.dot_general(terms, values, (((1,), (0,)), ((), ())), preferred_element_type=FULL)


def forward_terms(xs, gate_rows, upper_rows):
    scale = xs.shape[1] ** (-0.5)
    gate = into_units(gate_rows, xs) * scale
    upper = into_units(upper_rows, xs) * scale
    sigma = 1.0 / (1.0 + jnp.exp(-gate))
    swish = gate * sigma
    return (swish * upper).astype(HALF), swish, upper * sigma * (1.0 + gate * (1.0 - sigma))


def backward_terms(cots, down_rows, swish, slope, scale):
    back = into_units(down_rows, cots) * scale
    return (back * slope).astype(HALF), (back * swish).astype(HALF)


def unit_grads(xs, cots, rows, scale):
    hidden, swish, slope = forward_terms(xs, rows[0], rows[1])
    dgate, dupper = backward_terms(cots, rows[2], swish, slope, scale)
    width_scale = xs.shape[1] ** (-0.5)
    return jnp.stack(
        [
            over_tokens(dgate, xs) * width_scale,
            over_tokens(dupper, xs) * width_scale,
            over_tokens(hidden, cots) * scale,
        ]
    )


def call(kernel, outs, ins, after=(), flops=0, name=None):
    count = len(ins)

    def body(*refs):
        kernel(*refs[:count], *refs[count + len(after) :])

    return pl.pallas_call(
        body,
        out_shape=outs,
        in_specs=[pl.BlockSpec(memory_space=pltpu.VMEM)] * count
        + [pl.BlockSpec(memory_space=pl.ANY)] * len(after),
        out_specs=[pl.BlockSpec(memory_space=pltpu.VMEM)] * len(outs),
        cost_estimate=pl.CostEstimate(flops=flops, bytes_accessed=0, transcendentals=0),
        compiler_params=pltpu.CompilerParams(vmem_limit_bytes=32 * 2**20),
        name=name,
    )(*ins, *after)


def array(shape, dtype):
    return jax.ShapeDtypeStruct(shape, dtype)


def near_forward(own_x, pair_x, inner_x, rows, hidden, swish, slope):
    size = own_x.shape[0]
    for i, xs in enumerate((own_x, pair_x, inner_x)):
        place = pl.ds(i * size, size)
        hidden[:, place], swish[:, place], slope[:, place] = forward_terms(
            xs[...], rows[0], rows[1]
        )


def near_backward(
    own_x, pair_x, inner_x, own_g, pair_g, inner_g,
    rows, hidden, swish, slope, grads, *, scale
):
    size, width = own_x.shape
    totals = [0.0, 0.0, 0.0]
    shards = ((own_x, (own_g,)), (pair_x, (pair_g,)), (inner_x, (inner_g,)))
    for i, (xs, parts) in enumerate(shards):
        place = pl.ds(i * size, size)
        cots = joined(parts)
        dgate, dupper = backward_terms(cots, rows[2], swish[:, place], slope[:, place], scale)
        totals[0] += over_tokens(dgate, xs[...])
        totals[1] += over_tokens(dupper, xs[...])
        totals[2] += over_tokens(hidden[:, place], cots)
    for k in range(3):
        grads[k] = totals[k] * (scale if k == 2 else width ** (-0.5))


def ahead_forward(
    inner_x, far_x, inner_g, rows, pair_rows,
    far_hidden, far_swish, far_slope, hidden, swish, slope, dgate, dupper, *, scale
):
    size = inner_x.shape[0]
    first, second = pl.ds(0, size), pl.ds(size, size)
    hidden[:, first], near_swish, near_slope = forward_terms(
        inner_x[...], pair_rows[0], pair_rows[1]
    )
    dgate[...], dupper[...] = backward_terms(
        inner_g[...], pair_rows[2], near_swish, near_slope, scale
    )
    hidden[:, second], swish[...], slope[...] = forward_terms(
        far_x[...], pair_rows[0], pair_rows[1]
    )
    far_hidden[...], far_swish[...], far_slope[...] = forward_terms(far_x[...], rows[0], rows[1])


def pair_down(inner_g, far_g, hidden, sent, *, start, scale):
    size = inner_g.shape[0]
    columns = pl.ds(start, far_g.shape[1])
    total = over_tokens(hidden[:, :size], inner_g[:, columns])
    total += over_tokens(hidden[:, size:], far_g[...])
    sent[...] = (total * scale).astype(HALF)


def joined(parts):
    return jnp.concatenate([v[...] for v in parts], axis=1)


def pair_upper(
    inner_x, far_x, far_g, pair_rows, swish, slope, dgate, dupper, sent, far_dgate, *, scale
):
    width_scale = inner_x.shape[1] ** (-0.5)
    far_dgate[...], far_dupper = backward_terms(
        far_g[...], pair_rows[2], swish[...], slope[...], scale
    )
    total = over_tokens(dupper[...], inner_x[...]) + over_tokens(far_dupper, far_x[...])
    sent[...] = (total * width_scale).astype(HALF)


def pair_gate(inner_x, far_x, dgate, far_dgate, sent):
    width_scale = inner_x.shape[1] ** (-0.5)
    total = over_tokens(dgate[...], inner_x[...]) + over_tokens(far_dgate[...], far_x[...])
    sent[...] = (total * width_scale).astype(HALF)


def far_backward(far_x, far_g, rows, hidden, swish, slope, near, grads, *, scale):
    width_scale = far_x.shape[1] ** (-0.5)
    cots = far_g[...]
    dgate, dupper = backward_terms(cots, rows[2], swish[...], slope[...], scale)
    grads[0] = near[0] + over_tokens(dgate, far_x[...]) * width_scale
    grads[1] = near[1] + over_tokens(dupper, far_x[...]) * width_scale
    grads[2] = near[2] + over_tokens(hidden[...], cots) * scale


def line_of_four(tokens, cots, rows, sent_rows, scale):
    pairs = [(0, 1), (1, 0), (2, 3), (3, 2)]
    middle = [(1, 2), (2, 1)]
    units, width = rows.shape[1:]
    size = tokens.shape[0]

    def send(block, route):
        return lax.ppermute(block, "tp", route)

    inner_x = send(tokens, middle)
    pair_x = send(tokens, pairs)
    inner_g = send(cots, middle)
    pair_gs = [send(cots, pairs)]
    pair_rows = send(sent_rows, pairs)
    far_x = send(pair_x, middle)
    far_gs = [send(v, middle) for v in pair_gs]
    work = 20_000_000_000
    near_terms = call(
        near_forward,
        [array((units, 3 * size), t) for t in (HALF, FULL, FULL)],
        (tokens, pair_x, inner_x, rows),
        flops=work,
        name="near_forward",
    )
    near = call(
        functools.partial(near_backward, scale=scale),
        [array((3, units, width), FULL)],
        (tokens, pair_x, inner_x, cots, *pair_gs, inner_g, rows, *near_terms),
        name="near_backward",
    )[0]
    ahead = call(
        functools.partial(ahead_forward, scale=scale),
        [array((units, size), t) for t in (HALF, FULL, FULL)]
        + [array((units, 2 * size), HALF)]
        + [array((units, size), t) for t in (FULL, FULL, HALF, HALF)],
        (inner_x, far_x, inner_g, rows, pair_rows),
        after=(near,),
        flops=work,
        name="ahead_forward",
    )
    far_terms, (hidden, swish, slope, dgate, dupper) = ahead[:3], ahead[3:]
    pieces, last, start = [], (), 0
    for far_g in far_gs:
        sent = call(
            functools.partial(pair_down, start=start, scale=scale),
            [array((units, far_g.shape[1]), HALF)],
            (inner_g, far_g, hidden),
            after=last,
            name="pair_down",
        )[0]
        pieces.append(((2, start, far_g.shape[1]), [send(sent, pairs)]))
        last = (sent,)
        start += far_g.shape[1]
    sent, far_dgate = call(
        functools.partial(pair_upper, scale=scale),
        [array((units, width), HALF), array((units, size), HALF)],
        (inner_x, far_x, *far_gs, pair_rows, swish, slope, dgate, dupper),
        after=last,
        name="pair_upper",
    )
    pieces.append(((1, 0, width), [send(sent, pairs)]))
    sent = call(
        pair_gate,
        [array((units, width), HALF)],
        (inner_x, far_x, dgate, far_dgate),
        name="pair_gate",
    )[0]
    pieces.append(((0, 0, width), [send(sent, pairs)]))
    grads = call(
        functools.partial(far_backward, scale=scale),
        [array((3, units, width), FULL)],
        (far_x, *far_gs, rows, *far_terms, near),
        after=(sent,),
        name="far_backward",
    )[0]
    return grads, pieces


def gathered(tokens, cots, rows, scale):
    return unit_grads(
        lax.all_gather(tokens, "tp", axis=0, tiled=True),
        lax.all_gather(cots, "tp", axis=0, tiled=True),
        rows,
        scale,
    )


def still_kernel(rows, first, second, still, step, same_rows):
    master = rows[...].astype(FULL)
    total = adam_step(0.9 * first[...].astype(FULL), 0.95 * second[...].astype(FULL))
    step[...] = total
    still[...] = master - 0.1 * (total + 0.1 * master)
    same_rows[...] = rows[...]


def still_values(rows, first, second):
    units, width = rows.shape[1:]
    slab = pl.BlockSpec((1, units, width), lambda k: (k, 0, 0))
    return pl.pallas_call(
        still_kernel,
        grid=(3,),
        out_shape=[array(rows.shape, t) for t in (FULL, FULL, HALF)],
        in_specs=[slab] * 3,
        out_specs=[slab] * 3,
        compiler_params=pltpu.CompilerParams(vmem_limit_bytes=32 * 2**20),
        name="still",
    )(rows, first, second)


def base_kernel(still, before, after, base):
    base[...] = (still[...] + before[...] + after[...]) / 3.0


def change_kernel(grads, still_step, first, second, *rest, piece, parts):
    *came, change, sent = rest
    k, start, size = piece
    place = pl.ds(start, size)
    grad = grads[k, :, place]
    for part in came[:parts]:
        grad = grad + part[...].astype(FULL)
    moment_one = 0.9 * first[k, :, place].astype(FULL) + 0.1 * grad
    moment_two = 0.95 * second[k, :, place].astype(FULL) + 0.05 * grad * grad
    total = 0.1 * (still_step[k, :, place] - adam_step(moment_one, moment_two))
    change[...] = total
    sent[...] = total.astype(HALF)


def change_of(piece, grads, still_step, first, second, came, after):
    shape = (grads.shape[1], piece[2])
    return call(
        functools.partial(change_kernel, piece=piece, parts=len(came)),
        [array(shape, FULL), array(shape, HALF)],
        (grads, still_step, first, second, *came),
        after=after,
        name="change",
    )


def finish_kernel(base, change, before, following, *rest, piece, bands):
    out, total, done = rest[-3:]
    units = base.shape[1]
    k, start, size = piece
    columns = pl.ds(start, size)
    copies = []
    for i, band in enumerate(bands):
        place = pl.ds(band, (*bands, units)[i + 1] - band)
        around = before[place, :].astype(FULL) + following[place, :].astype(FULL)
        total[place, :] = base[k, place, columns] + (change[place, :] + around) / 3.0
        copies.append(
            pltpu.make_async_copy(total.at[place, :], out.at[k, place, columns], done.at[i])
        )
        copies[-1].start()
    for copy in copies:
        copy.wait()


def finish(piece, out, base, change, before, following, after):
    units = base.shape[1]
    bands = tuple(range(0, units - 15, 48))
    vmem, anywhere = pl.BlockSpec(memory_space=pltpu.VMEM), pl.BlockSpec(memory_space=pl.ANY)
    held = () if out is None else (out,)
    return pl.pallas_call(
        functools.partial(finish_kernel, piece=piece, bands=bands),
        out_shape=array(base.shape, FULL),
        in_specs=[vmem] * 4 + [anywhere] * (len(held) + len(after)),
        out_specs=anywhere,
        scratch_shapes=[
            pltpu.VMEM((units, piece[2]), FULL),
            pltpu.SemaphoreType.DMA((len(bands),)),
        ],
        input_output_aliases={4: 0} if held else {},
        cost_estimate=pl.CostEstimate(flops=2_000_000_000, bytes_accessed=0, transcendentals=0),
        compiler_params=pltpu.CompilerParams(vmem_limit_bytes=32 * 2**20),
        name="finish",
    )(base, change, before, following, *held, *after)


def on_device(tokens, cotangent, weights, first_moment, second_moment):
    rows, first, second = (
        jnp.swapaxes(v[0], 0, 1) for v in (weights, first_moment, second_moment)
    )
    scale = (rows.shape[1] * lax.axis_size("tp")) ** (-0.5)
    still, still_step, sent_rows = still_values(rows, first, second)
    still_before, still_after = shifted(still, "blk", 1), shifted(still, "blk", -1)
    if lax.axis_size("tp") == 4:
        grads, pieces = line_of_four(tokens, cotangent, rows, sent_rows, scale)
    else:
        grads = gathered(tokens, cotangent, rows, scale)
        pieces = [((k, 0, rows.shape[2]), []) for k in ORDER]
    base = call(
        base_kernel, [array(rows.shape, FULL)], (still, still_before, still_after), name="base"
    )[0]
    changes, last = [], (base,)
    for piece, came in pieces:
        change, sent = change_of(piece, grads, still_step, first, second, came, last)
        changes.append((piece, change, shifted(sent, "blk", 1), shifted(sent, "blk", -1)))
        last = (sent,)
    out = None
    for piece, change, before, following in changes:
        out = finish(piece, out, base, change, before, following, last)
        last = ()
    return jnp.swapaxes(out, 0, 1)[None]


def solution(mesh):
    in_specs = (
        P(("blk", "tp"), None),
        P(("blk", "tp"), None),
        P("blk", "tp", None, None),
        P("blk", "tp", None, None),
        P("blk", "tp", None, None),
    )
    out_specs = P("blk", "tp", None, None)
    return jax.shard_map(
        on_device, mesh=mesh, in_specs=in_specs, out_specs=out_specs, check_vma=False
    )
```

time: 85.3 us -> 78.4 us (0.919); the launches traced: 84.8 us -> 76.9 us
  waiting for transfers between devices: 38.4 us -> 32.3 us
  Pallas kernels: 16.9 us -> 12.3 us
  starting transfers between devices: 24.4 us -> 28.7 us
  local copies, waits for them, and re-layouts: 4.89 us -> 3.45 us
    ppermute x8, starting transfers between devices: 4.08 us -> 8.47 us  [shifted(): lax.ppermute(block, axis, [((i - distance) % count, i) for i in range(cou...]
    ppermute x8, waiting for transfers between devices: 9.46 us -> 5.39 us  [shifted(): lax.ppermute(block, axis, [((i - distance) % count, i) for i in range(cou...]
    pallas_call x6 -> x4, Pallas kernels: 7.96 us -> 4.02 us  [the longest x3 2.6 us: finish(): pl.pallas_call(functools.partial(finish_kernel, piece=piece, bands=bands)...]
    ppermute x10, waiting for transfers between devices: 28.9 us -> 26.9 us  [send(): return lax.ppermute(block, 'tp', route)]
    unnamed x18 -> x16, local copies, waits for them, and re-layouts: 4.89 us -> 3.45 us
    pallas_call x8 -> x11, Pallas kernels: 8.94 us -> 8.26 us  [call(): pl.pallas_call(body, out_shape=outs, in_specs=[pl.BlockSpec(memory_space=...]
  transfers between devices with their start and end apart: 18 -> 18, of which waited for: 10 -> 9; matrix products, arithmetic and copies ran while one was open for 0% -> 0% of each run, Pallas kernels for 18% -> 15%
where the time goes in v3:
time: 78.4 us; the launch traced here: 76.9 us
  waiting for transfers between devices  32.3 us (41%)
  starting transfers between devices  28.7 us (37%)
  Pallas kernels  12.3 us (16%)
  local copies, waits for them, and re-layouts  3.45 us (4%)
    ppermute x10, waiting for transfers between devices, send(): return lax.ppermute(block, 'tp', route)  26.9 us
    ppermute x10, starting transfers between devices, send(): return lax.ppermute(block, 'tp', route)  20.2 us
    ppermute x8, starting transfers between devices, shifted(): lax.ppermute(block, axis, [((i - distance) % count, i) for i in range(cou...  8.47 us
    pallas_call x11, Pallas kernels, call(): pl.pallas_call(body, out_shape=outs, in_specs=[pl.BlockSpec(memory_space=...  8.26 us
    ppermute x8, waiting for transfers between devices, shifted(): lax.ppermute(block, axis, [((i - distance) % count, i) for i in range(cou...  5.39 us
    unnamed x16, local copies, waits for them, and re-layouts  3.45 us
    pallas_call x3, Pallas kernels, finish(): pl.pallas_call(functools.partial(finish_kernel, piece=piece, bands=bands)...  2.6 us
  transfers between devices with their start and end apart: 18, of which 9 were waited for; matrix products, arithmetic and copies ran while one was open for 0% of the time, Pallas kernels for 15%

profile of v3, /device:TPU:0, one launch (start us, length us, event | category | flops | bytes accessed | tf_op | source)
XLA Modules:
  0.0 76.9 jit_solution(13495069363436354785)
XLA Ops:
  0.0 3.0 %collective-permute-start.2 = (bf16[256,896]{1,0:T(8,128)(2,1)}, bf16[256,896]{1,0:T(8,128)(2,1)S(1)}, u32[]{:S(2)}, u32[]{:S(2)}) collective-permute-start(bf16[256,896]{1,0:T(8,128)(2,1)} %refs_0_.3), channel_id=1, source_target_pairs={{0,1},{1,0},{2,3},{3,2},{4,5},{5,4},{6,7},{7,6},{8,9},{9,8},{10,11... | collective-permute-start | bytes 1376264 | tf_op jit(solution)/shard_map/ppermute | solution.py:174
  3.0 0.7 collective-permute-start.6
  3.7 4.4 %collective-permute-start.4 = (bf16[256,896]{1,0:T(8,128)(2,1)}, bf16[256,896]{1,0:T(8,128)(2,1)S(1)}, u32[]{:S(2)}, u32[]{:S(2)}) collective-permute-start(bf16[256,896]{1,0:T(8,128)(2,1)} %refs_3_.1), channel_id=1, source_target_pairs={{0,1},{1,0},{2,3},{3,2},{4,5},{5,4},{6,7},{7,6},{8,9},{9,8},{10,11... | collective-permute-start | bytes 1376264 | tf_op jit(solution)/shard_map/ppermute | solution.py:174
  8.1 0.7 collective-permute-start.7
  8.8 0.0 copy-start
  8.8 1.1 %copy-done = bf16[1,152,3,896]{3,1,2,0:T(8,128)(2,1)S(1)} copy-done((bf16[1,152,3,896]{3,1,2,0:T(8,128)(2,1)S(1)}, bf16[1,152,3,896]{3,1,2,0:T(8,128)(2,1)}, u32[]{:S(2)}) %copy-start) | copy-done | bytes 817176
  10.0 1.1 %copy-done.2 = bf16[1,152,3,896]{3,1,2,0:T(8,128)(2,1)S(1)} copy-done((bf16[1,152,3,896]{3,1,2,0:T(8,128)(2,1)S(1)}, bf16[1,152,3,896]{3,1,2,0:T(8,128)(2,1)}, u32[]{:S(2)}) %copy-start.2) | copy-done | bytes 817176
  11.1 1.1 %copy-done.4 = bf16[1,152,3,896]{3,1,2,0:T(8,128)(2,1)S(1)} copy-done((bf16[1,152,3,896]{3,1,2,0:T(8,128)(2,1)S(1)}, bf16[1,152,3,896]{3,1,2,0:T(8,128)(2,1)}, u32[]{:S(2)}) %copy-start.4) | copy-done | bytes 817176
  12.3 1.4 %still.1 = (f32[3,152,896]{2,1,0:T(8,128)S(1)}, f32[3,152,896]{2,1,0:T(8,128)S(1)}, bf16[3,152,896]{2,1,0:T(8,128)(2,1)S(1)}) custom-call(bf16[3,152,896]{2,1,0:T(8,128)(2,1)S(1)} %bitcast.20, bf16[3,152,896]{2,1,0:T(8,128)(2,1)S(1)} %bitcast.12, bf16[3,152,896]{2,1,0:T(8,128)(2,1)S(1)} %bitcast.16), custom_call_target="tpu_custom_call" | custom-call | tf_op jit(solution)/shard_map/still/pallas_call | solution.py:265
  13.7 0.1 collective-permute-start
  13.8 0.8 %collective-permute-done.2.refs_1_ = bf16[256,896]{1,0:T(8,128)(2,1)S(1)} collective-permute-done((bf16[256,896]{1,0:T(8,128)(2,1)}, bf16[256,896]{1,0:T(8,128)(2,1)S(1)}, u32[]{:S(2)}, u32[]{:S(2)}) %collective-permute-start.2) | collective-permute-done | bytes 458784 | tf_op jit(solution)/shard_map/ppermute | solution.py:174
  14.6 2.1 %collective-permute-start.8 = (bf16[3,152,896]{2,1,0:T(8,128)(2,1)S(1)}, bf16[3,152,896]{2,1,0:T(8,128)(2,1)S(1)}, u32[]{:S(2)}, u32[]{:S(2)}) collective-permute-start(bf16[3,152,896]{2,1,0:T(8,128)(2,1)S(1)} %get-tuple-element.28), channel_id=1, source_target_pairs={{0,1},{1,0},{2,3},{3,2},{4,5},{5,4},{6,7},{7,6},{8,9},{9,8},{10,11... | collective-permute-start | bytes 2451464 | tf_op jit(solution)/shard_map/ppermute | solution.py:174
  16.6 0.7 collective-permute-start.3
  17.3 1.1 %near_forward.1 = (bf16[152,768]{1,0:T(8,128)(2,1)S(1)}, f32[152,768]{1,0:T(8,128)S(1)}, f32[152,768]{1,0:T(8,128)S(1)}) custom-call(bf16[256,896]{1,0:T(8,128)(2,1)S(1)} %copy-done.6, bf16[256,896]{1,0:T(8,128)(2,1)S(1)} %collective-permute-done.2.refs_1_, bf16[256,896]{1,0:T(8,128)(2,1)S(1)} %collective-permute-done.6.refs_2_.refs_0_, ...), custom_call_target="tpu_custom_call" | custom-call | flops 20000000000 | tf_op jit(solution)/shard_map/near_forward/pallas_call | solution.py:68
  18.5 5.9 %collective-permute-done.4.refs_4_ = bf16[256,896]{1,0:T(8,128)(2,1)S(1)} collective-permute-done((bf16[256,896]{1,0:T(8,128)(2,1)}, bf16[256,896]{1,0:T(8,128)(2,1)S(1)}, u32[]{:S(2)}, u32[]{:S(2)}) %collective-permute-start.4) | collective-permute-done | bytes 458784 | tf_op jit(solution)/shard_map/ppermute | solution.py:174
  24.4 0.4 collective-permute-start.1
  24.8 0.7 collective-permute-start.5
  25.5 1.8 %near_backward.1.refs_5_.refs_6_ = f32[3,152,896]{2,1,0:T(8,128)S(1)} custom-call(bf16[256,896]{1,0:T(8,128)(2,1)S(1)} %copy-done.6, bf16[256,896]{1,0:T(8,128)(2,1)S(1)} %collective-permute-done.2.refs_1_, bf16[256,896]{1,0:T(8,128)(2,1)S(1)} %collective-permute-done.6.refs_2_.refs_0_, bf16[256,896]{1,0:T(8,128)(2,1)S(1)} %copy-done.7, ...), custom_call_target="tpu_custom_call" | custom-call | tf_op jit(solution)/shard_map/near_backward/pallas_call | solution.py:68
  27.3 13.8 %collective-permute-done.8.refs_4_.refs_3_ = bf16[3,152,896]{2,1,0:T(8,128)(2,1)S(1)} collective-permute-done((bf16[3,152,896]{2,1,0:T(8,128)(2,1)S(1)}, bf16[3,152,896]{2,1,0:T(8,128)(2,1)S(1)}, u32[]{:S(2)}, u32[]{:S(2)}) %collective-permute-start.8) | collective-permute-done | bytes 817184 | tf_op jit(solution)/shard_map/ppermute | solution.py:174
  41.1 1.2 %ahead_forward.1 = (bf16[152,256]{1,0:T(8,128)(2,1)S(1)}, f32[152,256]{1,0:T(8,128)S(1)}, f32[152,256]{1,0:T(8,128)S(1)}, bf16[152,512]{1,0:T(8,128)(2,1)S(1)}, ...) custom-call(bf16[256,896]{1,0:T(8,128)(2,1)S(1)} %collective-permute, ...), custom_call_target="tpu_custom_call" | custom-call | flops 20000000000 | tf_op jit(solution)/shard_map/ahead_forward/pallas_call | solution.py:68
  42.3 0.3 pair_down.1.refs_8_
  42.6 5.8 %collective-permute-start.11 = (bf16[152,896]{1,0:T(8,128)(2,1)S(1)}, bf16[152,896]{1,0:T(8,128)(2,1)S(1)}, u32[]{:S(2)}, u32[]{:S(2)}) collective-permute-start(bf16[152,896]{1,0:T(8,128)(2,1)S(1)} %pair_down.1.refs_8_), channel_id=1, source_target_pairs={{0,1},{1,0},{2,3},{3,2},{4,5},{5,4},{6,7},{7,6},{8,9},{9,8},{10,11... | collective-permute-start | bytes 817160 | tf_op jit(solution)/shard_map/ppermute | solution.py:174
  48.4 0.8 %pair_upper.1 = (bf16[152,896]{1,0:T(8,128)(2,1)S(1)}, bf16[152,256]{1,0:T(8,128)(2,1)S(1)}) custom-call(bf16[256,896]{1,0:T(8,128)(2,1)S(1)} %collective-permute-done.6.refs_2_.refs_0_, bf16[256,896]{1,0:T(8,128)(2,1)S(1)} %collective-permute-done.3.refs_1_.refs_0_, bf16[256,896]{1,0:T(8,128)(2,1)S(1)} %collective-permute-done.5.refs_1_.refs_2_, ...), custom_call_target="tpu_custom_call" | custom-call | tf_op jit(solution)/shard_map/pair_upper/pallas_call | solution.py:68
  49.2 0.1 collective-permute-start.10
  49.3 0.3 pair_gate.1.refs_7_
  49.7 2.1 %collective-permute-start.9 = (bf16[152,896]{1,0:T(8,128)(2,1)S(1)}, bf16[152,896]{1,0:T(8,128)(2,1)S(1)}, u32[]{:S(2)}, u32[]{:S(2)}) collective-permute-start(bf16[152,896]{1,0:T(8,128)(2,1)S(1)} %pair_gate.1.refs_7_), channel_id=1, source_target_pairs={{0,1},{1,0},{2,3},{3,2},{4,5},{5,4},{6,7},{7,6},{8,9},{9,8},{10,11... | collective-permute-start | bytes 817160 | tf_op jit(solution)/shard_map/ppermute | solution.py:174
  51.7 0.9 %far_backward.1.refs_0_ = f32[3,152,896]{2,1,0:T(8,128)S(1)} custom-call(bf16[256,896]{1,0:T(8,128)(2,1)S(1)} %collective-permute-done.3.refs_1_.refs_0_, bf16[256,896]{1,0:T(8,128)(2,1)S(1)} %collective-permute-done.5.refs_1_.refs_2_, bf16[3,152,896]{2,1,0:T(8,128)(2,1)S(1)} %bitcast.24, bf16[152,256]{1,0:T(8,128)(2,1)S(1)} %get-tuple-element.32.refs_3_, ...), custom_call_target="tpu_custom_call" | custom-call | tf_op jit(solution)/shard_map/far_backward/pallas_call | solution.py:68
  52.6 0.0 copy-start.1
  52.6 0.0 copy-start.3
  52.7 0.4 base.1.refs_5_
  53.0 2.8 %collective-permute-done.11.refs_4_ = bf16[152,896]{1,0:T(8,128)(2,1)S(1)} collective-permute-done((bf16[152,896]{1,0:T(8,128)(2,1)S(1)}, bf16[152,896]{1,0:T(8,128)(2,1)S(1)}, u32[]{:S(2)}, u32[]{:S(2)}) %collective-permute-start.11) | collective-permute-done | bytes 272416 | tf_op jit(solution)/shard_map/ppermute | solution.py:174
  55.9 0.5 change.3
  56.3 0.1 collective-permute-start.16
  56.4 2.6 %collective-permute-start.17 = (bf16[152,896]{1,0:T(8,128)(2,1)S(1)}, bf16[152,896]{1,0:T(8,128)(2,1)S(1)}, u32[]{:S(2)}, u32[]{:S(2)}) collective-permute-start(bf16[152,896]{1,0:T(8,128)(2,1)S(1)} %get-tuple-element.43.refs_5_), channel_id=1, source_target_pairs={{4,0},{8,4},{12,8},{16,12},{20,16},{24,20},{28,24},{0,28},{5,1},{9... | collective-permute-start | bytes 817160 | tf_op jit(solution)/shard_map/ppermute | solution.py:20
  59.0 2.7 %collective-permute-done.10.refs_4_ = bf16[152,896]{1,0:T(8,128)(2,1)S(1)} collective-permute-done((bf16[152,896]{1,0:T(8,128)(2,1)S(1)}, bf16[152,896]{1,0:T(8,128)(2,1)S(1)}, u32[]{:S(2)}, u32[]{:S(2)}) %collective-permute-start.10) | collective-permute-done | bytes 272416 | tf_op jit(solution)/shard_map/ppermute | solution.py:174
  61.7 0.5 change.4
  62.2 0.1 collective-permute-start.14
  62.2 2.6 %collective-permute-start.15 = (bf16[152,896]{1,0:T(8,128)(2,1)S(1)}, bf16[152,896]{1,0:T(8,128)(2,1)S(1)}, u32[]{:S(2)}, u32[]{:S(2)}) collective-permute-start(bf16[152,896]{1,0:T(8,128)(2,1)S(1)} %get-tuple-element.44.refs_5_), channel_id=1, source_target_pairs={{4,0},{8,4},{12,8},{16,12},{20,16},{24,20},{28,24},{0,28},{5,1},{9... | collective-permute-start | bytes 817160 | tf_op jit(solution)/shard_map/ppermute | solution.py:20
  64.9 0.9 %collective-permute-done.9.refs_4_ = bf16[152,896]{1,0:T(8,128)(2,1)S(1)} collective-permute-done((bf16[152,896]{1,0:T(8,128)(2,1)S(1)}, bf16[152,896]{1,0:T(8,128)(2,1)S(1)}, u32[]{:S(2)}, u32[]{:S(2)}) %collective-permute-start.9) | collective-permute-done | bytes 272416 | tf_op jit(solution)/shard_map/ppermute | solution.py:174
  65.7 0.5 change.5
  66.2 0.1 collective-permute-start.12
  66.3 2.6 %collective-permute-start.13 = (bf16[152,896]{1,0:T(8,128)(2,1)S(1)}, bf16[152,896]{1,0:T(8,128)(2,1)S(1)}, u32[]{:S(2)}, u32[]{:S(2)}) collective-permute-start(bf16[152,896]{1,0:T(8,128)(2,1)S(1)} %get-tuple-element.46.rest_0_), channel_id=1, source_target_pairs={{4,0},{8,4},{12,8},{16,12},{20,16},{24,20},{28,24},{0,28},{5,1},{9... | collective-permute-start | bytes 817160 | tf_op jit(solution)/shard_map/ppermute | solution.py:20
  68.9 0.9 %finish.3.rest_0_ = f32[3,152,896]{2,1,0:T(8,128)} custom-call(f32[3,152,896]{2,1,0:T(8,128)S(1)} %base.1.refs_5_, f32[152,896]{1,0:T(8,128)S(1)} %get-tuple-element.48.change, bf16[152,896]{1,0:T(8,128)(2,1)S(1)} %collective-permute-done.16.before, bf16[152,896]{1,0:T(8,128)(2,1)S(1)} %collective-permute-done.17.following, ...), custom_call_target="tpu_custom_call" | custom-call | flops 2000000000 | tf_op jit(solution)/shard_map/finish/pallas_call | solution.py:328
  69.8 0.3 collective-permute-done.14.before
  70.1 1.8 %collective-permute-done.15.following = bf16[152,896]{1,0:T(8,128)(2,1)S(1)} collective-permute-done((bf16[152,896]{1,0:T(8,128)(2,1)S(1)}, bf16[152,896]{1,0:T(8,128)(2,1)S(1)}, u32[]{:S(2)}, u32[]{:S(2)}) %collective-permute-start.15) | collective-permute-done | bytes 272416 | tf_op jit(solution)/shard_map/ppermute | solution.py:20
  71.9 0.9 %finish.4.rest_0_ = f32[3,152,896]{2,1,0:T(8,128)} custom-call(f32[3,152,896]{2,1,0:T(8,128)S(1)} %base.1.refs_5_, f32[152,896]{1,0:T(8,128)S(1)} %get-tuple-element.47.change, bf16[152,896]{1,0:T(8,128)(2,1)S(1)} %collective-permute-done.14.before, bf16[152,896]{1,0:T(8,128)(2,1)S(1)} %collective-permute-done.15.following, ...), custom_call_target="tpu_custom_call", output_to_operand_aliasing={{}: (4, {})} | custom-call | flops 2000000000 | tf_op jit(solution)/shard_map/finish/pallas_call | solution.py:328
  72.7 3.3 %collective-permute-done.12.before = bf16[152,896]{1,0:T(8,128)(2,1)S(1)} collective-permute-done((bf16[152,896]{1,0:T(8,128)(2,1)S(1)}, bf16[152,896]{1,0:T(8,128)(2,1)S(1)}, u32[]{:S(2)}, u32[]{:S(2)}) %collective-permute-start.12) | collective-permute-done | bytes 272416 | tf_op jit(solution)/shard_map/ppermute | solution.py:20
  76.1 0.9 %finish.5 = f32[3,152,896]{2,1,0:T(8,128)} custom-call(f32[3,152,896]{2,1,0:T(8,128)S(1)} %base.1.refs_5_, f32[152,896]{1,0:T(8,128)S(1)} %get-tuple-element.45.change, bf16[152,896]{1,0:T(8,128)(2,1)S(1)} %collective-permute-done.12.before, bf16[152,896]{1,0:T(8,128)(2,1)S(1)} %collective-permute-done.13.following, ...), custom_call_target="tpu_custom_call", output_to_operand_aliasing={{}: (4, {})} | custom-call | flops 2000000000 | tf_op jit(solution)/shard_map/finish/pallas_call | solution.py:328
  (19 shorter events, 0.0 us)
Async XLA Ops:
  0.0 14.6 %collective-permute-start.2 = (bf16[256,896]{1,0:T(8,128)(2,1)}, bf16[256,896]{1,0:T(8,128)(2,1)S(1)}, u32[]{:S(2)}, u32[]{:S(2)}) collective-permute-start(bf16[256,896]{1,0:T(8,128)(2,1)} %refs_0_.3), channel_id=1, source_target_pairs={{0,1},{1,0},{2,3},{3,2},{4,5},{5,4},{6,7},{7,6},{8,9},{9,8},{10,11... | collective-permute-start | bytes 1376264 | tf_op jit(solution)/shard_map/ppermute | solution.py:174
  3.0 13.6 %collective-permute-start.6 = (bf16[256,896]{1,0:T(8,128)(2,1)}, bf16[256,896]{1,0:T(8,128)(2,1)S(1)}, u32[]{:S(2)}, u32[]{:S(2)}) collective-permute-start(bf16[256,896]{1,0:T(8,128)(2,1)} %refs_0_.3), channel_id=1, source_target_pairs={{1,2},{2,1},{5,6},{6,5},{9,10},{10,9},{13,14},{14,13},{17,18},{18,... | collective-permute-start | bytes 1376264 | tf_op jit(solution)/shard_map/ppermute | solution.py:174
  3.7 20.7 %collective-permute-start.4 = (bf16[256,896]{1,0:T(8,128)(2,1)}, bf16[256,896]{1,0:T(8,128)(2,1)S(1)}, u32[]{:S(2)}, u32[]{:S(2)}) collective-permute-start(bf16[256,896]{1,0:T(8,128)(2,1)} %refs_3_.1), channel_id=1, source_target_pairs={{0,1},{1,0},{2,3},{3,2},{4,5},{5,4},{6,7},{7,6},{8,9},{9,8},{10,11... | collective-permute-start | bytes 1376264 | tf_op jit(solution)/shard_map/ppermute | solution.py:174
  8.1 16.6 %collective-permute-start.7 = (bf16[256,896]{1,0:T(8,128)(2,1)}, bf16[256,896]{1,0:T(8,128)(2,1)S(1)}, u32[]{:S(2)}, u32[]{:S(2)}) collective-permute-start(bf16[256,896]{1,0:T(8,128)(2,1)} %refs_3_.1), channel_id=1, source_target_pairs={{1,2},{2,1},{5,6},{6,5},{9,10},{10,9},{13,14},{14,13},{17,18},{18,... | collective-permute-start | bytes 1376264 | tf_op jit(solution)/shard_map/ppermute | solution.py:174
  8.8 1.1 %copy-start = (bf16[1,152,3,896]{3,1,2,0:T(8,128)(2,1)S(1)}, bf16[1,152,3,896]{3,1,2,0:T(8,128)(2,1)}, u32[]{:S(2)}) copy-start(bf16[1,152,3,896]{3,1,2,0:T(8,128)(2,1)} %param.8) | copy-start | bytes 2451460
  10.0 1.1 %copy-start.2 = (bf16[1,152,3,896]{3,1,2,0:T(8,128)(2,1)S(1)}, bf16[1,152,3,896]{3,1,2,0:T(8,128)(2,1)}, u32[]{:S(2)}) copy-start(bf16[1,152,3,896]{3,1,2,0:T(8,128)(2,1)} %param.9) | copy-start | bytes 2451460
  11.1 1.1 %copy-start.4 = (bf16[1,152,3,896]{3,1,2,0:T(8,128)(2,1)S(1)}, bf16[1,152,3,896]{3,1,2,0:T(8,128)(2,1)}, u32[]{:S(2)}) copy-start(bf16[1,152,3,896]{3,1,2,0:T(8,128)(2,1)} %param.7) | copy-start | bytes 2451460
  12.3 5.1 %copy-start.6 = (bf16[256,896]{1,0:T(8,128)(2,1)S(1)}, bf16[256,896]{1,0:T(8,128)(2,1)}, u32[]{:S(2)}) copy-start(bf16[256,896]{1,0:T(8,128)(2,1)} %refs_0_.3) | copy-start | bytes 1376260
  13.7 39.0 %collective-permute-start = (f32[3,152,896]{2,1,0:T(8,128)S(1)}, f32[3,152,896]{2,1,0:T(8,128)S(1)}, u32[]{:S(2)}, u32[]{:S(2)}) collective-permute-start(f32[3,152,896]{2,1,0:T(8,128)S(1)} %get-tuple-element.27.refs_0_), channel_id=1, source_target_pairs={{28,0},{0,4},{4,8},{8,12},{12,16},{16,20},{20,24},{24,28},{29,1},{... | collective-permute-start | bytes 4902920 | tf_op jit(solution)/shard_map/ppermute | solution.py:20
  14.6 10.9 %copy-start.7 = (bf16[256,896]{1,0:T(8,128)(2,1)S(1)}, bf16[256,896]{1,0:T(8,128)(2,1)}, u32[]{:S(2)}) copy-start(bf16[256,896]{1,0:T(8,128)(2,1)} %refs_3_.1) | copy-start | bytes 1376260
  14.6 26.5 %collective-permute-start.8 = (bf16[3,152,896]{2,1,0:T(8,128)(2,1)S(1)}, bf16[3,152,896]{2,1,0:T(8,128)(2,1)S(1)}, u32[]{:S(2)}, u32[]{:S(2)}) collective-permute-start(bf16[3,152,896]{2,1,0:T(8,128)(2,1)S(1)} %get-tuple-element.28), channel_id=1, source_target_pairs={{0,1},{1,0},{2,3},{3,2},{4,5},{5,4},{6,7},{7,6},{8,9},{9,8},{10,11... | collective-permute-start | bytes 2451464 | tf_op jit(solution)/shard_map/ppermute | solution.py:174
  16.6 24.4 %collective-permute-start.3 = (bf16[256,896]{1,0:T(8,128)(2,1)S(1)}, bf16[256,896]{1,0:T(8,128)(2,1)S(1)}, u32[]{:S(2)}, u32[]{:S(2)}) collective-permute-start(bf16[256,896]{1,0:T(8,128)(2,1)S(1)} %collective-permute-done.2.refs_1_), channel_id=1, source_target_pairs={{1,2},{2,1},{5,6},{6,5},{9,10},{10,9},{13,14},{14,13},{17,18},{18,... | collective-permute-start | bytes 1376264 | tf_op jit(solution)/shard_map/ppermute | solution.py:174
  24.4 28.3 %collective-permute-start.1 = (f32[3,152,896]{2,1,0:T(8,128)S(1)}, f32[3,152,896]{2,1,0:T(8,128)S(1)}, u32[]{:S(2)}, u32[]{:S(2)}) collective-permute-start(f32[3,152,896]{2,1,0:T(8,128)S(1)} %get-tuple-element.27.refs_0_), channel_id=1, source_target_pairs={{4,0},{8,4},{12,8},{16,12},{20,16},{24,20},{28,24},{0,28},{5,1},{9... | collective-permute-start | bytes 4902920 | tf_op jit(solution)/shard_map/ppermute | solution.py:20
  24.8 17.5 %collective-permute-start.5 = (bf16[256,896]{1,0:T(8,128)(2,1)S(1)}, bf16[256,896]{1,0:T(8,128)(2,1)S(1)}, u32[]{:S(2)}, u32[]{:S(2)}) collective-permute-start(bf16[256,896]{1,0:T(8,128)(2,1)S(1)} %collective-permute-done.4.refs_4_), channel_id=1, source_target_pairs={{1,2},{2,1},{5,6},{6,5},{9,10},{10,9},{13,14},{14,13},{17,18},{18,... | collective-permute-start | bytes 1376264 | tf_op jit(solution)/shard_map/ppermute | solution.py:174
  42.6 13.2 %collective-permute-start.11 = (bf16[152,896]{1,0:T(8,128)(2,1)S(1)}, bf16[152,896]{1,0:T(8,128)(2,1)S(1)}, u32[]{:S(2)}, u32[]{:S(2)}) collective-permute-start(bf16[152,896]{1,0:T(8,128)(2,1)S(1)} %pair_down.1.refs_8_), channel_id=1, source_target_pairs={{0,1},{1,0},{2,3},{3,2},{4,5},{5,4},{6,7},{7,6},{8,9},{9,8},{10,11... | collective-permute-start | bytes 817160 | tf_op jit(solution)/shard_map/ppermute | solution.py:174
  48.4 3.3 %copy-start.5 = (bf16[1,152,3,896]{3,1,2,0:T(8,128)(2,1)S(1)}, bf16[1,152,3,896]{3,1,2,0:T(8,128)(2,1)}, u32[]{:S(2)}) copy-start(bf16[1,152,3,896]{3,1,2,0:T(8,128)(2,1)} %param.7) | copy-start | bytes 2451460
  49.2 12.5 %collective-permute-start.10 = (bf16[152,896]{1,0:T(8,128)(2,1)S(1)}, bf16[152,896]{1,0:T(8,128)(2,1)S(1)}, u32[]{:S(2)}, u32[]{:S(2)}) collective-permute-start(bf16[152,896]{1,0:T(8,128)(2,1)S(1)} %get-tuple-element.42), channel_id=1, source_target_pairs={{0,1},{1,0},{2,3},{3,2},{4,5},{5,4},{6,7},{7,6},{8,9},{9,8},{10,11... | collective-permute-start | bytes 817160 | tf_op jit(solution)/shard_map/ppermute | solution.py:174
  49.7 16.1 %collective-permute-start.9 = (bf16[152,896]{1,0:T(8,128)(2,1)S(1)}, bf16[152,896]{1,0:T(8,128)(2,1)S(1)}, u32[]{:S(2)}, u32[]{:S(2)}) collective-permute-start(bf16[152,896]{1,0:T(8,128)(2,1)S(1)} %pair_gate.1.refs_7_), channel_id=1, source_target_pairs={{0,1},{1,0},{2,3},{3,2},{4,5},{5,4},{6,7},{7,6},{8,9},{9,8},{10,11... | collective-permute-start | bytes 817160 | tf_op jit(solution)/shard_map/ppermute | solution.py:174
  52.6 3.2 %copy-start.1 = (bf16[1,152,3,896]{3,1,2,0:T(8,128)(2,1)S(1)}, bf16[1,152,3,896]{3,1,2,0:T(8,128)(2,1)}, u32[]{:S(2)}) copy-start(bf16[1,152,3,896]{3,1,2,0:T(8,128)(2,1)} %param.8) | copy-start | bytes 2451460
  52.6 3.2 %copy-start.3 = (bf16[1,152,3,896]{3,1,2,0:T(8,128)(2,1)S(1)}, bf16[1,152,3,896]{3,1,2,0:T(8,128)(2,1)}, u32[]{:S(2)}) copy-start(bf16[1,152,3,896]{3,1,2,0:T(8,128)(2,1)} %param.9) | copy-start | bytes 2451460
  56.3 9.9 %collective-permute-start.16 = (bf16[152,896]{1,0:T(8,128)(2,1)S(1)}, bf16[152,896]{1,0:T(8,128)(2,1)S(1)}, u32[]{:S(2)}, u32[]{:S(2)}) collective-permute-start(bf16[152,896]{1,0:T(8,128)(2,1)S(1)} %get-tuple-element.43.refs_5_), channel_id=1, source_target_pairs={{28,0},{0,4},{4,8},{8,12},{12,16},{16,20},{20,24},{24,28},{29,1},{... | collective-permute-start | bytes 817160 | tf_op jit(solution)/shard_map/ppermute | solution.py:20
  56.4 12.5 %collective-permute-start.17 = (bf16[152,896]{1,0:T(8,128)(2,1)S(1)}, bf16[152,896]{1,0:T(8,128)(2,1)S(1)}, u32[]{:S(2)}, u32[]{:S(2)}) collective-permute-start(bf16[152,896]{1,0:T(8,128)(2,1)S(1)} %get-tuple-element.43.refs_5_), channel_id=1, source_target_pairs={{4,0},{8,4},{12,8},{16,12},{20,16},{24,20},{28,24},{0,28},{5,1},{9... | collective-permute-start | bytes 817160 | tf_op jit(solution)/shard_map/ppermute | solution.py:20
  62.2 7.9 %collective-permute-start.14 = (bf16[152,896]{1,0:T(8,128)(2,1)S(1)}, bf16[152,896]{1,0:T(8,128)(2,1)S(1)}, u32[]{:S(2)}, u32[]{:S(2)}) collective-permute-start(bf16[152,896]{1,0:T(8,128)(2,1)S(1)} %get-tuple-element.44.refs_5_), channel_id=1, source_target_pairs={{28,0},{0,4},{4,8},{8,12},{12,16},{16,20},{20,24},{24,28},{29,1},{... | collective-permute-start | bytes 817160 | tf_op jit(solution)/shard_map/ppermute | solution.py:20
  62.2 9.6 %collective-permute-start.15 = (bf16[152,896]{1,0:T(8,128)(2,1)S(1)}, bf16[152,896]{1,0:T(8,128)(2,1)S(1)}, u32[]{:S(2)}, u32[]{:S(2)}) collective-permute-start(bf16[152,896]{1,0:T(8,128)(2,1)S(1)} %get-tuple-element.44.refs_5_), channel_id=1, source_target_pairs={{4,0},{8,4},{12,8},{16,12},{20,16},{24,20},{28,24},{0,28},{5,1},{9... | collective-permute-start | bytes 817160 | tf_op jit(solution)/shard_map/ppermute | solution.py:20
  66.2 9.8 %collective-permute-start.12 = (bf16[152,896]{1,0:T(8,128)(2,1)S(1)}, bf16[152,896]{1,0:T(8,128)(2,1)S(1)}, u32[]{:S(2)}, u32[]{:S(2)}) collective-permute-start(bf16[152,896]{1,0:T(8,128)(2,1)S(1)} %get-tuple-element.46.rest_0_), channel_id=1, source_target_pairs={{28,0},{0,4},{4,8},{8,12},{12,16},{16,20},{20,24},{24,28},{29,1},{... | collective-permute-start | bytes 817160 | tf_op jit(solution)/shard_map/ppermute | solution.py:20
  66.3 9.8 %collective-permute-start.13 = (bf16[152,896]{1,0:T(8,128)(2,1)S(1)}, bf16[152,896]{1,0:T(8,128)(2,1)S(1)}, u32[]{:S(2)}, u32[]{:S(2)}) collective-permute-start(bf16[152,896]{1,0:T(8,128)(2,1)S(1)} %get-tuple-element.46.rest_0_), channel_id=1, source_target_pairs={{4,0},{8,4},{12,8},{16,12},{20,16},{24,20},{28,24},{0,28},{5,1},{9... | collective-permute-start | bytes 817160 | tf_op jit(solution)/shard_map/ppermute | solution.py:20

commit v4 on v2

v4 whole, which is shorter than its diff:
```python
import functools

import jax
import jax.numpy as jnp
from jax import lax
from jax.experimental import pallas as pl
from jax.experimental.pallas import tpu as pltpu
from jax.sharding import PartitionSpec as P

STEP = 10
CORRECT_ONE = 1.0 - 0.9**STEP
CORRECT_TWO = 1.0 - 0.95**STEP
HALF = jnp.bfloat16
FULL = jnp.float32
ORDER = (2, 1, 0)
AHEAD = 2
STILL_BY = 0
PIECES = (5, 6, 6)
NEAR_WORK = 5_000_000_000
PAIR_WORK = 20_000_000_000
AHEAD_WORK = 20_000_000_000
ACROSS_WORK = (20_000_000_000, 2_000_000_000, 2_000_000_000, 30_000_000_000)
FAR_WORK = 20_000_000_000


def neighbour(block, side):
    count = lax.axis_size("blk")
    if count % 2:
        route = [((i + 1 - 2 * side) % count, i) for i in range(count)]
    else:
        route = [((side + i) % count, (side + i + 1) % count) for i in range(0, count, 2)]
        route += [(j, i) for i, j in route]
    return lax.ppermute(block, "blk", route)


def adam_step(moment_one, moment_two):
    return moment_one / CORRECT_ONE / (jnp.sqrt(moment_two / CORRECT_TWO) + 1e-08)


def into_units(matrix, values):
    return lax.dot_general(matrix, values, (((1,), (1,)), ((), ())), preferred_element_type=FULL)


def over_tokens(terms, values):
    return lax.dot_general(terms, values, (((1,), (0,)), ((), ())), preferred_element_type=FULL)


def forward_terms(xs, gate_rows, upper_rows):
    scale = xs.shape[1] ** (-0.5)
    gate = into_units(gate_rows, xs) * scale
    upper = into_units(upper_rows, xs) * scale
    sigma = 1.0 / (1.0 + jnp.exp(-gate))
    swish = gate * sigma
    return (swish * upper).astype(HALF), swish, upper * sigma * (1.0 + gate * (1.0 - sigma))


def backward_terms(cots, down_rows, swish, slope, scale):
    back = into_units(down_rows, cots) * scale
    return (back * slope).astype(HALF), (back * swish).astype(HALF)


def unit_grads(xs, cots, rows, scale):
    hidden, swish, slope = forward_terms(xs, rows[0], rows[1])
    dgate, dupper = backward_terms(cots, rows[2], swish, slope, scale)
    width_scale = xs.shape[1] ** (-0.5)
    return jnp.stack(
        [
            over_tokens(dgate, xs) * width_scale,
            over_tokens(dupper, xs) * width_scale,
            over_tokens(hidden, cots) * scale,
        ]
    )


def call(kernel, outs, ins, after=(), flops=0, name=None):
    count = len(ins)

    def body(*refs):
        kernel(*refs[:count], *refs[count + len(after) :])

    return pl.pallas_call(
        body,
        out_shape=outs,
        in_specs=[pl.BlockSpec(memory_space=pltpu.VMEM)] * count
        + [pl.BlockSpec(memory_space=pl.ANY)] * len(after),
        out_specs=[pl.BlockSpec(memory_space=pltpu.VMEM)] * len(outs),
        cost_estimate=pl.CostEstimate(flops=flops, bytes_accessed=0, transcendentals=0),
        compiler_params=pltpu.CompilerParams(vmem_limit_bytes=32 * 2**20),
        name=name,
    )(*ins, *after)


def array(shape, dtype):
    return jax.ShapeDtypeStruct(shape, dtype)


def near_forward(*refs):
    *shards, rows, hidden, swish, slope = refs
    size = shards[0].shape[0]
    for i, xs in enumerate(shards):
        place = pl.ds(i * size, size)
        hidden[:, place], swish[:, place], slope[:, place] = forward_terms(
            xs[...], rows[0], rows[1]
        )


def joined(*parts):
    return jnp.concatenate([v[...] for v in parts], axis=1)


def inner_forward(*refs):
    near_forward(*refs[:-1])
    rows, top = refs[2], refs[-1]
    top[...] = rows[:2]


def near_backward(
    own_x, inner_x, pair_x, own_g, inner_g, pair_g,
    rows, hidden, swish, slope, pair_hidden, pair_swish, pair_slope, grads, more, *, scale
):
    size, width = own_x.shape
    more[...] = pair_g[:, width - more.shape[1] :]
    totals = [0.0, 0.0, 0.0]
    first, second = pl.ds(0, size), pl.ds(size, size)
    shards = (
        (own_x, own_g[...], hidden[:, first], swish[:, first], slope[:, first]),
        (inner_x, inner_g[...], hidden[:, second], swish[:, second], slope[:, second]),
        (pair_x, pair_g[...], pair_hidden[...], pair_swish[...], pair_slope[...]),
    )
    for xs, cots, hid, swi, slo in shards:
        dgate, dupper = backward_terms(cots, rows[2], swi, slo, scale)
        totals[0] += over_tokens(dgate, xs[...])
        totals[1] += over_tokens(dupper, xs[...])
        totals[2] += over_tokens(hid, cots)
    for k in range(3):
        grads[k] = totals[k] * (scale if k == 2 else width ** (-0.5))


def ahead_forward(inner_x, far_x, rows, pair_top, *terms):
    far_hidden, far_swish, far_slope, hidden, swish, slope = terms
    size = inner_x.shape[0]
    for i, xs in enumerate((inner_x, far_x)):
        place = pl.ds(i * size, size)
        hidden[:, place], swish[:, place], slope[:, place] = forward_terms(
            xs[...], pair_top[0], pair_top[1]
        )
    far_hidden[...], far_swish[...], far_slope[...] = forward_terms(far_x[...], rows[0], rows[1])


def ahead_backward(inner_g, pair_low, swish, slope, dgate, dupper, *, scale):
    size = inner_g.shape[0]
    dgate[...], dupper[...] = backward_terms(
        inner_g[...], pair_low[...], swish[:, :size], slope[:, :size], scale
    )


def pair_first(inner_x, inner_g, far_g, hidden, sent, *, scale):
    size = inner_x.shape[0]
    cut = sent.shape[1]
    total = over_tokens(hidden[:, :size], inner_g[:, :cut])
    total += over_tokens(hidden[:, size:], far_g[...])
    sent[...] = (total * scale).astype(HALF)


def pair_rest(
    inner_x, far_x, inner_g, far_g, more_g, pair_low, hidden, swish, slope, dgate, dupper,
    second, third, last, *, cut, scale
):
    size, width = inner_x.shape
    width_scale = width ** (-0.5)
    total = over_tokens(hidden[:, :size], inner_g[:, cut:])
    total += over_tokens(hidden[:, size:], more_g[...])
    columns = [(total * scale).astype(HALF)]
    far_terms = backward_terms(
        joined(far_g, more_g), pair_low[...], swish[:, size:], slope[:, size:], scale
    )
    for near, far in zip((dupper, dgate), far_terms[::-1]):
        total = over_tokens(near[...], inner_x[...]) + over_tokens(far, far_x[...])
        columns.append((total * width_scale).astype(HALF))
    columns = jnp.concatenate(columns, axis=1)
    start = 0
    for part in (second, third, last):
        part[...] = columns[:, start : start + part.shape[1]]
        start += part.shape[1]


def far_backward(far_x, far_g, more_g, rows, hidden, swish, slope, near, grads, *, scale):
    width_scale = far_x.shape[1] ** (-0.5)
    cots = joined(far_g, more_g)
    dgate, dupper = backward_terms(cots, rows[2], swish[...], slope[...], scale)
    grads[0] = near[0] + over_tokens(dgate, far_x[...]) * width_scale
    grads[1] = near[1] + over_tokens(dupper, far_x[...]) * width_scale
    grads[2] = near[2] + over_tokens(hidden[...], cots) * scale


def cut_columns(whole, rows, part, low):
    part[...] = whole[:, : part.shape[1]]
    low[...] = rows[2]


def line_of_four(tokens, cots, sent_cots, cuts, rows, still, scale):
    pairs = [(0, 1), (1, 0), (2, 3), (3, 2)]
    middle = [(1, 2), (2, 1)]
    units, width = rows.shape[1:]
    size = tokens.shape[0]

    def send(block, route):
        return lax.ppermute(block, "tp", route)

    inner_x = send(tokens, middle)
    pair_x = send(tokens, pairs)
    inner_g = send(cots, middle)
    pair_g = send(sent_cots, pairs)
    far_x = send(pair_x, middle)
    *near_terms, top = call(
        inner_forward,
        [array((units, 2 * size), t) for t in (HALF, FULL, FULL)]
        + [array((2, units, width), HALF)],
        (tokens, inner_x, rows),
        after=(still,),
        flops=NEAR_WORK,
        name="near_forward",
    )
    pair_top = send(top, pairs)
    pair_terms = call(
        near_forward,
        [array((units, size), t) for t in (HALF, FULL, FULL)],
        (pair_x, rows),
        after=near_terms[:1],
        flops=PAIR_WORK,
        name="pair_forward",
    )
    pair_part, low = call(
        cut_columns,
        [array((size, cuts[0]), HALF), array((units, width), HALF)],
        (pair_g, rows),
        after=pair_terms[:1],
        name="cut",
    )
    pair_low = send(low, pairs)
    near, pair_more = call(
        functools.partial(near_backward, scale=scale),
        [array((3, units, width), FULL), array((size, cuts[1]), HALF)],
        (tokens, inner_x, pair_x, cots, inner_g, pair_g, rows, *near_terms, *pair_terms),
        after=(pair_part,),
        name="near_backward",
    )
    far_gs = [send(v, middle) for v in (pair_part, pair_more)]
    ahead = call(
        ahead_forward,
        [array((units, size), t) for t in (HALF, FULL, FULL)]
        + [array((units, 2 * size), t) for t in (HALF, FULL, FULL)],
        (inner_x, far_x, rows, pair_top),
        after=(near,),
        flops=AHEAD_WORK,
        name="ahead_forward",
    )
    far_terms, (hidden, swish, slope) = ahead[:3], ahead[3:]
    sizes = [width * v // (7 * 128) * 128 for v in PIECES]
    sizes.append(3 * width - sum(sizes))
    cut, more = sizes[0], sizes[0] + sizes[1] - width
    ends = width - sizes[3]
    first = call(
        functools.partial(pair_first, scale=scale),
        [array((units, sizes[0]), HALF)],
        (inner_x, inner_g, far_gs[0], hidden),
        name="pair_first",
    )[0]
    dgate, dupper = call(
        functools.partial(ahead_backward, scale=scale),
        [array((units, size), HALF)] * 2,
        (inner_g, pair_low, swish, slope),
        after=(first,),
        name="ahead_backward",
    )
    grads = call(
        functools.partial(far_backward, scale=scale),
        [array((3, units, width), FULL)],
        (far_x, *far_gs, rows, *far_terms, near),
        after=(dgate,),
        flops=FAR_WORK,
        name="far_backward",
    )[0]
    second, third, last = call(
        functools.partial(pair_rest, cut=cut, scale=scale),
        [array((units, v), HALF) for v in sizes[1:]],
        (inner_x, far_x, inner_g, *far_gs, pair_low, hidden, swish, slope, dgate, dupper),
        after=(grads,),
        name="pair_rest",
    )
    pieces = [
        ([(2, 0, cut)], first),
        ([(2, cut, width - cut), (1, 0, more)], second),
        ([(1, more, width - more), (0, 0, ends)], third),
        ([(0, ends, sizes[3])], last),
    ]
    pieces = [(tuple(v for v in piece if v[2]), parts) for piece, parts in pieces]
    return grads, pieces, lambda block: send(block, pairs)


def gathered(tokens, cots, rows, scale):
    return unit_grads(
        lax.all_gather(tokens, "tp", axis=0, tiled=True),
        lax.all_gather(cots, "tp", axis=0, tiled=True),
        rows,
        scale,
    )


def still_kernel(rows, first, second, cots, still, step, same_cots):
    master = rows[...].astype(FULL)
    total = adam_step(0.9 * first[...].astype(FULL), 0.95 * second[...].astype(FULL))
    step[...] = total
    still[...] = master - 0.1 * (total + 0.1 * master)

    @pl.when(pl.program_id(0) == 0)
    def _():
        same_cots[...] = cots[...]


def still_values(rows, first, second, cots):
    slab = pl.BlockSpec((1, *rows.shape[1:]), lambda k: (k, 0, 0))
    whole = pl.BlockSpec(cots.shape, lambda k: (0, 0))
    return pl.pallas_call(
        still_kernel,
        grid=(3,),
        out_shape=[array(rows.shape, FULL)] * 2 + [array(cots.shape, cots.dtype)],
        in_specs=[slab] * 3 + [whole],
        out_specs=[slab] * 2 + [whole],
        compiler_params=pltpu.CompilerParams(vmem_limit_bytes=32 * 2**20),
        name="still",
    )(rows, first, second, cots)


def spans(piece):
    start = 0
    for k, first, size in piece:
        yield k, pl.ds(first, size), pl.ds(start, size)
        start += size


def columns_of(piece):
    return sum(size for _, _, size in piece)


def change_kernel(grads, still, still_step, first, second, *rest, piece, parts, ready):
    came, rest = rest[:parts], rest[parts:]
    ready, (updated, sent, *passed) = rest[:ready], rest[ready:]
    for block, same in zip(ready, passed):
        same[...] = block[...]
    for k, place, here in spans(piece):
        grad = grads[k, :, place]
        for part in came:
            grad = grad + part[:, here].astype(FULL)
        moment_one = 0.9 * first[k, :, place].astype(FULL) + 0.1 * grad
        moment_two = 0.95 * second[k, :, place].astype(FULL) + 0.05 * grad * grad
        total = 0.1 * (still_step[k, :, place] - adam_step(moment_one, moment_two))
        updated[:, here] = still[k, :, place] + total
        sent[:, here] = total.astype(HALF)


def change_of(piece, grads, still, still_step, first, second, came, ready, after):
    shape = (grads.shape[1], columns_of(piece))
    return call(
        functools.partial(change_kernel, piece=piece, parts=len(came), ready=len(ready)),
        [array(shape, FULL), array(shape, HALF)] + [array(v.shape, v.dtype) for v in ready],
        (grads, still, still_step, first, second, *came, *ready),
        after=after,
        name="change",
    )


def join_kernel(*refs):
    *blocks, joint = refs
    start = 0
    for block in blocks:
        joint[:, pl.ds(start, block.shape[1])] = block[...]
        start += block.shape[1]


def across_kernel(updated, still, far, total, *, piece):
    for k, place, here in spans(piece):
        total[:, here] = updated[:, here] + still[k, :, place] + far[:, here].astype(FULL)


def finish_kernel(*refs, pieces, bands):
    *parts, near, out, total, done = refs
    units = near.shape[0]
    copies, start = [], 0
    for part, piece in zip(parts, pieces):
        for k, place, here in spans(piece):
            there = pl.ds(start, place.size)
            for i, band in enumerate(bands):
                rows = pl.ds(band, (*bands, units)[i + 1] - band)
                total[rows, there] = (part[rows, here] + near[rows, there]) / 3.0
                copies.append(
                    pltpu.make_async_copy(
                        total.at[rows, there], out.at[k, rows, place], done.at[len(copies)]
                    )
                )
                copies[-1].start()
            start += place.size
    for copy in copies:
        copy.wait()


def finish(pieces, parts, near, shape):
    units = shape[1]
    bands = (0, units // 32 * 16)
    vmem = pl.BlockSpec(memory_space=pltpu.VMEM)
    return pl.pallas_call(
        functools.partial(finish_kernel, pieces=pieces, bands=bands),
        out_shape=array(shape, FULL),
        in_specs=[vmem] * (len(parts) + 1),
        out_specs=pl.BlockSpec(memory_space=pl.ANY),
        scratch_shapes=[
            pltpu.VMEM(near.shape, FULL),
            pltpu.SemaphoreType.DMA((2 * sum(len(v) for v in pieces),)),
        ],
        cost_estimate=pl.CostEstimate(flops=0, bytes_accessed=0, transcendentals=0),
        compiler_params=pltpu.CompilerParams(vmem_limit_bytes=32 * 2**20),
        name="finish",
    )(*parts, near)


def on_device(tokens, cotangent, weights, first_moment, second_moment):
    rows, first, second = (
        jnp.swapaxes(v[0], 0, 1) for v in (weights, first_moment, second_moment)
    )
    scale = (rows.shape[1] * lax.axis_size("tp")) ** (-0.5)
    width = rows.shape[2]
    cuts = (width * PIECES[0] // (7 * 128) * 128,)
    cuts += (width - cuts[0],)
    still, still_step, sent_cots = still_values(rows, first, second, cotangent)
    still_far = neighbour(still, 1)
    if lax.axis_size("tp") == 4:
        grads, pieces, send = line_of_four(
            tokens, cotangent, sent_cots, cuts, rows, still, scale
        )
    else:
        grads = gathered(tokens, cotangent, rows, scale)
        pieces = [([(k, 0, rows.shape[2])], None) for k in ORDER]
    came = [[] if v is None else [send(v)] for _, v in pieces[:AHEAD]]
    changes, last = [], ()
    for i, (piece, _) in enumerate(pieces):
        ready = [v for _, v in pieces[i + AHEAD : i + AHEAD + 1] if v is not None]
        updated, sent, *ready = change_of(
            piece, grads, still, still_step, first, second, came[i], ready, last
        )
        came.append([send(v) for v in ready])
        changes.append((piece, updated, neighbour(sent, 1)))
        last = (sent, still_far) if i == STILL_BY else (sent,)
    updates = [v for _, v, _ in changes]
    joint = call(
        join_kernel, [array((rows.shape[1], 3 * width), FULL)], updates, name="join"
    )[0]
    near = neighbour(joint, 0)
    totals, last = [], (joint,)
    for i, (piece, updated, far) in enumerate(changes):
        totals += call(
            functools.partial(across_kernel, piece=piece),
            [array(updated.shape, FULL)],
            (updated, still_far, far),
            after=last,
            flops=ACROSS_WORK[i],
            name="across",
        )
        last = totals[-1:]
    out = finish([v for v, _, _ in changes], totals, near, rows.shape)
    return jnp.swapaxes(out, 0, 1)[None]


def solution(mesh):
    in_specs = (
        P(("blk", "tp"), None),
        P(("blk", "tp"), None),
        P("blk", "tp", None, None),
        P("blk", "tp", None, None),
        P("blk", "tp", None, None),
    )
    out_specs = P("blk", "tp", None, None)
    return jax.shard_map(
        on_device, mesh=mesh, in_specs=in_specs, out_specs=out_specs, check_vma=False
    )
```

time: 85.3 us -> 76.8 us (0.900)
  waiting for transfers between devices: 38.4 us -> 27.9 us
  starting transfers between devices: 24.4 us -> 32.4 us
  Pallas kernels: 16.9 us -> 11.4 us
    ppermute x10 -> x13, waiting for transfers between devices: 28.9 us -> 17.8 us  [send(): return lax.ppermute(block, 'tp', route)]
    ppermute x10 -> x13, starting transfers between devices: 20.4 us -> 29.5 us  [send(): return lax.ppermute(block, 'tp', route)]
    pallas_call x6 -> x2, Pallas kernels: 7.96 us -> 2.68 us  [the longest x1 1.39 us: still_values(): pl.pallas_call(still_kernel, grid=(3,), out_shape=[array(rows.shape, FULL...]
    ppermute x8 -> x6, starting transfers between devices: 4.08 us -> 2.86 us  [neighbour(): return lax.ppermute(block, 'blk', route)]
    ppermute x8 -> x6, waiting for transfers between devices: 9.46 us -> 10.2 us  [neighbour(): return lax.ppermute(block, 'blk', route)]
    unnamed x18 -> x16, local copies, waits for them, and re-layouts: 4.89 us -> 4.47 us
    pallas_call x8 -> x18, Pallas kernels: 8.94 us -> 8.77 us  [call(): pl.pallas_call(body, out_shape=outs, in_specs=[pl.BlockSpec(memory_space=...]
  transfers between devices with their start and end apart: 18 -> 19, of which waited for: 10 -> 9; matrix products, arithmetic and copies ran while one was open for 0% -> 0% of each run, Pallas kernels for 18% -> 13%
where the time goes in v4:
time: 76.8 us; the launch traced here: 76.5 us
  starting transfers between devices  32.4 us (42%)
  waiting for transfers between devices  27.9 us (36%)
  Pallas kernels  11.4 us (15%)
  local copies, waits for them, and re-layouts  4.47 us (6%)
    ppermute x13, starting transfers between devices, send(): return lax.ppermute(block, 'tp', route)  29.5 us
    ppermute x13, waiting for transfers between devices, send(): return lax.ppermute(block, 'tp', route)  17.8 us
    ppermute x6, waiting for transfers between devices, neighbour(): return lax.ppermute(block, 'blk', route)  10.2 us
    pallas_call x18, Pallas kernels, call(): pl.pallas_call(body, out_shape=outs, in_specs=[pl.BlockSpec(memory_space=...  8.77 us
    unnamed x16, local copies, waits for them, and re-layouts  4.47 us
    ppermute x6, starting transfers between devices, neighbour(): return lax.ppermute(block, 'blk', route)  2.86 us
  transfers between devices with their start and end apart: 19, of which 9 were waited for; matrix products, arithmetic and copies ran while one was open for 0% of the time, Pallas kernels for 13%

profile of v4, /device:TPU:0, one launch (start us, length us, event | category | flops | bytes accessed | tf_op | source)
XLA Modules:
  0.0 76.5 jit_solution(16695954940564267)
XLA Ops:
  0.0 0.7 collective-permute-start.3
  0.7 5.9 %collective-permute-start = (bf16[256,896]{1,0:T(8,128)(2,1)}, bf16[256,896]{1,0:T(8,128)(2,1)S(1)}, u32[]{:S(2)}, u32[]{:S(2)}) collective-permute-start(bf16[256,896]{1,0:T(8,128)(2,1)} %refs_0_.3), channel_id=1, source_target_pairs={{0,1},{1,0},{2,3},{3,2},{4,5},{5,4},{6,7},{7,6},{8,9},{9,8},{10,11... | collective-permute-start | bytes 1376264 | tf_op jit(solution)/shard_map/ppermute | solution.py:208
  6.6 0.7 collective-permute-start.5
  7.3 1.1 %copy-done = bf16[1,152,3,896]{3,1,2,0:T(8,128)(2,1)S(1)} copy-done((bf16[1,152,3,896]{3,1,2,0:T(8,128)(2,1)S(1)}, bf16[1,152,3,896]{3,1,2,0:T(8,128)(2,1)}, u32[]{:S(2)}) %copy-start) | copy-done | bytes 817176
  8.4 1.1 %copy-done.2 = bf16[1,152,3,896]{3,1,2,0:T(8,128)(2,1)S(1)} copy-done((bf16[1,152,3,896]{3,1,2,0:T(8,128)(2,1)S(1)}, bf16[1,152,3,896]{3,1,2,0:T(8,128)(2,1)}, u32[]{:S(2)}) %copy-start.2) | copy-done | bytes 817176
  9.5 1.1 %copy-done.4 = bf16[1,152,3,896]{3,1,2,0:T(8,128)(2,1)S(1)} copy-done((bf16[1,152,3,896]{3,1,2,0:T(8,128)(2,1)S(1)}, bf16[1,152,3,896]{3,1,2,0:T(8,128)(2,1)}, u32[]{:S(2)}) %copy-start.4) | copy-done | bytes 817176
  10.7 1.0 %copy-done.6 = bf16[256,896]{1,0:T(8,128)(2,1)S(1)} copy-done((bf16[256,896]{1,0:T(8,128)(2,1)S(1)}, bf16[256,896]{1,0:T(8,128)(2,1)}, u32[]{:S(2)}) %copy-start.6) | copy-done | bytes 458776
  11.7 1.4 %still.1 = (f32[3,152,896]{2,1,0:T(8,128)S(1)}, f32[3,152,896]{2,1,0:T(8,128)S(1)}, bf16[256,896]{1,0:T(8,128)(2,1)S(1)}) custom-call(bf16[3,152,896]{2,1,0:T(8,128)(2,1)S(1)} %bitcast.22, bf16[3,152,896]{2,1,0:T(8,128)(2,1)S(1)} %bitcast.12, bf16[3,152,896]{2,1,0:T(8,128)(2,1)S(1)} %bitcast.17, bf16[256,896]{1,0:T(8,128)(2,1)S(1)} %copy-done.6), custom_call_target="tpu_custom_call" | custom-call | tf_op jit(solution)/shard_map/still/pallas_call | solution.py:324
  13.1 1.8 %collective-permute-start.2 = (bf16[256,896]{1,0:T(8,128)(2,1)S(1)}, bf16[256,896]{1,0:T(8,128)(2,1)S(1)}, u32[]{:S(2)}, u32[]{:S(2)}) collective-permute-start(bf16[256,896]{1,0:T(8,128)(2,1)S(1)} %get-tuple-element.40), channel_id=1, source_target_pairs={{0,1},{1,0},{2,3},{3,2},{4,5},{5,4},{6,7},{7,6},{8,9},{9,8},{10,11... | collective-permute-start | bytes 1376264 | tf_op jit(solution)/shard_map/ppermute | solution.py:208
  14.9 1.0 %collective-permute-start.10 = (f32[3,152,896]{2,1,0:T(8,128)S(1)}, f32[3,152,896]{2,1,0:T(8,128)S(1)}, u32[]{:S(2)}, u32[]{:S(2)}) collective-permute-start(f32[3,152,896]{2,1,0:T(8,128)S(1)} %get-tuple-element.41.refs_3_.refs_1_), channel_id=1, source_target_pairs={{4,8},{12,16},{20,24},{28,0},{8,4},{16,12},{24,20},{0,28},{5,9},{1... | collective-permute-start | bytes 4902920 | tf_op jit(solution)/shard_map/ppermute | solution.py:33
  15.9 0.8 %near_forward.1 = (bf16[152,512]{1,0:T(8,128)(2,1)S(1)}, f32[152,512]{1,0:T(8,128)S(1)}, f32[152,512]{1,0:T(8,128)S(1)}, bf16[2,152,896]{2,1,0:T(8,128)(2,1)S(1)}) custom-call(bf16[256,896]{1,0:T(8,128)(2,1)S(1)} %copy-done.7, bf16[256,896]{1,0:T(8,128)(2,1)S(1)} %collective-permute-done.3.refs_1_.refs_0_, bf16[3,152,896]{2,1,0:T(8,128)(2,1)S(1)} %bitcast.23, ...), custom_call_target="tpu_custom_call" | custom-call | flops 5000000000 | tf_op jit(solution)/shard_map/near_forward/pallas_call | solution.py:81
  16.8 2.7 %collective-permute-start.7 = (bf16[2,152,896]{2,1,0:T(8,128)(2,1)S(1)}, bf16[2,152,896]{2,1,0:T(8,128)(2,1)S(1)}, u32[]{:S(2)}, u32[]{:S(2)}) collective-permute-start(bf16[2,152,896]{2,1,0:T(8,128)(2,1)S(1)} %get-tuple-element.50), channel_id=1, source_target_pairs={{0,1},{1,0},{2,3},{3,2},{4,5},{5,4},{6,7},{7,6},{8,9},{9,8},{10,11... | collective-permute-start | bytes 1634312 | tf_op jit(solution)/shard_map/ppermute | solution.py:208
  19.4 0.7 collective-permute-start.1
  20.1 0.5 pair_forward.1
  20.6 7.4 %collective-permute-done.2.refs_0_.refs_5_ = bf16[256,896]{1,0:T(8,128)(2,1)S(1)} collective-permute-done((bf16[256,896]{1,0:T(8,128)(2,1)S(1)}, bf16[256,896]{1,0:T(8,128)(2,1)S(1)}, u32[]{:S(2)}, u32[]{:S(2)}) %collective-permute-start.2) | collective-permute-done | bytes 458784 | tf_op jit(solution)/shard_map/ppermute | solution.py:208
  28.0 0.7 collective-permute-start.4
  28.7 1.8 %near_backward.1 = (f32[3,152,896]{2,1,0:T(8,128)S(1)}, bf16[256,256]{1,0:T(8,128)(2,1)S(1)}) custom-call(bf16[256,896]{1,0:T(8,128)(2,1)S(1)} %copy-done.7, bf16[256,896]{1,0:T(8,128)(2,1)S(1)} %collective-permute-done.3.refs_1_.refs_0_, bf16[256,896]{1,0:T(8,128)(2,1)S(1)} %collective-permute-done.refs_0_.refs_2_, bf16[256,896]{1,0:T(8,128)(2,1)S(1)} %copy-done.6, ...), custom_call_target="tpu_custom_call" | custom-call | tf_op jit(solution)/shard_map/near_backward/pallas_call | solution.py:81
  30.6 0.7 collective-permute-start.6
  31.3 6.9 %collective-permute-start.8 = (bf16[152,896]{1,0:T(8,128)(2,1)S(1)}, bf16[152,896]{1,0:T(8,128)(2,1)S(1)}, u32[]{:S(2)}, u32[]{:S(2)}) collective-permute-start(bf16[152,896]{1,0:T(8,128)(2,1)S(1)} %get-tuple-element.55), channel_id=1, source_target_pairs={{0,1},{1,0},{2,3},{3,2},{4,5},{5,4},{6,7},{7,6},{8,9},{9,8},{10,11... | collective-permute-start | bytes 817160 | tf_op jit(solution)/shard_map/ppermute | solution.py:208
  38.2 1.5 %collective-permute-done.7.refs_3_ = bf16[2,152,896]{2,1,0:T(8,128)(2,1)S(1)} collective-permute-done((bf16[2,152,896]{2,1,0:T(8,128)(2,1)S(1)}, bf16[2,152,896]{2,1,0:T(8,128)(2,1)S(1)}, u32[]{:S(2)}, u32[]{:S(2)}) %collective-permute-start.7) | collective-permute-done | bytes 544800 | tf_op jit(solution)/shard_map/ppermute | solution.py:208
  39.7 1.1 %ahead_forward.1 = (bf16[152,256]{1,0:T(8,128)(2,1)S(1)}, f32[152,256]{1,0:T(8,128)S(1)}, f32[152,256]{1,0:T(8,128)S(1)}, bf16[152,512]{1,0:T(8,128)(2,1)S(1)}, ...) custom-call(bf16[256,896]{1,0:T(8,128)(2,1)S(1)} %collective-permute-done.3.refs_1_.refs_0_, ...), custom_call_target="tpu_custom_call" | custom-call | flops 20000000000 | tf_op jit(solution)/shard_map/ahead_forward/pallas_call | solution.py:81
  40.8 0.3 pair_first.1.refs_4_
  41.1 4.5 %collective-permute-start.9 = (bf16[152,640]{1,0:T(8,128)(2,1)S(1)}, bf16[152,640]{1,0:T(8,128)(2,1)S(1)}, u32[]{:S(2)}, u32[]{:S(2)}) collective-permute-start(bf16[152,640]{1,0:T(8,128)(2,1)S(1)} %pair_first.1.refs_4_), channel_id=1, source_target_pairs={{0,1},{1,0},{2,3},{3,2},{4,5},{5,4},{6,7},{7,6},{8,9},{9,8},{10,11... | collective-permute-start | bytes 583688 | tf_op jit(solution)/shard_map/ppermute | solution.py:208
  45.6 0.3 ahead_backward.1
  45.9 0.9 %far_backward.1.refs_11_.refs_0_ = f32[3,152,896]{2,1,0:T(8,128)S(1)} custom-call(bf16[256,896]{1,0:T(8,128)(2,1)S(1)} %collective-permute-done.1.refs_1_.refs_0_, bf16[256,640]{1,0:T(8,128)(2,1)S(1)} %collective-permute-done.4.refs_2_.refs_1_.refs_3_, bf16[256,256]{1,0:T(8,128)(2,1)S(1)} %collective-permute-done.6.refs_2_.refs_4_, ...), custom_call_target="tpu_custom_call" | custom-call | flops 20000000000 | tf_op jit(solution)/shard_map/far_backward/pallas_call | solution.py:81
  46.8 1.0 %pair_rest.1 = (bf16[152,768]{1,0:T(8,128)(2,1)S(1)}, bf16[152,768]{1,0:T(8,128)(2,1)S(1)}, bf16[152,512]{1,0:T(8,128)(2,1)S(1)}) custom-call(bf16[256,896]{1,0:T(8,128)(2,1)S(1)} %collective-permute-done.3.refs_1_.refs_0_, bf16[256,896]{1,0:T(8,128)(2,1)S(1)} %collective-permute-done.1.refs_1_.refs_0_, ...), custom_call_target="tpu_custom_call" | custom-call | tf_op jit(solution)/shard_map/pair_rest/pallas_call | solution.py:81
  47.8 1.0 %collective-permute-start.12 = (bf16[152,768]{1,0:T(8,128)(2,1)S(1)}, bf16[152,768]{1,0:T(8,128)(2,1)S(1)}, u32[]{:S(2)}, u32[]{:S(2)}) collective-permute-start(bf16[152,768]{1,0:T(8,128)(2,1)S(1)} %get-tuple-element.65), channel_id=1, source_target_pairs={{0,1},{1,0},{2,3},{3,2},{4,5},{5,4},{6,7},{7,6},{8,9},{9,8},{10,11... | collective-permute-start | bytes 700424 | tf_op jit(solution)/shard_map/ppermute | solution.py:208
  48.8 0.9 %collective-permute-done.9.refs_5_ = bf16[152,640]{1,0:T(8,128)(2,1)S(1)} collective-permute-done((bf16[152,640]{1,0:T(8,128)(2,1)S(1)}, bf16[152,640]{1,0:T(8,128)(2,1)S(1)}, u32[]{:S(2)}, u32[]{:S(2)}) %collective-permute-start.9) | collective-permute-done | bytes 194592 | tf_op jit(solution)/shard_map/ppermute | solution.py:208
  49.7 0.4 change.4
  50.1 2.4 %collective-permute-start.13 = (bf16[152,768]{1,0:T(8,128)(2,1)S(1)}, bf16[152,768]{1,0:T(8,128)(2,1)S(1)}, u32[]{:S(2)}, u32[]{:S(2)}) collective-permute-start(bf16[152,768]{1,0:T(8,128)(2,1)S(1)} %get-tuple-element.68), channel_id=1, source_target_pairs={{0,1},{1,0},{2,3},{3,2},{4,5},{5,4},{6,7},{7,6},{8,9},{9,8},{10,11... | collective-permute-start | bytes 700424 | tf_op jit(solution)/shard_map/ppermute | solution.py:208
  52.5 4.0 %collective-permute-done.12.refs_5_ = bf16[152,768]{1,0:T(8,128)(2,1)S(1)} collective-permute-done((bf16[152,768]{1,0:T(8,128)(2,1)S(1)}, bf16[152,768]{1,0:T(8,128)(2,1)S(1)}, u32[]{:S(2)}, u32[]{:S(2)}) %collective-permute-start.12) | collective-permute-done | bytes 233504 | tf_op jit(solution)/shard_map/ppermute | solution.py:208
  56.5 0.4 change.5
  57.0 1.0 %collective-permute-start.14 = (bf16[152,512]{1,0:T(8,128)(2,1)S(1)}, bf16[152,512]{1,0:T(8,128)(2,1)S(1)}, u32[]{:S(2)}, u32[]{:S(2)}) collective-permute-start(bf16[152,512]{1,0:T(8,128)(2,1)S(1)} %get-tuple-element.71), channel_id=1, source_target_pairs={{0,1},{1,0},{2,3},{3,2},{4,5},{5,4},{6,7},{7,6},{8,9},{9,8},{10,11... | collective-permute-start | bytes 466952 | tf_op jit(solution)/shard_map/ppermute | solution.py:208
  58.0 2.9 %collective-permute-done.13.refs_5_ = bf16[152,768]{1,0:T(8,128)(2,1)S(1)} collective-permute-done((bf16[152,768]{1,0:T(8,128)(2,1)S(1)}, bf16[152,768]{1,0:T(8,128)(2,1)S(1)}, u32[]{:S(2)}, u32[]{:S(2)}) %collective-permute-start.13) | collective-permute-done | bytes 233504 | tf_op jit(solution)/shard_map/ppermute | solution.py:208
  60.9 0.5 change.6
  61.3 0.1 collective-permute-start.16
  61.4 1.1 %collective-permute-done.14.refs_5_ = bf16[152,512]{1,0:T(8,128)(2,1)S(1)} collective-permute-done((bf16[152,512]{1,0:T(8,128)(2,1)S(1)}, bf16[152,512]{1,0:T(8,128)(2,1)S(1)}, u32[]{:S(2)}, u32[]{:S(2)}) %collective-permute-start.14) | collective-permute-done | bytes 155680 | tf_op jit(solution)/shard_map/ppermute | solution.py:208
  62.5 0.3 change.7
  62.8 1.6 %collective-permute-start.17 = (bf16[152,512]{1,0:T(8,128)(2,1)S(1)}, bf16[152,512]{1,0:T(8,128)(2,1)S(1)}, u32[]{:S(2)}, u32[]{:S(2)}) collective-permute-start(bf16[152,512]{1,0:T(8,128)(2,1)S(1)} %get-tuple-element.74), channel_id=1, source_target_pairs={{4,8},{12,16},{20,24},{28,0},{8,4},{16,12},{24,20},{0,28},{5,9},{1... | collective-permute-start | bytes 466952 | tf_op jit(solution)/shard_map/ppermute | solution.py:33
  64.4 0.1 join.1.refs_3_
  64.5 0.2 collective-permute-start.18
  64.7 0.1 across.4.refs_3_.refs_0_
  64.8 2.0 %collective-permute-done.15.refs_2_ = bf16[152,768]{1,0:T(8,128)(2,1)S(1)} collective-permute-done((bf16[152,768]{1,0:T(8,128)(2,1)S(1)}, bf16[152,768]{1,0:T(8,128)(2,1)S(1)}, u32[]{:S(2)}, u32[]{:S(2)}) %collective-permute-start.15) | collective-permute-done | bytes 233504 | tf_op jit(solution)/shard_map/ppermute | solution.py:33
  66.8 0.1 across.5.refs_3_.refs_1_
  66.9 4.9 %collective-permute-done.16.refs_2_ = bf16[152,768]{1,0:T(8,128)(2,1)S(1)} collective-permute-done((bf16[152,768]{1,0:T(8,128)(2,1)S(1)}, bf16[152,768]{1,0:T(8,128)(2,1)S(1)}, u32[]{:S(2)}, u32[]{:S(2)}) %collective-permute-start.16) | collective-permute-done | bytes 233504 | tf_op jit(solution)/shard_map/ppermute | solution.py:33
  71.8 0.1 across.6.refs_3_.refs_2_
  71.9 3.3 %collective-permute-done.17.refs_2_ = bf16[152,512]{1,0:T(8,128)(2,1)S(1)} collective-permute-done((bf16[152,512]{1,0:T(8,128)(2,1)S(1)}, bf16[152,512]{1,0:T(8,128)(2,1)S(1)}, u32[]{:S(2)}, u32[]{:S(2)}) %collective-permute-start.17) | collective-permute-done | bytes 155680 | tf_op jit(solution)/shard_map/ppermute | solution.py:33
  75.2 1.3 %finish.1 = f32[3,152,896]{2,1,0:T(8,128)} custom-call(f32[152,640]{1,0:T(8,128)S(1)} %across.4.refs_3_.refs_0_, f32[152,768]{1,0:T(8,128)S(1)} %across.5.refs_3_.refs_1_, f32[152,768]{1,0:T(8,128)S(1)} %across.6.refs_3_.refs_2_, f32[152,512]{1,0:T(8,128)S(1)} %across.7.refs_3_, f32[152,2688]{1,0:T(8,128)S(1)} %collective-permute-done.18.refs_4_), custom_call_target="tpu_custom_call" | custom-call | tf_op jit(solution)/shard_map/finish/pallas_call | solution.py:411
  (26 shorter events, 0.2 us)
Async XLA Ops:
  0.0 15.9 %collective-permute-start.3 = (bf16[256,896]{1,0:T(8,128)(2,1)}, bf16[256,896]{1,0:T(8,128)(2,1)S(1)}, u32[]{:S(2)}, u32[]{:S(2)}) collective-permute-start(bf16[256,896]{1,0:T(8,128)(2,1)} %refs_0_.3), channel_id=1, source_target_pairs={{1,2},{2,1},{5,6},{6,5},{9,10},{10,9},{13,14},{14,13},{17,18},{18,... | collective-permute-start | bytes 1376264 | tf_op jit(solution)/shard_map/ppermute | solution.py:208
  0.7 18.7 %collective-permute-start = (bf16[256,896]{1,0:T(8,128)(2,1)}, bf16[256,896]{1,0:T(8,128)(2,1)S(1)}, u32[]{:S(2)}, u32[]{:S(2)}) collective-permute-start(bf16[256,896]{1,0:T(8,128)(2,1)} %refs_0_.3), channel_id=1, source_target_pairs={{0,1},{1,0},{2,3},{3,2},{4,5},{5,4},{6,7},{7,6},{8,9},{9,8},{10,11... | collective-permute-start | bytes 1376264 | tf_op jit(solution)/shard_map/ppermute | solution.py:208
  6.6 22.2 %collective-permute-start.5 = (bf16[256,896]{1,0:T(8,128)(2,1)}, bf16[256,896]{1,0:T(8,128)(2,1)S(1)}, u32[]{:S(2)}, u32[]{:S(2)}) collective-permute-start(bf16[256,896]{1,0:T(8,128)(2,1)} %refs_3_.1), channel_id=1, source_target_pairs={{1,2},{2,1},{5,6},{6,5},{9,10},{10,9},{13,14},{14,13},{17,18},{18,... | collective-permute-start | bytes 1376264 | tf_op jit(solution)/shard_map/ppermute | solution.py:208
  7.3 1.1 %copy-start = (bf16[1,152,3,896]{3,1,2,0:T(8,128)(2,1)S(1)}, bf16[1,152,3,896]{3,1,2,0:T(8,128)(2,1)}, u32[]{:S(2)}) copy-start(bf16[1,152,3,896]{3,1,2,0:T(8,128)(2,1)} %param.8) | copy-start | bytes 2451460
  8.4 1.1 %copy-start.2 = (bf16[1,152,3,896]{3,1,2,0:T(8,128)(2,1)S(1)}, bf16[1,152,3,896]{3,1,2,0:T(8,128)(2,1)}, u32[]{:S(2)}) copy-start(bf16[1,152,3,896]{3,1,2,0:T(8,128)(2,1)} %param.9) | copy-start | bytes 2451460
  9.5 1.1 %copy-start.4 = (bf16[1,152,3,896]{3,1,2,0:T(8,128)(2,1)S(1)}, bf16[1,152,3,896]{3,1,2,0:T(8,128)(2,1)}, u32[]{:S(2)}) copy-start(bf16[1,152,3,896]{3,1,2,0:T(8,128)(2,1)} %param.7) | copy-start | bytes 2451460
  10.7 1.0 %copy-start.6 = (bf16[256,896]{1,0:T(8,128)(2,1)S(1)}, bf16[256,896]{1,0:T(8,128)(2,1)}, u32[]{:S(2)}) copy-start(bf16[256,896]{1,0:T(8,128)(2,1)} %refs_3_.1) | copy-start | bytes 1376260
  11.7 4.2 %copy-start.7 = (bf16[256,896]{1,0:T(8,128)(2,1)S(1)}, bf16[256,896]{1,0:T(8,128)(2,1)}, u32[]{:S(2)}) copy-start(bf16[256,896]{1,0:T(8,128)(2,1)} %refs_0_.3) | copy-start | bytes 1376260
  13.1 14.9 %collective-permute-start.2 = (bf16[256,896]{1,0:T(8,128)(2,1)S(1)}, bf16[256,896]{1,0:T(8,128)(2,1)S(1)}, u32[]{:S(2)}, u32[]{:S(2)}) collective-permute-start(bf16[256,896]{1,0:T(8,128)(2,1)S(1)} %get-tuple-element.40), channel_id=1, source_target_pairs={{0,1},{1,0},{2,3},{3,2},{4,5},{5,4},{6,7},{7,6},{8,9},{9,8},{10,11... | collective-permute-start | bytes 1376264 | tf_op jit(solution)/shard_map/ppermute | solution.py:208
  14.9 41.6 %collective-permute-start.10 = (f32[3,152,896]{2,1,0:T(8,128)S(1)}, f32[3,152,896]{2,1,0:T(8,128)S(1)}, u32[]{:S(2)}, u32[]{:S(2)}) collective-permute-start(f32[3,152,896]{2,1,0:T(8,128)S(1)} %get-tuple-element.41.refs_3_.refs_1_), channel_id=1, source_target_pairs={{4,8},{12,16},{20,24},{28,0},{8,4},{16,12},{24,20},{0,28},{5,9},{1... | collective-permute-start | bytes 4902920 | tf_op jit(solution)/shard_map/ppermute | solution.py:33
  16.8 22.9 %collective-permute-start.7 = (bf16[2,152,896]{2,1,0:T(8,128)(2,1)S(1)}, bf16[2,152,896]{2,1,0:T(8,128)(2,1)S(1)}, u32[]{:S(2)}, u32[]{:S(2)}) collective-permute-start(bf16[2,152,896]{2,1,0:T(8,128)(2,1)S(1)} %get-tuple-element.50), channel_id=1, source_target_pairs={{0,1},{1,0},{2,3},{3,2},{4,5},{5,4},{6,7},{7,6},{8,9},{9,8},{10,11... | collective-permute-start | bytes 1634312 | tf_op jit(solution)/shard_map/ppermute | solution.py:208
  19.4 11.8 %collective-permute-start.1 = (bf16[256,896]{1,0:T(8,128)(2,1)S(1)}, bf16[256,896]{1,0:T(8,128)(2,1)S(1)}, u32[]{:S(2)}, u32[]{:S(2)}) collective-permute-start(bf16[256,896]{1,0:T(8,128)(2,1)S(1)} %collective-permute-done.refs_0_.refs_2_), channel_id=1, source_target_pairs={{1,2},{2,1},{5,6},{6,5},{9,10},{10,9},{13,14},{14,13},{17,18},{18,... | collective-permute-start | bytes 1376264 | tf_op jit(solution)/shard_map/ppermute | solution.py:208
  28.0 12.8 %collective-permute-start.4 = (bf16[256,640]{1,0:T(8,128)(2,1)S(1)}, bf16[256,640]{1,0:T(8,128)(2,1)S(1)}, u32[]{:S(2)}, u32[]{:S(2)}) collective-permute-start(bf16[256,640]{1,0:T(8,128)(2,1)S(1)} %get-tuple-element.44.refs_13_), channel_id=1, source_target_pairs={{1,2},{2,1},{5,6},{6,5},{9,10},{10,9},{13,14},{14,13},{17,18},{18,... | collective-permute-start | bytes 983048 | tf_op jit(solution)/shard_map/ppermute | solution.py:208
  30.6 15.3 %collective-permute-start.6 = (bf16[256,256]{1,0:T(8,128)(2,1)S(1)}, bf16[256,256]{1,0:T(8,128)(2,1)S(1)}, u32[]{:S(2)}, u32[]{:S(2)}) collective-permute-start(bf16[256,256]{1,0:T(8,128)(2,1)S(1)} %get-tuple-element.49), channel_id=1, source_target_pairs={{1,2},{2,1},{5,6},{6,5},{9,10},{10,9},{13,14},{14,13},{17,18},{18,... | collective-permute-start | bytes 393224 | tf_op jit(solution)/shard_map/ppermute | solution.py:208
  31.3 14.3 %collective-permute-start.8 = (bf16[152,896]{1,0:T(8,128)(2,1)S(1)}, bf16[152,896]{1,0:T(8,128)(2,1)S(1)}, u32[]{:S(2)}, u32[]{:S(2)}) collective-permute-start(bf16[152,896]{1,0:T(8,128)(2,1)S(1)} %get-tuple-element.55), channel_id=1, source_target_pairs={{0,1},{1,0},{2,3},{3,2},{4,5},{5,4},{6,7},{7,6},{8,9},{9,8},{10,11... | collective-permute-start | bytes 817160 | tf_op jit(solution)/shard_map/ppermute | solution.py:208
  40.8 5.1 %copy-start.5 = (bf16[1,152,3,896]{3,1,2,0:T(8,128)(2,1)S(1)}, bf16[1,152,3,896]{3,1,2,0:T(8,128)(2,1)}, u32[]{:S(2)}) copy-start(bf16[1,152,3,896]{3,1,2,0:T(8,128)(2,1)} %param.7) | copy-start | bytes 2451460
  41.1 8.6 %collective-permute-start.9 = (bf16[152,640]{1,0:T(8,128)(2,1)S(1)}, bf16[152,640]{1,0:T(8,128)(2,1)S(1)}, u32[]{:S(2)}, u32[]{:S(2)}) collective-permute-start(bf16[152,640]{1,0:T(8,128)(2,1)S(1)} %pair_first.1.refs_4_), channel_id=1, source_target_pairs={{0,1},{1,0},{2,3},{3,2},{4,5},{5,4},{6,7},{7,6},{8,9},{9,8},{10,11... | collective-permute-start | bytes 583688 | tf_op jit(solution)/shard_map/ppermute | solution.py:208
  46.8 2.9 %copy-start.1 = (bf16[1,152,3,896]{3,1,2,0:T(8,128)(2,1)S(1)}, bf16[1,152,3,896]{3,1,2,0:T(8,128)(2,1)}, u32[]{:S(2)}) copy-start(bf16[1,152,3,896]{3,1,2,0:T(8,128)(2,1)} %param.8) | copy-start | bytes 2451460
  46.8 2.9 %copy-start.3 = (bf16[1,152,3,896]{3,1,2,0:T(8,128)(2,1)S(1)}, bf16[1,152,3,896]{3,1,2,0:T(8,128)(2,1)}, u32[]{:S(2)}) copy-start(bf16[1,152,3,896]{3,1,2,0:T(8,128)(2,1)} %param.9) | copy-start | bytes 2451460
  47.8 8.7 %collective-permute-start.12 = (bf16[152,768]{1,0:T(8,128)(2,1)S(1)}, bf16[152,768]{1,0:T(8,128)(2,1)S(1)}, u32[]{:S(2)}, u32[]{:S(2)}) collective-permute-start(bf16[152,768]{1,0:T(8,128)(2,1)S(1)} %get-tuple-element.65), channel_id=1, source_target_pairs={{0,1},{1,0},{2,3},{3,2},{4,5},{5,4},{6,7},{7,6},{8,9},{9,8},{10,11... | collective-permute-start | bytes 700424 | tf_op jit(solution)/shard_map/ppermute | solution.py:208
  50.1 10.8 %collective-permute-start.13 = (bf16[152,768]{1,0:T(8,128)(2,1)S(1)}, bf16[152,768]{1,0:T(8,128)(2,1)S(1)}, u32[]{:S(2)}, u32[]{:S(2)}) collective-permute-start(bf16[152,768]{1,0:T(8,128)(2,1)S(1)} %get-tuple-element.68), channel_id=1, source_target_pairs={{0,1},{1,0},{2,3},{3,2},{4,5},{5,4},{6,7},{7,6},{8,9},{9,8},{10,11... | collective-permute-start | bytes 700424 | tf_op jit(solution)/shard_map/ppermute | solution.py:208
  52.5 12.2 %collective-permute-start.11 = (bf16[152,640]{1,0:T(8,128)(2,1)S(1)}, bf16[152,640]{1,0:T(8,128)(2,1)S(1)}, u32[]{:S(2)}, u32[]{:S(2)}) collective-permute-start(bf16[152,640]{1,0:T(8,128)(2,1)S(1)} %get-tuple-element.64.refs_7_), channel_id=1, source_target_pairs={{4,8},{12,16},{20,24},{28,0},{8,4},{16,12},{24,20},{0,28},{5,9},{1... | collective-permute-start | bytes 583688 | tf_op jit(solution)/shard_map/ppermute | solution.py:33
  57.0 5.6 %collective-permute-start.14 = (bf16[152,512]{1,0:T(8,128)(2,1)S(1)}, bf16[152,512]{1,0:T(8,128)(2,1)S(1)}, u32[]{:S(2)}, u32[]{:S(2)}) collective-permute-start(bf16[152,512]{1,0:T(8,128)(2,1)S(1)} %get-tuple-element.71), channel_id=1, source_target_pairs={{0,1},{1,0},{2,3},{3,2},{4,5},{5,4},{6,7},{7,6},{8,9},{9,8},{10,11... | collective-permute-start | bytes 466952 | tf_op jit(solution)/shard_map/ppermute | solution.py:208
  58.0 8.8 %collective-permute-start.15 = (bf16[152,768]{1,0:T(8,128)(2,1)S(1)}, bf16[152,768]{1,0:T(8,128)(2,1)S(1)}, u32[]{:S(2)}, u32[]{:S(2)}) collective-permute-start(bf16[152,768]{1,0:T(8,128)(2,1)S(1)} %get-tuple-element.69.refs_6_), channel_id=1, source_target_pairs={{4,8},{12,16},{20,24},{28,0},{8,4},{16,12},{24,20},{0,28},{5,9},{1... | collective-permute-start | bytes 700424 | tf_op jit(solution)/shard_map/ppermute | solution.py:33
  61.3 10.4 %collective-permute-start.16 = (bf16[152,768]{1,0:T(8,128)(2,1)S(1)}, bf16[152,768]{1,0:T(8,128)(2,1)S(1)}, u32[]{:S(2)}, u32[]{:S(2)}) collective-permute-start(bf16[152,768]{1,0:T(8,128)(2,1)S(1)} %get-tuple-element.72.refs_6_), channel_id=1, source_target_pairs={{4,8},{12,16},{20,24},{28,0},{8,4},{16,12},{24,20},{0,28},{5,9},{1... | collective-permute-start | bytes 700424 | tf_op jit(solution)/shard_map/ppermute | solution.py:33
  62.8 12.3 %collective-permute-start.17 = (bf16[152,512]{1,0:T(8,128)(2,1)S(1)}, bf16[152,512]{1,0:T(8,128)(2,1)S(1)}, u32[]{:S(2)}, u32[]{:S(2)}) collective-permute-start(bf16[152,512]{1,0:T(8,128)(2,1)S(1)} %get-tuple-element.74), channel_id=1, source_target_pairs={{4,8},{12,16},{20,24},{28,0},{8,4},{16,12},{24,20},{0,28},{5,9},{1... | collective-permute-start | bytes 466952 | tf_op jit(solution)/shard_map/ppermute | solution.py:33
  64.5 10.7 %collective-permute-start.18 = (f32[152,2688]{1,0:T(8,128)S(1)}, f32[152,2688]{1,0:T(8,128)S(1)}, u32[]{:S(2)}, u32[]{:S(2)}) collective-permute-start(f32[152,2688]{1,0:T(8,128)S(1)} %join.1.refs_3_), channel_id=1, source_target_pairs={{0,4},{8,12},{16,20},{24,28},{4,0},{12,8},{20,16},{28,24},{1,5},{9... | collective-permute-start | bytes 4902920 | tf_op jit(solution)/shard_map/ppermute | solution.py:33

commit v5 on v4

--- a/solution.py
+++ b/solution.py
@@ -15,7 +15,7 @@
 ORDER = (2, 1, 0)
 AHEAD = 2
 STILL_BY = 0
-PIECES = (5, 6, 6)
+PIECES = (6, 5, 5)
 NEAR_WORK = 5_000_000_000
 PAIR_WORK = 20_000_000_000
 AHEAD_WORK = 20_000_000_000

time: 76.8 us -> 75.3 us (0.980)
  waiting for transfers between devices: 27.9 us -> 20.5 us
  starting transfers between devices: 32.4 us -> 38.1 us
    ppermute x6, waiting for transfers between devices: 10.2 us -> 5.51 us  [neighbour(): return lax.ppermute(block, 'blk', route)]
    ppermute x6, starting transfers between devices: 2.86 us -> 7.43 us  [neighbour(): return lax.ppermute(block, 'blk', route)]
    ppermute x13, waiting for transfers between devices: 17.8 us -> 15 us  [send(): return lax.ppermute(block, 'tp', route)]
    ppermute x13, starting transfers between devices: 29.5 us -> 30.6 us  [send(): return lax.ppermute(block, 'tp', route)]
  transfers between devices with their start and end apart: 19 -> 19, of which waited for: 9 -> 7; matrix products, arithmetic and copies ran while one was open for 0% -> 0% of each run, Pallas kernels for 13% -> 14%
where the time goes in v5:
time: 75.3 us; the launch traced here: 74.7 us
  starting transfers between devices  38.1 us (51%)
  waiting for transfers between devices  20.5 us (27%)
  Pallas kernels  11.5 us (15%)
  local copies, waits for them, and re-layouts  4.47 us (6%)
    ppermute x13, starting transfers between devices, send(): return lax.ppermute(block, 'tp', route)  30.6 us
    ppermute x13, waiting for transfers between devices, send(): return lax.ppermute(block, 'tp', route)  15 us
    pallas_call x18, Pallas kernels, call(): pl.pallas_call(body, out_shape=outs, in_specs=[pl.BlockSpec(memory_space=...  8.83 us
    ppermute x6, starting transfers between devices, neighbour(): return lax.ppermute(block, 'blk', route)  7.43 us
    ppermute x6, waiting for transfers between devices, neighbour(): return lax.ppermute(block, 'blk', route)  5.51 us
    unnamed x16, local copies, waits for them, and re-layouts  4.47 us
  transfers between devices with their start and end apart: 19, of which 7 were waited for; matrix products, arithmetic and copies ran while one was open for 0% of the time, Pallas kernels for 14%

profile of v5, /device:TPU:0, one launch (start us, length us, event | category | flops | bytes accessed | tf_op | source)
XLA Modules:
  0.0 74.7 jit_solution(1069838285100118374)
XLA Ops:
  0.0 0.7 collective-permute-start.3
  0.7 5.9 %collective-permute-start = (bf16[256,896]{1,0:T(8,128)(2,1)}, bf16[256,896]{1,0:T(8,128)(2,1)S(1)}, u32[]{:S(2)}, u32[]{:S(2)}) collective-permute-start(bf16[256,896]{1,0:T(8,128)(2,1)} %refs_0_.3), channel_id=1, source_target_pairs={{0,1},{1,0},{2,3},{3,2},{4,5},{5,4},{6,7},{7,6},{8,9},{9,8},{10,11... | collective-permute-start | bytes 1376264 | tf_op jit(solution)/shard_map/ppermute | solution.py:208
  6.6 0.7 collective-permute-start.5
  7.3 1.1 %copy-done = bf16[1,152,3,896]{3,1,2,0:T(8,128)(2,1)S(1)} copy-done((bf16[1,152,3,896]{3,1,2,0:T(8,128)(2,1)S(1)}, bf16[1,152,3,896]{3,1,2,0:T(8,128)(2,1)}, u32[]{:S(2)}) %copy-start) | copy-done | bytes 817176
  8.4 1.1 %copy-done.2 = bf16[1,152,3,896]{3,1,2,0:T(8,128)(2,1)S(1)} copy-done((bf16[1,152,3,896]{3,1,2,0:T(8,128)(2,1)S(1)}, bf16[1,152,3,896]{3,1,2,0:T(8,128)(2,1)}, u32[]{:S(2)}) %copy-start.2) | copy-done | bytes 817176
  9.5 1.1 %copy-done.4 = bf16[1,152,3,896]{3,1,2,0:T(8,128)(2,1)S(1)} copy-done((bf16[1,152,3,896]{3,1,2,0:T(8,128)(2,1)S(1)}, bf16[1,152,3,896]{3,1,2,0:T(8,128)(2,1)}, u32[]{:S(2)}) %copy-start.4) | copy-done | bytes 817176
  10.7 1.0 %copy-done.6 = bf16[256,896]{1,0:T(8,128)(2,1)S(1)} copy-done((bf16[256,896]{1,0:T(8,128)(2,1)S(1)}, bf16[256,896]{1,0:T(8,128)(2,1)}, u32[]{:S(2)}) %copy-start.6) | copy-done | bytes 458776
  11.7 1.4 %still.1 = (f32[3,152,896]{2,1,0:T(8,128)S(1)}, f32[3,152,896]{2,1,0:T(8,128)S(1)}, bf16[256,896]{1,0:T(8,128)(2,1)S(1)}) custom-call(bf16[3,152,896]{2,1,0:T(8,128)(2,1)S(1)} %bitcast.22, bf16[3,152,896]{2,1,0:T(8,128)(2,1)S(1)} %bitcast.12, bf16[3,152,896]{2,1,0:T(8,128)(2,1)S(1)} %bitcast.17, bf16[256,896]{1,0:T(8,128)(2,1)S(1)} %copy-done.6), custom_call_target="tpu_custom_call" | custom-call | tf_op jit(solution)/shard_map/still/pallas_call | solution.py:324
  13.1 1.8 %collective-permute-start.2 = (bf16[256,896]{1,0:T(8,128)(2,1)S(1)}, bf16[256,896]{1,0:T(8,128)(2,1)S(1)}, u32[]{:S(2)}, u32[]{:S(2)}) collective-permute-start(bf16[256,896]{1,0:T(8,128)(2,1)S(1)} %get-tuple-element.40), channel_id=1, source_target_pairs={{0,1},{1,0},{2,3},{3,2},{4,5},{5,4},{6,7},{7,6},{8,9},{9,8},{10,11... | collective-permute-start | bytes 1376264 | tf_op jit(solution)/shard_map/ppermute | solution.py:208
  14.9 1.0 %collective-permute-start.10 = (f32[3,152,896]{2,1,0:T(8,128)S(1)}, f32[3,152,896]{2,1,0:T(8,128)S(1)}, u32[]{:S(2)}, u32[]{:S(2)}) collective-permute-start(f32[3,152,896]{2,1,0:T(8,128)S(1)} %get-tuple-element.41.refs_3_.refs_1_), channel_id=1, source_target_pairs={{4,8},{12,16},{20,24},{28,0},{8,4},{16,12},{24,20},{0,28},{5,9},{1... | collective-permute-start | bytes 4902920 | tf_op jit(solution)/shard_map/ppermute | solution.py:33
  15.9 0.8 %near_forward.1 = (bf16[152,512]{1,0:T(8,128)(2,1)S(1)}, f32[152,512]{1,0:T(8,128)S(1)}, f32[152,512]{1,0:T(8,128)S(1)}, bf16[2,152,896]{2,1,0:T(8,128)(2,1)S(1)}) custom-call(bf16[256,896]{1,0:T(8,128)(2,1)S(1)} %copy-done.7, bf16[256,896]{1,0:T(8,128)(2,1)S(1)} %collective-permute-done.3.refs_1_.refs_0_, bf16[3,152,896]{2,1,0:T(8,128)(2,1)S(1)} %bitcast.23, ...), custom_call_target="tpu_custom_call" | custom-call | flops 5000000000 | tf_op jit(solution)/shard_map/near_forward/pallas_call | solution.py:81
  16.8 2.7 %collective-permute-start.7 = (bf16[2,152,896]{2,1,0:T(8,128)(2,1)S(1)}, bf16[2,152,896]{2,1,0:T(8,128)(2,1)S(1)}, u32[]{:S(2)}, u32[]{:S(2)}) collective-permute-start(bf16[2,152,896]{2,1,0:T(8,128)(2,1)S(1)} %get-tuple-element.50), channel_id=1, source_target_pairs={{0,1},{1,0},{2,3},{3,2},{4,5},{5,4},{6,7},{7,6},{8,9},{9,8},{10,11... | collective-permute-start | bytes 1634312 | tf_op jit(solution)/shard_map/ppermute | solution.py:208
  19.4 0.7 collective-permute-start.1
  20.1 0.5 pair_forward.1
  20.6 7.4 %collective-permute-done.2.refs_0_.refs_5_ = bf16[256,896]{1,0:T(8,128)(2,1)S(1)} collective-permute-done((bf16[256,896]{1,0:T(8,128)(2,1)S(1)}, bf16[256,896]{1,0:T(8,128)(2,1)S(1)}, u32[]{:S(2)}, u32[]{:S(2)}) %collective-permute-start.2) | collective-permute-done | bytes 458784 | tf_op jit(solution)/shard_map/ppermute | solution.py:208
  28.0 0.7 collective-permute-start.4
  28.8 1.8 %near_backward.1 = (f32[3,152,896]{2,1,0:T(8,128)S(1)}, bf16[256,128]{1,0:T(8,128)(2,1)S(1)}) custom-call(bf16[256,896]{1,0:T(8,128)(2,1)S(1)} %copy-done.7, bf16[256,896]{1,0:T(8,128)(2,1)S(1)} %collective-permute-done.3.refs_1_.refs_0_, bf16[256,896]{1,0:T(8,128)(2,1)S(1)} %collective-permute-done.refs_0_.refs_2_, bf16[256,896]{1,0:T(8,128)(2,1)S(1)} %copy-done.6, ...), custom_call_target="tpu_custom_call" | custom-call | tf_op jit(solution)/shard_map/near_backward/pallas_call | solution.py:81
  30.6 0.7 collective-permute-start.6
  31.3 6.9 %collective-permute-start.8 = (bf16[152,896]{1,0:T(8,128)(2,1)S(1)}, bf16[152,896]{1,0:T(8,128)(2,1)S(1)}, u32[]{:S(2)}, u32[]{:S(2)}) collective-permute-start(bf16[152,896]{1,0:T(8,128)(2,1)S(1)} %get-tuple-element.55), channel_id=1, source_target_pairs={{0,1},{1,0},{2,3},{3,2},{4,5},{5,4},{6,7},{7,6},{8,9},{9,8},{10,11... | collective-permute-start | bytes 817160 | tf_op jit(solution)/shard_map/ppermute | solution.py:208
  38.2 1.5 %collective-permute-done.7.refs_3_ = bf16[2,152,896]{2,1,0:T(8,128)(2,1)S(1)} collective-permute-done((bf16[2,152,896]{2,1,0:T(8,128)(2,1)S(1)}, bf16[2,152,896]{2,1,0:T(8,128)(2,1)S(1)}, u32[]{:S(2)}, u32[]{:S(2)}) %collective-permute-start.7) | collective-permute-done | bytes 544800 | tf_op jit(solution)/shard_map/ppermute | solution.py:208
  39.7 1.1 %ahead_forward.1 = (bf16[152,256]{1,0:T(8,128)(2,1)S(1)}, f32[152,256]{1,0:T(8,128)S(1)}, f32[152,256]{1,0:T(8,128)S(1)}, bf16[152,512]{1,0:T(8,128)(2,1)S(1)}, ...) custom-call(bf16[256,896]{1,0:T(8,128)(2,1)S(1)} %collective-permute-done.3.refs_1_.refs_0_, ...), custom_call_target="tpu_custom_call" | custom-call | flops 20000000000 | tf_op jit(solution)/shard_map/ahead_forward/pallas_call | solution.py:81
  40.8 0.3 pair_first.1.refs_4_
  41.1 5.4 %collective-permute-start.9 = (bf16[152,768]{1,0:T(8,128)(2,1)S(1)}, bf16[152,768]{1,0:T(8,128)(2,1)S(1)}, u32[]{:S(2)}, u32[]{:S(2)}) collective-permute-start(bf16[152,768]{1,0:T(8,128)(2,1)S(1)} %pair_first.1.refs_4_), channel_id=1, source_target_pairs={{0,1},{1,0},{2,3},{3,2},{4,5},{5,4},{6,7},{7,6},{8,9},{9,8},{10,11... | collective-permute-start | bytes 700424 | tf_op jit(solution)/shard_map/ppermute | solution.py:208
  46.5 0.3 ahead_backward.1
  46.9 0.9 %far_backward.1.refs_11_.refs_0_ = f32[3,152,896]{2,1,0:T(8,128)S(1)} custom-call(bf16[256,896]{1,0:T(8,128)(2,1)S(1)} %collective-permute-done.1.refs_1_.refs_0_, bf16[256,768]{1,0:T(8,128)(2,1)S(1)} %collective-permute-done.4.refs_2_.refs_1_.refs_3_, bf16[256,128]{1,0:T(8,128)(2,1)S(1)} %collective-permute-done.6.refs_2_.refs_4_, ...), custom_call_target="tpu_custom_call" | custom-call | flops 20000000000 | tf_op jit(solution)/shard_map/far_backward/pallas_call | solution.py:81
  47.8 1.0 %pair_rest.1 = (bf16[152,640]{1,0:T(8,128)(2,1)S(1)}, bf16[152,640]{1,0:T(8,128)(2,1)S(1)}, bf16[152,640]{1,0:T(8,128)(2,1)S(1)}) custom-call(bf16[256,896]{1,0:T(8,128)(2,1)S(1)} %collective-permute-done.3.refs_1_.refs_0_, bf16[256,896]{1,0:T(8,128)(2,1)S(1)} %collective-permute-done.1.refs_1_.refs_0_, ...), custom_call_target="tpu_custom_call" | custom-call | tf_op jit(solution)/shard_map/pair_rest/pallas_call | solution.py:81
  48.8 0.5 collective-permute-start.12
  49.3 2.9 %collective-permute-done.9.refs_5_ = bf16[152,768]{1,0:T(8,128)(2,1)S(1)} collective-permute-done((bf16[152,768]{1,0:T(8,128)(2,1)S(1)}, bf16[152,768]{1,0:T(8,128)(2,1)S(1)}, u32[]{:S(2)}, u32[]{:S(2)}) %collective-permute-start.9) | collective-permute-done | bytes 233504 | tf_op jit(solution)/shard_map/ppermute | solution.py:208
  52.2 0.5 change.4
  52.7 0.1 collective-permute-start.11
  52.8 2.5 %collective-permute-start.13 = (bf16[152,640]{1,0:T(8,128)(2,1)S(1)}, bf16[152,640]{1,0:T(8,128)(2,1)S(1)}, u32[]{:S(2)}, u32[]{:S(2)}) collective-permute-start(bf16[152,640]{1,0:T(8,128)(2,1)S(1)} %get-tuple-element.68), channel_id=1, source_target_pairs={{0,1},{1,0},{2,3},{3,2},{4,5},{5,4},{6,7},{7,6},{8,9},{9,8},{10,11... | collective-permute-start | bytes 583688 | tf_op jit(solution)/shard_map/ppermute | solution.py:208
  55.3 0.4 change.5
  55.7 1.5 %collective-permute-start.14 = (bf16[152,640]{1,0:T(8,128)(2,1)S(1)}, bf16[152,640]{1,0:T(8,128)(2,1)S(1)}, u32[]{:S(2)}, u32[]{:S(2)}) collective-permute-start(bf16[152,640]{1,0:T(8,128)(2,1)S(1)} %get-tuple-element.71), channel_id=1, source_target_pairs={{0,1},{1,0},{2,3},{3,2},{4,5},{5,4},{6,7},{7,6},{8,9},{9,8},{10,11... | collective-permute-start | bytes 583688 | tf_op jit(solution)/shard_map/ppermute | solution.py:208
  57.2 0.9 %collective-permute-start.15 = (bf16[152,640]{1,0:T(8,128)(2,1)S(1)}, bf16[152,640]{1,0:T(8,128)(2,1)S(1)}, u32[]{:S(2)}, u32[]{:S(2)}) collective-permute-start(bf16[152,640]{1,0:T(8,128)(2,1)S(1)} %get-tuple-element.69.refs_6_), channel_id=1, source_target_pairs={{4,8},{12,16},{20,24},{28,0},{8,4},{16,12},{24,20},{0,28},{5,9},{1... | collective-permute-start | bytes 583688 | tf_op jit(solution)/shard_map/ppermute | solution.py:33
  58.1 2.1 %collective-permute-done.13.refs_5_ = bf16[152,640]{1,0:T(8,128)(2,1)S(1)} collective-permute-done((bf16[152,640]{1,0:T(8,128)(2,1)S(1)}, bf16[152,640]{1,0:T(8,128)(2,1)S(1)}, u32[]{:S(2)}, u32[]{:S(2)}) %collective-permute-start.13) | collective-permute-done | bytes 194592 | tf_op jit(solution)/shard_map/ppermute | solution.py:208
  60.2 0.4 change.6
  60.6 2.7 %collective-permute-start.16 = (bf16[152,640]{1,0:T(8,128)(2,1)S(1)}, bf16[152,640]{1,0:T(8,128)(2,1)S(1)}, u32[]{:S(2)}, u32[]{:S(2)}) collective-permute-start(bf16[152,640]{1,0:T(8,128)(2,1)S(1)} %get-tuple-element.72.refs_6_), channel_id=1, source_target_pairs={{4,8},{12,16},{20,24},{28,0},{8,4},{16,12},{24,20},{0,28},{5,9},{1... | collective-permute-start | bytes 583688 | tf_op jit(solution)/shard_map/ppermute | solution.py:33
  63.3 1.1 %collective-permute-done.14.refs_5_ = bf16[152,640]{1,0:T(8,128)(2,1)S(1)} collective-permute-done((bf16[152,640]{1,0:T(8,128)(2,1)S(1)}, bf16[152,640]{1,0:T(8,128)(2,1)S(1)}, u32[]{:S(2)}, u32[]{:S(2)}) %collective-permute-start.14) | collective-permute-done | bytes 194592 | tf_op jit(solution)/shard_map/ppermute | solution.py:208
  64.4 0.4 change.7
  64.8 2.7 %collective-permute-start.17 = (bf16[152,640]{1,0:T(8,128)(2,1)S(1)}, bf16[152,640]{1,0:T(8,128)(2,1)S(1)}, u32[]{:S(2)}, u32[]{:S(2)}) collective-permute-start(bf16[152,640]{1,0:T(8,128)(2,1)S(1)} %get-tuple-element.74), channel_id=1, source_target_pairs={{4,8},{12,16},{20,24},{28,0},{8,4},{16,12},{24,20},{0,28},{5,9},{1... | collective-permute-start | bytes 583688 | tf_op jit(solution)/shard_map/ppermute | solution.py:33
  67.4 0.1 join.1.refs_3_
  67.5 0.1 collective-permute-start.18
  67.6 0.1 across.4.refs_3_.refs_0_
  67.8 1.4 %collective-permute-done.16.refs_2_ = bf16[152,640]{1,0:T(8,128)(2,1)S(1)} collective-permute-done((bf16[152,640]{1,0:T(8,128)(2,1)S(1)}, bf16[152,640]{1,0:T(8,128)(2,1)S(1)}, u32[]{:S(2)}, u32[]{:S(2)}) %collective-permute-start.16) | collective-permute-done | bytes 194592 | tf_op jit(solution)/shard_map/ppermute | solution.py:33
  69.2 0.1 across.6.refs_3_.refs_2_
  69.3 4.1 %collective-permute-done.17.refs_2_ = bf16[152,640]{1,0:T(8,128)(2,1)S(1)} collective-permute-done((bf16[152,640]{1,0:T(8,128)(2,1)S(1)}, bf16[152,640]{1,0:T(8,128)(2,1)S(1)}, u32[]{:S(2)}, u32[]{:S(2)}) %collective-permute-start.17) | collective-permute-done | bytes 194592 | tf_op jit(solution)/shard_map/ppermute | solution.py:33
  73.4 0.1 across.7.refs_3_
  73.5 1.3 %finish.1 = f32[3,152,896]{2,1,0:T(8,128)} custom-call(f32[152,768]{1,0:T(8,128)S(1)} %across.4.refs_3_.refs_0_, f32[152,640]{1,0:T(8,128)S(1)} %across.5.refs_3_.refs_1_, f32[152,640]{1,0:T(8,128)S(1)} %across.6.refs_3_.refs_2_, f32[152,640]{1,0:T(8,128)S(1)} %across.7.refs_3_, f32[152,2688]{1,0:T(8,128)S(1)} %collective-permute-done.18.refs_4_), custom_call_target="tpu_custom_call" | custom-call | tf_op jit(solution)/shard_map/finish/pallas_call | solution.py:411
  (26 shorter events, 0.2 us)
Async XLA Ops:
  0.0 15.9 %collective-permute-start.3 = (bf16[256,896]{1,0:T(8,128)(2,1)}, bf16[256,896]{1,0:T(8,128)(2,1)S(1)}, u32[]{:S(2)}, u32[]{:S(2)}) collective-permute-start(bf16[256,896]{1,0:T(8,128)(2,1)} %refs_0_.3), channel_id=1, source_target_pairs={{1,2},{2,1},{5,6},{6,5},{9,10},{10,9},{13,14},{14,13},{17,18},{18,... | collective-permute-start | bytes 1376264 | tf_op jit(solution)/shard_map/ppermute | solution.py:208
  0.7 18.7 %collective-permute-start = (bf16[256,896]{1,0:T(8,128)(2,1)}, bf16[256,896]{1,0:T(8,128)(2,1)S(1)}, u32[]{:S(2)}, u32[]{:S(2)}) collective-permute-start(bf16[256,896]{1,0:T(8,128)(2,1)} %refs_0_.3), channel_id=1, source_target_pairs={{0,1},{1,0},{2,3},{3,2},{4,5},{5,4},{6,7},{7,6},{8,9},{9,8},{10,11... | collective-permute-start | bytes 1376264 | tf_op jit(solution)/shard_map/ppermute | solution.py:208
  6.6 22.2 %collective-permute-start.5 = (bf16[256,896]{1,0:T(8,128)(2,1)}, bf16[256,896]{1,0:T(8,128)(2,1)S(1)}, u32[]{:S(2)}, u32[]{:S(2)}) collective-permute-start(bf16[256,896]{1,0:T(8,128)(2,1)} %refs_3_.1), channel_id=1, source_target_pairs={{1,2},{2,1},{5,6},{6,5},{9,10},{10,9},{13,14},{14,13},{17,18},{18,... | collective-permute-start | bytes 1376264 | tf_op jit(solution)/shard_map/ppermute | solution.py:208
  7.3 1.1 %copy-start = (bf16[1,152,3,896]{3,1,2,0:T(8,128)(2,1)S(1)}, bf16[1,152,3,896]{3,1,2,0:T(8,128)(2,1)}, u32[]{:S(2)}) copy-start(bf16[1,152,3,896]{3,1,2,0:T(8,128)(2,1)} %param.8) | copy-start | bytes 2451460
  8.4 1.1 %copy-start.2 = (bf16[1,152,3,896]{3,1,2,0:T(8,128)(2,1)S(1)}, bf16[1,152,3,896]{3,1,2,0:T(8,128)(2,1)}, u32[]{:S(2)}) copy-start(bf16[1,152,3,896]{3,1,2,0:T(8,128)(2,1)} %param.9) | copy-start | bytes 2451460
  9.5 1.1 %copy-start.4 = (bf16[1,152,3,896]{3,1,2,0:T(8,128)(2,1)S(1)}, bf16[1,152,3,896]{3,1,2,0:T(8,128)(2,1)}, u32[]{:S(2)}) copy-start(bf16[1,152,3,896]{3,1,2,0:T(8,128)(2,1)} %param.7) | copy-start | bytes 2451460
  10.7 1.0 %copy-start.6 = (bf16[256,896]{1,0:T(8,128)(2,1)S(1)}, bf16[256,896]{1,0:T(8,128)(2,1)}, u32[]{:S(2)}) copy-start(bf16[256,896]{1,0:T(8,128)(2,1)} %refs_3_.1) | copy-start | bytes 1376260
  11.7 4.2 %copy-start.7 = (bf16[256,896]{1,0:T(8,128)(2,1)S(1)}, bf16[256,896]{1,0:T(8,128)(2,1)}, u32[]{:S(2)}) copy-start(bf16[256,896]{1,0:T(8,128)(2,1)} %refs_0_.3) | copy-start | bytes 1376260
  13.1 14.9 %collective-permute-start.2 = (bf16[256,896]{1,0:T(8,128)(2,1)S(1)}, bf16[256,896]{1,0:T(8,128)(2,1)S(1)}, u32[]{:S(2)}, u32[]{:S(2)}) collective-permute-start(bf16[256,896]{1,0:T(8,128)(2,1)S(1)} %get-tuple-element.40), channel_id=1, source_target_pairs={{0,1},{1,0},{2,3},{3,2},{4,5},{5,4},{6,7},{7,6},{8,9},{9,8},{10,11... | collective-permute-start | bytes 1376264 | tf_op jit(solution)/shard_map/ppermute | solution.py:208
  14.9 40.4 %collective-permute-start.10 = (f32[3,152,896]{2,1,0:T(8,128)S(1)}, f32[3,152,896]{2,1,0:T(8,128)S(1)}, u32[]{:S(2)}, u32[]{:S(2)}) collective-permute-start(f32[3,152,896]{2,1,0:T(8,128)S(1)} %get-tuple-element.41.refs_3_.refs_1_), channel_id=1, source_target_pairs={{4,8},{12,16},{20,24},{28,0},{8,4},{16,12},{24,20},{0,28},{5,9},{1... | collective-permute-start | bytes 4902920 | tf_op jit(solution)/shard_map/ppermute | solution.py:33
  16.8 22.9 %collective-permute-start.7 = (bf16[2,152,896]{2,1,0:T(8,128)(2,1)S(1)}, bf16[2,152,896]{2,1,0:T(8,128)(2,1)S(1)}, u32[]{:S(2)}, u32[]{:S(2)}) collective-permute-start(bf16[2,152,896]{2,1,0:T(8,128)(2,1)S(1)} %get-tuple-element.50), channel_id=1, source_target_pairs={{0,1},{1,0},{2,3},{3,2},{4,5},{5,4},{6,7},{7,6},{8,9},{9,8},{10,11... | collective-permute-start | bytes 1634312 | tf_op jit(solution)/shard_map/ppermute | solution.py:208
  19.4 11.8 %collective-permute-start.1 = (bf16[256,896]{1,0:T(8,128)(2,1)S(1)}, bf16[256,896]{1,0:T(8,128)(2,1)S(1)}, u32[]{:S(2)}, u32[]{:S(2)}) collective-permute-start(bf16[256,896]{1,0:T(8,128)(2,1)S(1)} %collective-permute-done.refs_0_.refs_2_), channel_id=1, source_target_pairs={{1,2},{2,1},{5,6},{6,5},{9,10},{10,9},{13,14},{14,13},{17,18},{18,... | collective-permute-start | bytes 1376264 | tf_op jit(solution)/shard_map/ppermute | solution.py:208
  28.0 12.7 %collective-permute-start.4 = (bf16[256,768]{1,0:T(8,128)(2,1)S(1)}, bf16[256,768]{1,0:T(8,128)(2,1)S(1)}, u32[]{:S(2)}, u32[]{:S(2)}) collective-permute-start(bf16[256,768]{1,0:T(8,128)(2,1)S(1)} %get-tuple-element.44.refs_13_), channel_id=1, source_target_pairs={{1,2},{2,1},{5,6},{6,5},{9,10},{10,9},{13,14},{14,13},{17,18},{18,... | collective-permute-start | bytes 1179656 | tf_op jit(solution)/shard_map/ppermute | solution.py:208
  30.6 16.3 %collective-permute-start.6 = (bf16[256,128]{1,0:T(8,128)(2,1)S(1)}, bf16[256,128]{1,0:T(8,128)(2,1)S(1)}, u32[]{:S(2)}, u32[]{:S(2)}) collective-permute-start(bf16[256,128]{1,0:T(8,128)(2,1)S(1)} %get-tuple-element.49), channel_id=1, source_target_pairs={{1,2},{2,1},{5,6},{6,5},{9,10},{10,9},{13,14},{14,13},{17,18},{18,... | collective-permute-start | bytes 196616 | tf_op jit(solution)/shard_map/ppermute | solution.py:208
  31.3 15.3 %collective-permute-start.8 = (bf16[152,896]{1,0:T(8,128)(2,1)S(1)}, bf16[152,896]{1,0:T(8,128)(2,1)S(1)}, u32[]{:S(2)}, u32[]{:S(2)}) collective-permute-start(bf16[152,896]{1,0:T(8,128)(2,1)S(1)} %get-tuple-element.55), channel_id=1, source_target_pairs={{0,1},{1,0},{2,3},{3,2},{4,5},{5,4},{6,7},{7,6},{8,9},{9,8},{10,11... | collective-permute-start | bytes 817160 | tf_op jit(solution)/shard_map/ppermute | solution.py:208
  40.8 6.1 %copy-start.5 = (bf16[1,152,3,896]{3,1,2,0:T(8,128)(2,1)S(1)}, bf16[1,152,3,896]{3,1,2,0:T(8,128)(2,1)}, u32[]{:S(2)}) copy-start(bf16[1,152,3,896]{3,1,2,0:T(8,128)(2,1)} %param.7) | copy-start | bytes 2451460
  41.1 11.1 %collective-permute-start.9 = (bf16[152,768]{1,0:T(8,128)(2,1)S(1)}, bf16[152,768]{1,0:T(8,128)(2,1)S(1)}, u32[]{:S(2)}, u32[]{:S(2)}) collective-permute-start(bf16[152,768]{1,0:T(8,128)(2,1)S(1)} %pair_first.1.refs_4_), channel_id=1, source_target_pairs={{0,1},{1,0},{2,3},{3,2},{4,5},{5,4},{6,7},{7,6},{8,9},{9,8},{10,11... | collective-permute-start | bytes 700424 | tf_op jit(solution)/shard_map/ppermute | solution.py:208
  47.8 4.4 %copy-start.1 = (bf16[1,152,3,896]{3,1,2,0:T(8,128)(2,1)S(1)}, bf16[1,152,3,896]{3,1,2,0:T(8,128)(2,1)}, u32[]{:S(2)}) copy-start(bf16[1,152,3,896]{3,1,2,0:T(8,128)(2,1)} %param.8) | copy-start | bytes 2451460
  47.8 4.4 %copy-start.3 = (bf16[1,152,3,896]{3,1,2,0:T(8,128)(2,1)S(1)}, bf16[1,152,3,896]{3,1,2,0:T(8,128)(2,1)}, u32[]{:S(2)}) copy-start(bf16[1,152,3,896]{3,1,2,0:T(8,128)(2,1)} %param.9) | copy-start | bytes 2451460
  48.8 6.5 %collective-permute-start.12 = (bf16[152,640]{1,0:T(8,128)(2,1)S(1)}, bf16[152,640]{1,0:T(8,128)(2,1)S(1)}, u32[]{:S(2)}, u32[]{:S(2)}) collective-permute-start(bf16[152,640]{1,0:T(8,128)(2,1)S(1)} %get-tuple-element.65), channel_id=1, source_target_pairs={{0,1},{1,0},{2,3},{3,2},{4,5},{5,4},{6,7},{7,6},{8,9},{9,8},{10,11... | collective-permute-start | bytes 583688 | tf_op jit(solution)/shard_map/ppermute | solution.py:208
  52.7 15.0 %collective-permute-start.11 = (bf16[152,768]{1,0:T(8,128)(2,1)S(1)}, bf16[152,768]{1,0:T(8,128)(2,1)S(1)}, u32[]{:S(2)}, u32[]{:S(2)}) collective-permute-start(bf16[152,768]{1,0:T(8,128)(2,1)S(1)} %get-tuple-element.64.refs_7_), channel_id=1, source_target_pairs={{4,8},{12,16},{20,24},{28,0},{8,4},{16,12},{24,20},{0,28},{5,9},{1... | collective-permute-start | bytes 700424 | tf_op jit(solution)/shard_map/ppermute | solution.py:33
  52.8 7.5 %collective-permute-start.13 = (bf16[152,640]{1,0:T(8,128)(2,1)S(1)}, bf16[152,640]{1,0:T(8,128)(2,1)S(1)}, u32[]{:S(2)}, u32[]{:S(2)}) collective-permute-start(bf16[152,640]{1,0:T(8,128)(2,1)S(1)} %get-tuple-element.68), channel_id=1, source_target_pairs={{0,1},{1,0},{2,3},{3,2},{4,5},{5,4},{6,7},{7,6},{8,9},{9,8},{10,11... | collective-permute-start | bytes 583688 | tf_op jit(solution)/shard_map/ppermute | solution.py:208
  55.7 8.7 %collective-permute-start.14 = (bf16[152,640]{1,0:T(8,128)(2,1)S(1)}, bf16[152,640]{1,0:T(8,128)(2,1)S(1)}, u32[]{:S(2)}, u32[]{:S(2)}) collective-permute-start(bf16[152,640]{1,0:T(8,128)(2,1)S(1)} %get-tuple-element.71), channel_id=1, source_target_pairs={{0,1},{1,0},{2,3},{3,2},{4,5},{5,4},{6,7},{7,6},{8,9},{9,8},{10,11... | collective-permute-start | bytes 583688 | tf_op jit(solution)/shard_map/ppermute | solution.py:208
  57.2 10.5 %collective-permute-start.15 = (bf16[152,640]{1,0:T(8,128)(2,1)S(1)}, bf16[152,640]{1,0:T(8,128)(2,1)S(1)}, u32[]{:S(2)}, u32[]{:S(2)}) collective-permute-start(bf16[152,640]{1,0:T(8,128)(2,1)S(1)} %get-tuple-element.69.refs_6_), channel_id=1, source_target_pairs={{4,8},{12,16},{20,24},{28,0},{8,4},{16,12},{24,20},{0,28},{5,9},{1... | collective-permute-start | bytes 583688 | tf_op jit(solution)/shard_map/ppermute | solution.py:33
  60.6 8.6 %collective-permute-start.16 = (bf16[152,640]{1,0:T(8,128)(2,1)S(1)}, bf16[152,640]{1,0:T(8,128)(2,1)S(1)}, u32[]{:S(2)}, u32[]{:S(2)}) collective-permute-start(bf16[152,640]{1,0:T(8,128)(2,1)S(1)} %get-tuple-element.72.refs_6_), channel_id=1, source_target_pairs={{4,8},{12,16},{20,24},{28,0},{8,4},{16,12},{24,20},{0,28},{5,9},{1... | collective-permute-start | bytes 583688 | tf_op jit(solution)/shard_map/ppermute | solution.py:33
  64.8 8.6 %collective-permute-start.17 = (bf16[152,640]{1,0:T(8,128)(2,1)S(1)}, bf16[152,640]{1,0:T(8,128)(2,1)S(1)}, u32[]{:S(2)}, u32[]{:S(2)}) collective-permute-start(bf16[152,640]{1,0:T(8,128)(2,1)S(1)} %get-tuple-element.74), channel_id=1, source_target_pairs={{4,8},{12,16},{20,24},{28,0},{8,4},{16,12},{24,20},{0,28},{5,9},{1... | collective-permute-start | bytes 583688 | tf_op jit(solution)/shard_map/ppermute | solution.py:33
  67.5 5.9 %collective-permute-start.18 = (f32[152,2688]{1,0:T(8,128)S(1)}, f32[152,2688]{1,0:T(8,128)S(1)}, u32[]{:S(2)}, u32[]{:S(2)}) collective-permute-start(f32[152,2688]{1,0:T(8,128)S(1)} %join.1.refs_3_), channel_id=1, source_target_pairs={{0,4},{8,12},{16,20},{24,28},{4,0},{12,8},{20,16},{28,24},{1,5},{9... | collective-permute-start | bytes 4902920 | tf_op jit(solution)/shard_map/ppermute | solution.py:33

commit v6 on v5

--- a/solution.py
+++ b/solution.py
@@ -15,12 +15,13 @@
 ORDER = (2, 1, 0)
 AHEAD = 2
 STILL_BY = 0
-PIECES = (6, 5, 5)
+PIECES = (5, 5, 6)
 NEAR_WORK = 5_000_000_000
 PAIR_WORK = 20_000_000_000
 AHEAD_WORK = 20_000_000_000
 ACROSS_WORK = (20_000_000_000, 2_000_000_000, 2_000_000_000, 30_000_000_000)
-FAR_WORK = 20_000_000_000
+FAR_WORK = 0
+CHANGE_WORK = (0, 5_000_000_000, 5_000_000_000, 0)
 
 
 def neighbour(block, side):
@@ -116,10 +117,9 @@
 
 def near_backward(
     own_x, inner_x, pair_x, own_g, inner_g, pair_g,
-    rows, hidden, swish, slope, pair_hidden, pair_swish, pair_slope, grads, more, *, scale
+    rows, hidden, swish, slope, pair_hidden, pair_swish, pair_slope, grads, *, scale
 ):
     size, width = own_x.shape
-    more[...] = pair_g[:, width - more.shape[1] :]
     totals = [0.0, 0.0, 0.0]
     first, second = pl.ds(0, size), pl.ds(size, size)
     shards = (
@@ -136,15 +136,9 @@
         grads[k] = totals[k] * (scale if k == 2 else width ** (-0.5))
 
 
-def ahead_forward(inner_x, far_x, rows, pair_top, *terms):
-    far_hidden, far_swish, far_slope, hidden, swish, slope = terms
-    size = inner_x.shape[0]
-    for i, xs in enumerate((inner_x, far_x)):
-        place = pl.ds(i * size, size)
-        hidden[:, place], swish[:, place], slope[:, place] = forward_terms(
-            xs[...], pair_top[0], pair_top[1]
-        )
-    far_hidden[...], far_swish[...], far_slope[...] = forward_terms(far_x[...], rows[0], rows[1])
+def far_forward(far_x, rows, pair_g, hidden, swish, slope, more):
+    more[...] = pair_g[:, pair_g.shape[1] - more.shape[1] :]
+    hidden[...], swish[...], slope[...] = forward_terms(far_x[...], rows[0], rows[1])
 
 
 def ahead_backward(inner_g, pair_low, swish, slope, dgate, dupper, *, scale):
@@ -238,24 +232,30 @@
         name="cut",
     )
     pair_low = send(low, pairs)
-    near, pair_more = call(
+    near = call(
         functools.partial(near_backward, scale=scale),
-        [array((3, units, width), FULL), array((size, cuts[1]), HALF)],
+        [array((3, units, width), FULL)],
         (tokens, inner_x, pair_x, cots, inner_g, pair_g, rows, *near_terms, *pair_terms),
         after=(pair_part,),
         name="near_backward",
+    )[0]
+    *far_terms, pair_more = call(
+        far_forward,
+        [array((units, size), t) for t in (HALF, FULL, FULL)]
+        + [array((size, cuts[1]), HALF)],
+        (far_x, rows, pair_g),
+        after=(near,),
+        name="far_forward",
     )
     far_gs = [send(v, middle) for v in (pair_part, pair_more)]
-    ahead = call(
-        ahead_forward,
-        [array((units, size), t) for t in (HALF, FULL, FULL)]
-        + [array((units, 2 * size), t) for t in (HALF, FULL, FULL)],
-        (inner_x, far_x, rows, pair_top),
-        after=(near,),
+    hidden, swish, slope = call(
+        near_forward,
+        [array((units, 2 * size), t) for t in (HALF, FULL, FULL)],
+        (inner_x, far_x, pair_top),
+        after=(pair_more,),
         flops=AHEAD_WORK,
         name="ahead_forward",
     )
-    far_terms, (hidden, swish, slope) = ahead[:3], ahead[3:]
     sizes = [width * v // (7 * 128) * 128 for v in PIECES]
     sizes.append(3 * width - sum(sizes))
     cut, more = sizes[0], sizes[0] + sizes[1] - width
@@ -359,13 +359,14 @@
         sent[:, here] = total.astype(HALF)
 
 
-def change_of(piece, grads, still, still_step, first, second, came, ready, after):
+def change_of(piece, grads, still, still_step, first, second, came, ready, after, flops):
     shape = (grads.shape[1], columns_of(piece))
     return call(
         functools.partial(change_kernel, piece=piece, parts=len(came), ready=len(ready)),
         [array(shape, FULL), array(shape, HALF)] + [array(v.shape, v.dtype) for v in ready],
         (grads, still, still_step, first, second, *came, *ready),
         after=after,
+        flops=flops,
         name="change",
     )
 
@@ -381,6 +382,18 @@
 def across_kernel(updated, still, far, total, *, piece):
     for k, place, here in spans(piece):
         total[:, here] = updated[:, here] + still[k, :, place] + far[:, here].astype(FULL)
+
+
+def across_of(i, change, still, after):
+    piece, updated, far = change
+    return call(
+        functools.partial(across_kernel, piece=piece),
+        [array(updated.shape, FULL)],
+        (updated, still, far),
+        after=after,
+        flops=ACROSS_WORK[i],
+        name="across",
+    )[0]
 
 
 def finish_kernel(*refs, pieces, bands):
@@ -440,32 +453,36 @@
     else:
         grads = gathered(tokens, cotangent, rows, scale)
         pieces = [([(k, 0, rows.shape[2])], None) for k in ORDER]
+    count = len(pieces)
     came = [[] if v is None else [send(v)] for _, v in pieces[:AHEAD]]
     changes, last = [], ()
     for i, (piece, _) in enumerate(pieces):
         ready = [v for _, v in pieces[i + AHEAD : i + AHEAD + 1] if v is not None]
         updated, sent, *ready = change_of(
-            piece, grads, still, still_step, first, second, came[i], ready, last
+            piece,
+            grads,
+            still,
+            still_step,
+            first,
+            second,
+            came[i],
+            ready,
+            last,
+            CHANGE_WORK[i],
         )
         came.append([send(v) for v in ready])
         changes.append((piece, updated, neighbour(sent, 1)))
         last = (sent, still_far) if i == STILL_BY else (sent,)
+        if i == count - 2:
+            totals = [across_of(0, changes[0], still_far, last)]
+            last += (totals[0],)
     updates = [v for _, v, _ in changes]
     joint = call(
         join_kernel, [array((rows.shape[1], 3 * width), FULL)], updates, name="join"
     )[0]
     near = neighbour(joint, 0)
-    totals, last = [], (joint,)
-    for i, (piece, updated, far) in enumerate(changes):
-        totals += call(
-            functools.partial(across_kernel, piece=piece),
-            [array(updated.shape, FULL)],
-            (updated, still_far, far),
-            after=last,
-            flops=ACROSS_WORK[i],
-            name="across",
-        )
-        last = totals[-1:]
+    for i in range(1, count):
+        totals.append(across_of(i, changes[i], still_far, (joint, totals[-1])))
     out = finish([v for v, _, _ in changes], totals, near, rows.shape)
     return jnp.swapaxes(out, 0, 1)[None]
 

time: 75.3 us -> 74 us (0.983)
  starting transfers between devices: 38.1 us -> 33 us
  waiting for transfers between devices: 20.5 us -> 24.3 us
    ppermute x13, starting transfers between devices: 30.6 us -> 25.8 us  [send(): return lax.ppermute(block, 'tp', route)]
    ppermute x13, waiting for transfers between devices: 15 us -> 17.8 us  [send(): return lax.ppermute(block, 'tp', route)]
    ppermute x6, waiting for transfers between devices: 5.51 us -> 6.54 us  [neighbour(): return lax.ppermute(block, 'blk', route)]
    pallas_call x18 -> x19, Pallas kernels: 8.83 us -> 8.94 us  [call(): pl.pallas_call(body, out_shape=outs, in_specs=[pl.BlockSpec(memory_space=...]
    unnamed x16 -> x18, local copies, waits for them, and re-layouts: 4.47 us -> 4.47 us
  transfers between devices with their start and end apart: 19 -> 19, of which waited for: 7 -> 9; matrix products, arithmetic and copies ran while one was open for 0% -> 0% of each run, Pallas kernels for 14% -> 14%
where the time goes in v6:
time: 74 us; the launch traced here: 73.6 us
  starting transfers between devices  33 us (45%)
  waiting for transfers between devices  24.3 us (33%)
  Pallas kernels  11.6 us (16%)
  local copies, waits for them, and re-layouts  4.47 us (6%)
    ppermute x13, starting transfers between devices, send(): return lax.ppermute(block, 'tp', route)  25.8 us
    ppermute x13, waiting for transfers between devices, send(): return lax.ppermute(block, 'tp', route)  17.8 us
    pallas_call x19, Pallas kernels, call(): pl.pallas_call(body, out_shape=outs, in_specs=[pl.BlockSpec(memory_space=...  8.94 us
    ppermute x6, starting transfers between devices, neighbour(): return lax.ppermute(block, 'blk', route)  7.2 us
    ppermute x6, waiting for transfers between devices, neighbour(): return lax.ppermute(block, 'blk', route)  6.54 us
    unnamed x18, local copies, waits for them, and re-layouts  4.47 us
  transfers between devices with their start and end apart: 19, of which 9 were waited for; matrix products, arithmetic and copies ran while one was open for 0% of the time, Pallas kernels for 14%

profile of v6, /device:TPU:0, one launch (start us, length us, event | category | flops | bytes accessed | tf_op | source)
XLA Modules:
  0.0 73.6 jit_solution(14021347481568931244)
XLA Ops:
  0.0 0.7 collective-permute-start.3
  0.7 5.9 %collective-permute-start = (bf16[256,896]{1,0:T(8,128)(2,1)}, bf16[256,896]{1,0:T(8,128)(2,1)S(1)}, u32[]{:S(2)}, u32[]{:S(2)}) collective-permute-start(bf16[256,896]{1,0:T(8,128)(2,1)} %refs_0_.3), channel_id=1, source_target_pairs={{0,1},{1,0},{2,3},{3,2},{4,5},{5,4},{6,7},{7,6},{8,9},{9,8},{10,11... | collective-permute-start | bytes 1376264 | tf_op jit(solution)/shard_map/ppermute | solution.py:202
  6.6 0.7 collective-permute-start.5
  7.3 1.1 %copy-done = bf16[1,152,3,896]{3,1,2,0:T(8,128)(2,1)S(1)} copy-done((bf16[1,152,3,896]{3,1,2,0:T(8,128)(2,1)S(1)}, bf16[1,152,3,896]{3,1,2,0:T(8,128)(2,1)}, u32[]{:S(2)}) %copy-start) | copy-done | bytes 817176
  8.4 1.1 %copy-done.2 = bf16[1,152,3,896]{3,1,2,0:T(8,128)(2,1)S(1)} copy-done((bf16[1,152,3,896]{3,1,2,0:T(8,128)(2,1)S(1)}, bf16[1,152,3,896]{3,1,2,0:T(8,128)(2,1)}, u32[]{:S(2)}) %copy-start.2) | copy-done | bytes 817176
  9.5 1.1 %copy-done.4 = bf16[1,152,3,896]{3,1,2,0:T(8,128)(2,1)S(1)} copy-done((bf16[1,152,3,896]{3,1,2,0:T(8,128)(2,1)S(1)}, bf16[1,152,3,896]{3,1,2,0:T(8,128)(2,1)}, u32[]{:S(2)}) %copy-start.4) | copy-done | bytes 817176
  10.7 1.0 %copy-done.6 = bf16[256,896]{1,0:T(8,128)(2,1)S(1)} copy-done((bf16[256,896]{1,0:T(8,128)(2,1)S(1)}, bf16[256,896]{1,0:T(8,128)(2,1)}, u32[]{:S(2)}) %copy-start.6) | copy-done | bytes 458776
  11.7 1.4 %still.1 = (f32[3,152,896]{2,1,0:T(8,128)S(1)}, f32[3,152,896]{2,1,0:T(8,128)S(1)}, bf16[256,896]{1,0:T(8,128)(2,1)S(1)}) custom-call(bf16[3,152,896]{2,1,0:T(8,128)(2,1)S(1)} %bitcast.12, bf16[3,152,896]{2,1,0:T(8,128)(2,1)S(1)} %bitcast.19, bf16[3,152,896]{2,1,0:T(8,128)(2,1)S(1)} %bitcast.24, bf16[256,896]{1,0:T(8,128)(2,1)S(1)} %copy-done.6), custom_call_target="tpu_custom_call" | custom-call | tf_op jit(solution)/shard_map/still/pallas_call | solution.py:324
  13.1 1.8 %collective-permute-start.2 = (bf16[256,896]{1,0:T(8,128)(2,1)S(1)}, bf16[256,896]{1,0:T(8,128)(2,1)S(1)}, u32[]{:S(2)}, u32[]{:S(2)}) collective-permute-start(bf16[256,896]{1,0:T(8,128)(2,1)S(1)} %get-tuple-element.39), channel_id=1, source_target_pairs={{0,1},{1,0},{2,3},{3,2},{4,5},{5,4},{6,7},{7,6},{8,9},{9,8},{10,11... | collective-permute-start | bytes 1376264 | tf_op jit(solution)/shard_map/ppermute | solution.py:202
  14.9 1.0 %collective-permute-start.10 = (f32[3,152,896]{2,1,0:T(8,128)S(1)}, f32[3,152,896]{2,1,0:T(8,128)S(1)}, u32[]{:S(2)}, u32[]{:S(2)}) collective-permute-start(f32[3,152,896]{2,1,0:T(8,128)S(1)} %get-tuple-element.40.refs_3_.refs_1_), channel_id=1, source_target_pairs={{4,8},{12,16},{20,24},{28,0},{8,4},{16,12},{24,20},{0,28},{5,9},{1... | collective-permute-start | bytes 4902920 | tf_op jit(solution)/shard_map/ppermute | solution.py:34
  15.9 0.8 %near_forward.1 = (bf16[152,512]{1,0:T(8,128)(2,1)S(1)}, f32[152,512]{1,0:T(8,128)S(1)}, f32[152,512]{1,0:T(8,128)S(1)}, bf16[2,152,896]{2,1,0:T(8,128)(2,1)S(1)}) custom-call(bf16[256,896]{1,0:T(8,128)(2,1)S(1)} %copy-done.8, bf16[256,896]{1,0:T(8,128)(2,1)S(1)} %collective-permute-done.3.refs_1_.refs_0_, bf16[3,152,896]{2,1,0:T(8,128)(2,1)S(1)} %bitcast.13, ...), custom_call_target="tpu_custom_call" | custom-call | flops 5000000000 | tf_op jit(solution)/shard_map/near_forward/pallas_call | solution.py:82
  16.8 2.7 %collective-permute-start.8 = (bf16[2,152,896]{2,1,0:T(8,128)(2,1)S(1)}, bf16[2,152,896]{2,1,0:T(8,128)(2,1)S(1)}, u32[]{:S(2)}, u32[]{:S(2)}) collective-permute-start(bf16[2,152,896]{2,1,0:T(8,128)(2,1)S(1)} %get-tuple-element.53), channel_id=1, source_target_pairs={{0,1},{1,0},{2,3},{3,2},{4,5},{5,4},{6,7},{7,6},{8,9},{9,8},{10,11... | collective-permute-start | bytes 1634312 | tf_op jit(solution)/shard_map/ppermute | solution.py:202
  19.4 0.7 collective-permute-start.1
  20.1 0.5 pair_forward.1
  20.6 7.4 %collective-permute-done.2.refs_0_.refs_5_.refs_2_ = bf16[256,896]{1,0:T(8,128)(2,1)S(1)} collective-permute-done((bf16[256,896]{1,0:T(8,128)(2,1)S(1)}, bf16[256,896]{1,0:T(8,128)(2,1)S(1)}, u32[]{:S(2)}, u32[]{:S(2)}) %collective-permute-start.2) | collective-permute-done | bytes 458784 | tf_op jit(solution)/shard_map/ppermute | solution.py:202
  28.0 2.1 %collective-permute-start.7 = (bf16[152,896]{1,0:T(8,128)(2,1)S(1)}, bf16[152,896]{1,0:T(8,128)(2,1)S(1)}, u32[]{:S(2)}, u32[]{:S(2)}) collective-permute-start(bf16[152,896]{1,0:T(8,128)(2,1)S(1)} %get-tuple-element.52), channel_id=1, source_target_pairs={{0,1},{1,0},{2,3},{3,2},{4,5},{5,4},{6,7},{7,6},{8,9},{9,8},{10,11... | collective-permute-start | bytes 817160 | tf_op jit(solution)/shard_map/ppermute | solution.py:202
  30.2 0.7 collective-permute-start.4
  30.9 1.8 %near_backward.1.refs_3_.refs_7_ = f32[3,152,896]{2,1,0:T(8,128)S(1)} custom-call(bf16[256,896]{1,0:T(8,128)(2,1)S(1)} %copy-done.8, bf16[256,896]{1,0:T(8,128)(2,1)S(1)} %collective-permute-done.3.refs_1_.refs_0_, bf16[256,896]{1,0:T(8,128)(2,1)S(1)} %collective-permute-done.refs_0_.refs_2_, bf16[256,896]{1,0:T(8,128)(2,1)S(1)} %copy-done.7, ...), custom_call_target="tpu_custom_call" | custom-call | tf_op jit(solution)/shard_map/near_backward/pallas_call | solution.py:82
  32.7 0.5 far_forward.1
  33.2 0.7 collective-permute-start.6
  33.9 5.8 %collective-permute-done.8.refs_2_ = bf16[2,152,896]{2,1,0:T(8,128)(2,1)S(1)} collective-permute-done((bf16[2,152,896]{2,1,0:T(8,128)(2,1)S(1)}, bf16[2,152,896]{2,1,0:T(8,128)(2,1)S(1)}, u32[]{:S(2)}, u32[]{:S(2)}) %collective-permute-start.8) | collective-permute-done | bytes 544800 | tf_op jit(solution)/shard_map/ppermute | solution.py:202
  39.7 0.8 %ahead_forward.1 = (bf16[152,512]{1,0:T(8,128)(2,1)S(1)}, f32[152,512]{1,0:T(8,128)S(1)}, f32[152,512]{1,0:T(8,128)S(1)}) custom-call(bf16[256,896]{1,0:T(8,128)(2,1)S(1)} %collective-permute-done.3.refs_1_.refs_0_, bf16[256,896]{1,0:T(8,128)(2,1)S(1)} %collective-permute-done.1.refs_0_.refs_1_, bf16[2,152,896]{2,1,0:T(8,128)(2,1)S(1)} %collective-permute-done.8.refs_2_, ...), custom_call_target="tpu_custom_call" | custom-call | flops 20000000000 | tf_op jit(solution)/shard_map/ahead_forward/pallas_call | solution.py:82
  40.5 0.3 pair_first.1.refs_4_
  40.8 4.8 %collective-permute-start.9 = (bf16[152,640]{1,0:T(8,128)(2,1)S(1)}, bf16[152,640]{1,0:T(8,128)(2,1)S(1)}, u32[]{:S(2)}, u32[]{:S(2)}) collective-permute-start(bf16[152,640]{1,0:T(8,128)(2,1)S(1)} %pair_first.1.refs_4_), channel_id=1, source_target_pairs={{0,1},{1,0},{2,3},{3,2},{4,5},{5,4},{6,7},{7,6},{8,9},{9,8},{10,11... | collective-permute-start | bytes 583688 | tf_op jit(solution)/shard_map/ppermute | solution.py:202
  45.6 0.3 ahead_backward.1
  45.9 0.9 %far_backward.1.refs_11_.refs_0_ = f32[3,152,896]{2,1,0:T(8,128)S(1)} custom-call(bf16[256,896]{1,0:T(8,128)(2,1)S(1)} %collective-permute-done.1.refs_0_.refs_1_, bf16[256,640]{1,0:T(8,128)(2,1)S(1)} %collective-permute-done.4.refs_2_.refs_1_.refs_3_, bf16[256,256]{1,0:T(8,128)(2,1)S(1)} %collective-permute-done.6.refs_2_.refs_4_, ...), custom_call_target="tpu_custom_call" | custom-call | tf_op jit(solution)/shard_map/far_backward/pallas_call | solution.py:82
  46.9 1.0 %pair_rest.1 = (bf16[152,640]{1,0:T(8,128)(2,1)S(1)}, bf16[152,768]{1,0:T(8,128)(2,1)S(1)}, bf16[152,640]{1,0:T(8,128)(2,1)S(1)}) custom-call(bf16[256,896]{1,0:T(8,128)(2,1)S(1)} %collective-permute-done.3.refs_1_.refs_0_, bf16[256,896]{1,0:T(8,128)(2,1)S(1)} %collective-permute-done.1.refs_0_.refs_1_, ...), custom_call_target="tpu_custom_call" | custom-call | tf_op jit(solution)/shard_map/pair_rest/pallas_call | solution.py:82
  47.8 1.0 %collective-permute-start.13 = (bf16[152,640]{1,0:T(8,128)(2,1)S(1)}, bf16[152,640]{1,0:T(8,128)(2,1)S(1)}, u32[]{:S(2)}, u32[]{:S(2)}) collective-permute-start(bf16[152,640]{1,0:T(8,128)(2,1)S(1)} %get-tuple-element.64), channel_id=1, source_target_pairs={{0,1},{1,0},{2,3},{3,2},{4,5},{5,4},{6,7},{7,6},{8,9},{9,8},{10,11... | collective-permute-start | bytes 583688 | tf_op jit(solution)/shard_map/ppermute | solution.py:202
  48.8 0.8 %collective-permute-done.9.refs_5_ = bf16[152,640]{1,0:T(8,128)(2,1)S(1)} collective-permute-done((bf16[152,640]{1,0:T(8,128)(2,1)S(1)}, bf16[152,640]{1,0:T(8,128)(2,1)S(1)}, u32[]{:S(2)}, u32[]{:S(2)}) %collective-permute-start.9) | collective-permute-done | bytes 194592 | tf_op jit(solution)/shard_map/ppermute | solution.py:202
  49.7 0.4 change.4
  50.1 0.1 collective-permute-start.11
  50.2 2.4 %collective-permute-start.12 = (bf16[152,768]{1,0:T(8,128)(2,1)S(1)}, bf16[152,768]{1,0:T(8,128)(2,1)S(1)}, u32[]{:S(2)}, u32[]{:S(2)}) collective-permute-start(bf16[152,768]{1,0:T(8,128)(2,1)S(1)} %get-tuple-element.63), channel_id=1, source_target_pairs={{0,1},{1,0},{2,3},{3,2},{4,5},{5,4},{6,7},{7,6},{8,9},{9,8},{10,11... | collective-permute-start | bytes 700424 | tf_op jit(solution)/shard_map/ppermute | solution.py:202
  52.6 1.0 %collective-permute-done.13.refs_5_ = bf16[152,640]{1,0:T(8,128)(2,1)S(1)} collective-permute-done((bf16[152,640]{1,0:T(8,128)(2,1)S(1)}, bf16[152,640]{1,0:T(8,128)(2,1)S(1)}, u32[]{:S(2)}, u32[]{:S(2)}) %collective-permute-start.13) | collective-permute-done | bytes 194592 | tf_op jit(solution)/shard_map/ppermute | solution.py:202
  53.5 0.1 collective-permute-done.10.refs_8_.refs_1_
  53.7 0.4 change.5
  54.1 1.8 %collective-permute-start.15 = (bf16[152,640]{1,0:T(8,128)(2,1)S(1)}, bf16[152,640]{1,0:T(8,128)(2,1)S(1)}, u32[]{:S(2)}, u32[]{:S(2)}) collective-permute-start(bf16[152,640]{1,0:T(8,128)(2,1)S(1)} %get-tuple-element.70), channel_id=1, source_target_pairs={{0,1},{1,0},{2,3},{3,2},{4,5},{5,4},{6,7},{7,6},{8,9},{9,8},{10,11... | collective-permute-start | bytes 583688 | tf_op jit(solution)/shard_map/ppermute | solution.py:202
  55.9 0.6 collective-permute-start.14
  56.5 1.8 %collective-permute-done.12.refs_5_ = bf16[152,768]{1,0:T(8,128)(2,1)S(1)} collective-permute-done((bf16[152,768]{1,0:T(8,128)(2,1)S(1)}, bf16[152,768]{1,0:T(8,128)(2,1)S(1)}, u32[]{:S(2)}, u32[]{:S(2)}) %collective-permute-start.12) | collective-permute-done | bytes 233504 | tf_op jit(solution)/shard_map/ppermute | solution.py:202
  58.3 0.4 change.6
  58.7 2.7 %collective-permute-start.16 = (bf16[152,768]{1,0:T(8,128)(2,1)S(1)}, bf16[152,768]{1,0:T(8,128)(2,1)S(1)}, u32[]{:S(2)}, u32[]{:S(2)}) collective-permute-start(bf16[152,768]{1,0:T(8,128)(2,1)S(1)} %get-tuple-element.67.refs_3_.refs_6_), channel_id=1, source_target_pairs={{4,8},{12,16},{20,24},{28,0},{8,4},{16,12},{24,20},{0,28},{5,9},{1... | collective-permute-start | bytes 700424 | tf_op jit(solution)/shard_map/ppermute | solution.py:34
  61.5 1.0 %collective-permute-done.15.refs_5_ = bf16[152,640]{1,0:T(8,128)(2,1)S(1)} collective-permute-done((bf16[152,640]{1,0:T(8,128)(2,1)S(1)}, bf16[152,640]{1,0:T(8,128)(2,1)S(1)}, u32[]{:S(2)}, u32[]{:S(2)}) %collective-permute-start.15) | collective-permute-done | bytes 194592 | tf_op jit(solution)/shard_map/ppermute | solution.py:202
  62.5 0.4 change.7
  62.9 2.7 %collective-permute-start.17 = (bf16[152,640]{1,0:T(8,128)(2,1)S(1)}, bf16[152,640]{1,0:T(8,128)(2,1)S(1)}, u32[]{:S(2)}, u32[]{:S(2)}) collective-permute-start(bf16[152,640]{1,0:T(8,128)(2,1)S(1)} %get-tuple-element.72), channel_id=1, source_target_pairs={{4,8},{12,16},{20,24},{28,0},{8,4},{16,12},{24,20},{0,28},{5,9},{1... | collective-permute-start | bytes 583688 | tf_op jit(solution)/shard_map/ppermute | solution.py:34
  65.5 0.1 join.1.refs_3_
  65.8 2.3 %collective-permute-done.16.refs_2_ = bf16[152,768]{1,0:T(8,128)(2,1)S(1)} collective-permute-done((bf16[152,768]{1,0:T(8,128)(2,1)S(1)}, bf16[152,768]{1,0:T(8,128)(2,1)S(1)}, u32[]{:S(2)}, u32[]{:S(2)}) %collective-permute-start.16) | collective-permute-done | bytes 233504 | tf_op jit(solution)/shard_map/ppermute | solution.py:34
  68.1 0.1 across.6.refs_4_.refs_2_
  68.2 4.1 %collective-permute-done.17.refs_2_ = bf16[152,640]{1,0:T(8,128)(2,1)S(1)} collective-permute-done((bf16[152,640]{1,0:T(8,128)(2,1)S(1)}, bf16[152,640]{1,0:T(8,128)(2,1)S(1)}, u32[]{:S(2)}, u32[]{:S(2)}) %collective-permute-start.17) | collective-permute-done | bytes 194592 | tf_op jit(solution)/shard_map/ppermute | solution.py:34
  72.4 1.3 %finish.1 = f32[3,152,896]{2,1,0:T(8,128)} custom-call(f32[152,640]{1,0:T(8,128)S(1)} %across.4.refs_7_.refs_4_.refs_0_, f32[152,640]{1,0:T(8,128)S(1)} %across.5.refs_4_.refs_1_, f32[152,768]{1,0:T(8,128)S(1)} %across.6.refs_4_.refs_2_, f32[152,640]{1,0:T(8,128)S(1)} %across.7.refs_3_, f32[152,2688]{1,0:T(8,128)S(1)} %collective-permute-done.18.refs_4_), custom_call_target="tpu_custom_call" | custom-call | tf_op jit(solution)/shard_map/finish/pallas_call | solution.py:424
  (29 shorter events, 0.4 us)
Async XLA Ops:
  0.0 15.9 %collective-permute-start.3 = (bf16[256,896]{1,0:T(8,128)(2,1)}, bf16[256,896]{1,0:T(8,128)(2,1)S(1)}, u32[]{:S(2)}, u32[]{:S(2)}) collective-permute-start(bf16[256,896]{1,0:T(8,128)(2,1)} %refs_0_.3), channel_id=1, source_target_pairs={{1,2},{2,1},{5,6},{6,5},{9,10},{10,9},{13,14},{14,13},{17,18},{18,... | collective-permute-start | bytes 1376264 | tf_op jit(solution)/shard_map/ppermute | solution.py:202
  0.7 18.7 %collective-permute-start = (bf16[256,896]{1,0:T(8,128)(2,1)}, bf16[256,896]{1,0:T(8,128)(2,1)S(1)}, u32[]{:S(2)}, u32[]{:S(2)}) collective-permute-start(bf16[256,896]{1,0:T(8,128)(2,1)} %refs_0_.3), channel_id=1, source_target_pairs={{0,1},{1,0},{2,3},{3,2},{4,5},{5,4},{6,7},{7,6},{8,9},{9,8},{10,11... | collective-permute-start | bytes 1376264 | tf_op jit(solution)/shard_map/ppermute | solution.py:202
  6.6 23.6 %collective-permute-start.5 = (bf16[256,896]{1,0:T(8,128)(2,1)}, bf16[256,896]{1,0:T(8,128)(2,1)S(1)}, u32[]{:S(2)}, u32[]{:S(2)}) collective-permute-start(bf16[256,896]{1,0:T(8,128)(2,1)} %refs_3_.1), channel_id=1, source_target_pairs={{1,2},{2,1},{5,6},{6,5},{9,10},{10,9},{13,14},{14,13},{17,18},{18,... | collective-permute-start | bytes 1376264 | tf_op jit(solution)/shard_map/ppermute | solution.py:202
  7.3 1.1 %copy-start = (bf16[1,152,3,896]{3,1,2,0:T(8,128)(2,1)S(1)}, bf16[1,152,3,896]{3,1,2,0:T(8,128)(2,1)}, u32[]{:S(2)}) copy-start(bf16[1,152,3,896]{3,1,2,0:T(8,128)(2,1)} %param.7) | copy-start | bytes 2451460
  8.4 1.1 %copy-start.2 = (bf16[1,152,3,896]{3,1,2,0:T(8,128)(2,1)S(1)}, bf16[1,152,3,896]{3,1,2,0:T(8,128)(2,1)}, u32[]{:S(2)}) copy-start(bf16[1,152,3,896]{3,1,2,0:T(8,128)(2,1)} %param.8) | copy-start | bytes 2451460
  9.5 1.1 %copy-start.4 = (bf16[1,152,3,896]{3,1,2,0:T(8,128)(2,1)S(1)}, bf16[1,152,3,896]{3,1,2,0:T(8,128)(2,1)}, u32[]{:S(2)}) copy-start(bf16[1,152,3,896]{3,1,2,0:T(8,128)(2,1)} %param.9) | copy-start | bytes 2451460
  10.7 1.0 %copy-start.6 = (bf16[256,896]{1,0:T(8,128)(2,1)S(1)}, bf16[256,896]{1,0:T(8,128)(2,1)}, u32[]{:S(2)}) copy-start(bf16[256,896]{1,0:T(8,128)(2,1)} %refs_3_.1) | copy-start | bytes 1376260
  11.7 4.2 %copy-start.8 = (bf16[256,896]{1,0:T(8,128)(2,1)S(1)}, bf16[256,896]{1,0:T(8,128)(2,1)}, u32[]{:S(2)}) copy-start(bf16[256,896]{1,0:T(8,128)(2,1)} %refs_0_.3) | copy-start | bytes 1376260
  13.1 14.9 %collective-permute-start.2 = (bf16[256,896]{1,0:T(8,128)(2,1)S(1)}, bf16[256,896]{1,0:T(8,128)(2,1)S(1)}, u32[]{:S(2)}, u32[]{:S(2)}) collective-permute-start(bf16[256,896]{1,0:T(8,128)(2,1)S(1)} %get-tuple-element.39), channel_id=1, source_target_pairs={{0,1},{1,0},{2,3},{3,2},{4,5},{5,4},{6,7},{7,6},{8,9},{9,8},{10,11... | collective-permute-start | bytes 1376264 | tf_op jit(solution)/shard_map/ppermute | solution.py:202
  14.9 38.8 %collective-permute-start.10 = (f32[3,152,896]{2,1,0:T(8,128)S(1)}, f32[3,152,896]{2,1,0:T(8,128)S(1)}, u32[]{:S(2)}, u32[]{:S(2)}) collective-permute-start(f32[3,152,896]{2,1,0:T(8,128)S(1)} %get-tuple-element.40.refs_3_.refs_1_), channel_id=1, source_target_pairs={{4,8},{12,16},{20,24},{28,0},{8,4},{16,12},{24,20},{0,28},{5,9},{1... | collective-permute-start | bytes 4902920 | tf_op jit(solution)/shard_map/ppermute | solution.py:34
  16.8 22.9 %collective-permute-start.8 = (bf16[2,152,896]{2,1,0:T(8,128)(2,1)S(1)}, bf16[2,152,896]{2,1,0:T(8,128)(2,1)S(1)}, u32[]{:S(2)}, u32[]{:S(2)}) collective-permute-start(bf16[2,152,896]{2,1,0:T(8,128)(2,1)S(1)} %get-tuple-element.53), channel_id=1, source_target_pairs={{0,1},{1,0},{2,3},{3,2},{4,5},{5,4},{6,7},{7,6},{8,9},{9,8},{10,11... | collective-permute-start | bytes 1634312 | tf_op jit(solution)/shard_map/ppermute | solution.py:202
  19.4 13.3 %collective-permute-start.1 = (bf16[256,896]{1,0:T(8,128)(2,1)S(1)}, bf16[256,896]{1,0:T(8,128)(2,1)S(1)}, u32[]{:S(2)}, u32[]{:S(2)}) collective-permute-start(bf16[256,896]{1,0:T(8,128)(2,1)S(1)} %collective-permute-done.refs_0_.refs_2_), channel_id=1, source_target_pairs={{1,2},{2,1},{5,6},{6,5},{9,10},{10,9},{13,14},{14,13},{17,18},{18,... | collective-permute-start | bytes 1376264 | tf_op jit(solution)/shard_map/ppermute | solution.py:202
  20.6 10.2 %copy-start.7 = (bf16[256,896]{1,0:T(8,128)(2,1)S(1)}, bf16[256,896]{1,0:T(8,128)(2,1)}, u32[]{:S(2)}) copy-start(bf16[256,896]{1,0:T(8,128)(2,1)} %refs_3_.1) | copy-start | bytes 1376260
  28.0 17.5 %collective-permute-start.7 = (bf16[152,896]{1,0:T(8,128)(2,1)S(1)}, bf16[152,896]{1,0:T(8,128)(2,1)S(1)}, u32[]{:S(2)}, u32[]{:S(2)}) collective-permute-start(bf16[152,896]{1,0:T(8,128)(2,1)S(1)} %get-tuple-element.52), channel_id=1, source_target_pairs={{0,1},{1,0},{2,3},{3,2},{4,5},{5,4},{6,7},{7,6},{8,9},{9,8},{10,11... | collective-permute-start | bytes 817160 | tf_op jit(solution)/shard_map/ppermute | solution.py:202
  30.2 10.3 %collective-permute-start.4 = (bf16[256,640]{1,0:T(8,128)(2,1)S(1)}, bf16[256,640]{1,0:T(8,128)(2,1)S(1)}, u32[]{:S(2)}, u32[]{:S(2)}) collective-permute-start(bf16[256,640]{1,0:T(8,128)(2,1)S(1)} %get-tuple-element.43.refs_13_), channel_id=1, source_target_pairs={{1,2},{2,1},{5,6},{6,5},{9,10},{10,9},{13,14},{14,13},{17,18},{18,... | collective-permute-start | bytes 983048 | tf_op jit(solution)/shard_map/ppermute | solution.py:202
  33.2 12.7 %collective-permute-start.6 = (bf16[256,256]{1,0:T(8,128)(2,1)S(1)}, bf16[256,256]{1,0:T(8,128)(2,1)S(1)}, u32[]{:S(2)}, u32[]{:S(2)}) collective-permute-start(bf16[256,256]{1,0:T(8,128)(2,1)S(1)} %get-tuple-element.48.refs_3_), channel_id=1, source_target_pairs={{1,2},{2,1},{5,6},{6,5},{9,10},{10,9},{13,14},{14,13},{17,18},{18,... | collective-permute-start | bytes 393224 | tf_op jit(solution)/shard_map/ppermute | solution.py:202
  40.5 5.4 %copy-start.1 = (bf16[1,152,3,896]{3,1,2,0:T(8,128)(2,1)S(1)}, bf16[1,152,3,896]{3,1,2,0:T(8,128)(2,1)}, u32[]{:S(2)}) copy-start(bf16[1,152,3,896]{3,1,2,0:T(8,128)(2,1)} %param.7) | copy-start | bytes 2451460
  40.8 8.9 %collective-permute-start.9 = (bf16[152,640]{1,0:T(8,128)(2,1)S(1)}, bf16[152,640]{1,0:T(8,128)(2,1)S(1)}, u32[]{:S(2)}, u32[]{:S(2)}) collective-permute-start(bf16[152,640]{1,0:T(8,128)(2,1)S(1)} %pair_first.1.refs_4_), channel_id=1, source_target_pairs={{0,1},{1,0},{2,3},{3,2},{4,5},{5,4},{6,7},{7,6},{8,9},{9,8},{10,11... | collective-permute-start | bytes 583688 | tf_op jit(solution)/shard_map/ppermute | solution.py:202
  46.8 2.8 %copy-start.3 = (bf16[1,152,3,896]{3,1,2,0:T(8,128)(2,1)S(1)}, bf16[1,152,3,896]{3,1,2,0:T(8,128)(2,1)}, u32[]{:S(2)}) copy-start(bf16[1,152,3,896]{3,1,2,0:T(8,128)(2,1)} %param.8) | copy-start | bytes 2451460
  46.9 2.8 %copy-start.5 = (bf16[1,152,3,896]{3,1,2,0:T(8,128)(2,1)S(1)}, bf16[1,152,3,896]{3,1,2,0:T(8,128)(2,1)}, u32[]{:S(2)}) copy-start(bf16[1,152,3,896]{3,1,2,0:T(8,128)(2,1)} %param.9) | copy-start | bytes 2451460
  47.8 5.7 %collective-permute-start.13 = (bf16[152,640]{1,0:T(8,128)(2,1)S(1)}, bf16[152,640]{1,0:T(8,128)(2,1)S(1)}, u32[]{:S(2)}, u32[]{:S(2)}) collective-permute-start(bf16[152,640]{1,0:T(8,128)(2,1)S(1)} %get-tuple-element.64), channel_id=1, source_target_pairs={{0,1},{1,0},{2,3},{3,2},{4,5},{5,4},{6,7},{7,6},{8,9},{9,8},{10,11... | collective-permute-start | bytes 583688 | tf_op jit(solution)/shard_map/ppermute | solution.py:202
  50.1 11.3 %collective-permute-start.11 = (bf16[152,640]{1,0:T(8,128)(2,1)S(1)}, bf16[152,640]{1,0:T(8,128)(2,1)S(1)}, u32[]{:S(2)}, u32[]{:S(2)}) collective-permute-start(bf16[152,640]{1,0:T(8,128)(2,1)S(1)} %get-tuple-element.62.refs_7_), channel_id=1, source_target_pairs={{4,8},{12,16},{20,24},{28,0},{8,4},{16,12},{24,20},{0,28},{5,9},{1... | collective-permute-start | bytes 583688 | tf_op jit(solution)/shard_map/ppermute | solution.py:34
  50.2 8.1 %collective-permute-start.12 = (bf16[152,768]{1,0:T(8,128)(2,1)S(1)}, bf16[152,768]{1,0:T(8,128)(2,1)S(1)}, u32[]{:S(2)}, u32[]{:S(2)}) collective-permute-start(bf16[152,768]{1,0:T(8,128)(2,1)S(1)} %get-tuple-element.63), channel_id=1, source_target_pairs={{0,1},{1,0},{2,3},{3,2},{4,5},{5,4},{6,7},{7,6},{8,9},{9,8},{10,11... | collective-permute-start | bytes 700424 | tf_op jit(solution)/shard_map/ppermute | solution.py:202
  54.1 8.4 %collective-permute-start.15 = (bf16[152,640]{1,0:T(8,128)(2,1)S(1)}, bf16[152,640]{1,0:T(8,128)(2,1)S(1)}, u32[]{:S(2)}, u32[]{:S(2)}) collective-permute-start(bf16[152,640]{1,0:T(8,128)(2,1)S(1)} %get-tuple-element.70), channel_id=1, source_target_pairs={{0,1},{1,0},{2,3},{3,2},{4,5},{5,4},{6,7},{7,6},{8,9},{9,8},{10,11... | collective-permute-start | bytes 583688 | tf_op jit(solution)/shard_map/ppermute | solution.py:202
  55.9 9.9 %collective-permute-start.14 = (bf16[152,640]{1,0:T(8,128)(2,1)S(1)}, bf16[152,640]{1,0:T(8,128)(2,1)S(1)}, u32[]{:S(2)}, u32[]{:S(2)}) collective-permute-start(bf16[152,640]{1,0:T(8,128)(2,1)S(1)} %get-tuple-element.66.refs_6_), channel_id=1, source_target_pairs={{4,8},{12,16},{20,24},{28,0},{8,4},{16,12},{24,20},{0,28},{5,9},{1... | collective-permute-start | bytes 583688 | tf_op jit(solution)/shard_map/ppermute | solution.py:34
  58.7 9.4 %collective-permute-start.16 = (bf16[152,768]{1,0:T(8,128)(2,1)S(1)}, bf16[152,768]{1,0:T(8,128)(2,1)S(1)}, u32[]{:S(2)}, u32[]{:S(2)}) collective-permute-start(bf16[152,768]{1,0:T(8,128)(2,1)S(1)} %get-tuple-element.67.refs_3_.refs_6_), channel_id=1, source_target_pairs={{4,8},{12,16},{20,24},{28,0},{8,4},{16,12},{24,20},{0,28},{5,9},{1... | collective-permute-start | bytes 700424 | tf_op jit(solution)/shard_map/ppermute | solution.py:34
  62.9 9.4 %collective-permute-start.17 = (bf16[152,640]{1,0:T(8,128)(2,1)S(1)}, bf16[152,640]{1,0:T(8,128)(2,1)S(1)}, u32[]{:S(2)}, u32[]{:S(2)}) collective-permute-start(bf16[152,640]{1,0:T(8,128)(2,1)S(1)} %get-tuple-element.72), channel_id=1, source_target_pairs={{4,8},{12,16},{20,24},{28,0},{8,4},{16,12},{24,20},{0,28},{5,9},{1... | collective-permute-start | bytes 583688 | tf_op jit(solution)/shard_map/ppermute | solution.py:34
  65.7 6.7 %collective-permute-start.18 = (f32[152,2688]{1,0:T(8,128)S(1)}, f32[152,2688]{1,0:T(8,128)S(1)}, u32[]{:S(2)}, u32[]{:S(2)}) collective-permute-start(f32[152,2688]{1,0:T(8,128)S(1)} %join.1.refs_3_), channel_id=1, source_target_pairs={{0,4},{8,12},{16,20},{24,28},{4,0},{12,8},{20,16},{28,24},{1,5},{9... | collective-permute-start | bytes 4902920 | tf_op jit(solution)/shard_map/ppermute | solution.py:34

commit v7 on v6

--- a/solution.py
+++ b/solution.py
@@ -19,7 +19,7 @@
 NEAR_WORK = 5_000_000_000
 PAIR_WORK = 20_000_000_000
 AHEAD_WORK = 20_000_000_000
-ACROSS_WORK = (20_000_000_000, 2_000_000_000, 2_000_000_000, 30_000_000_000)
+ACROSS_WORK = (20_000_000_000, 2_000_000_000, 60_000_000_000, 30_000_000_000)
 FAR_WORK = 0
 CHANGE_WORK = (0, 5_000_000_000, 5_000_000_000, 0)
 
@@ -396,8 +396,11 @@
     )[0]
 
 
-def finish_kernel(*refs, pieces, bands):
-    *parts, near, out, total, done = refs
+def finish_kernel(*refs, pieces, bands, last):
+    parts, near, (total, done) = refs[: len(pieces)], refs[len(pieces)], refs[-2:]
+    out = refs[-3 if last else -4]
+    if not last:
+        refs[-3][...] = jnp.zeros_like(refs[-3])
     units = near.shape[0]
     copies, start = [], 0
     for part, piece in zip(parts, pieces):
@@ -417,15 +420,17 @@
         copy.wait()
 
 
-def finish(pieces, parts, near, shape):
+def finish(pieces, parts, near, shape, held=None):
     units = shape[1]
     bands = (0, units // 32 * 16)
-    vmem = pl.BlockSpec(memory_space=pltpu.VMEM)
+    vmem, anywhere = pl.BlockSpec(memory_space=pltpu.VMEM), pl.BlockSpec(memory_space=pl.ANY)
+    held = () if held is None else (held,)
     return pl.pallas_call(
-        functools.partial(finish_kernel, pieces=pieces, bands=bands),
-        out_shape=array(shape, FULL),
-        in_specs=[vmem] * (len(parts) + 1),
-        out_specs=pl.BlockSpec(memory_space=pl.ANY),
+        functools.partial(finish_kernel, pieces=pieces, bands=bands, last=bool(held)),
+        out_shape=[array(shape, FULL)] + [array((8, 128), FULL)] * (not held),
+        in_specs=[vmem] * (len(parts) + 1) + [anywhere] * len(held),
+        out_specs=[anywhere] + [vmem] * (not held),
+        input_output_aliases={len(parts) + 1: 0} if held else {},
         scratch_shapes=[
             pltpu.VMEM(near.shape, FULL),
             pltpu.SemaphoreType.DMA((2 * sum(len(v) for v in pieces),)),
@@ -433,7 +438,7 @@
         cost_estimate=pl.CostEstimate(flops=0, bytes_accessed=0, transcendentals=0),
         compiler_params=pltpu.CompilerParams(vmem_limit_bytes=32 * 2**20),
         name="finish",
-    )(*parts, near)
+    )(*parts, near, *held)
 
 
 def on_device(tokens, cotangent, weights, first_moment, second_moment):
@@ -477,13 +482,19 @@
             totals = [across_of(0, changes[0], still_far, last)]
             last += (totals[0],)
     updates = [v for _, v, _ in changes]
-    joint = call(
-        join_kernel, [array((rows.shape[1], 3 * width), FULL)], updates, name="join"
+    early = call(
+        join_kernel,
+        [array((rows.shape[1], 3 * width - updates[-1].shape[1]), FULL)],
+        updates[:-1],
+        name="join",
     )[0]
-    near = neighbour(joint, 0)
-    for i in range(1, count):
-        totals.append(across_of(i, changes[i], still_far, (joint, totals[-1])))
-    out = finish([v for v, _, _ in changes], totals, near, rows.shape)
+    early_near, late_near = neighbour(early, 0), neighbour(updates[-1], 0)
+    for i in range(1, count - 1):
+        totals.append(across_of(i, changes[i], still_far, (early, totals[-1])))
+    places = [v for v, _, _ in changes]
+    out, ended = finish(places[:-1], totals, early_near, rows.shape)
+    totals.append(across_of(count - 1, changes[-1], still_far, (ended,)))
+    (out,) = finish(places[-1:], totals[-1:], late_near, rows.shape, out)
     return jnp.swapaxes(out, 0, 1)[None]
 
 

time: 74 us -> 73.5 us (level)
  waiting for transfers between devices: 24.3 us -> 23.2 us
    ppermute x6 -> x7, waiting for transfers between devices: 6.54 us -> 5.56 us  [neighbour(): return lax.ppermute(block, 'blk', route)]
    pallas_call x1 -> x2, Pallas kernels: 1.28 us -> 1.92 us  [finish(): pl.pallas_call(functools.partial(finish_kernel, pieces=pieces, bands=band...]
    ppermute x6 -> x7, starting transfers between devices: 7.2 us -> 7.2 us  [neighbour(): return lax.ppermute(block, 'blk', route)]
  transfers between devices with their start and end apart: 19 -> 20, of which waited for: 9 -> 9; matrix products, arithmetic and copies ran while one was open for 0% -> 0% of each run, Pallas kernels for 14% -> 16%
where the time goes in v7:
time: 73.5 us; the launch traced here: 73.1 us
  starting transfers between devices  33 us (45%)
  waiting for transfers between devices  23.2 us (32%)
  Pallas kernels  12.3 us (17%)
  local copies, waits for them, and re-layouts  4.47 us (6%)
    ppermute x13, starting transfers between devices, send(): return lax.ppermute(block, 'tp', route)  25.8 us
    ppermute x13, waiting for transfers between devices, send(): return lax.ppermute(block, 'tp', route)  17.6 us
    pallas_call x19, Pallas kernels, call(): pl.pallas_call(body, out_shape=outs, in_specs=[pl.BlockSpec(memory_space=...  8.96 us
    ppermute x7, starting transfers between devices, neighbour(): return lax.ppermute(block, 'blk', route)  7.2 us
    ppermute x7, waiting for transfers between devices, neighbour(): return lax.ppermute(block, 'blk', route)  5.56 us
    unnamed x18, local copies, waits for them, and re-layouts  4.47 us
    pallas_call x2, Pallas kernels, finish(): pl.pallas_call(functools.partial(finish_kernel, pieces=pieces, bands=band...  1.92 us
  transfers between devices with their start and end apart: 20, of which 9 were waited for; matrix products, arithmetic and copies ran while one was open for 0% of the time, Pallas kernels for 16%

profile of v7, /device:TPU:0, one launch (start us, length us, event | category | flops | bytes accessed | tf_op | source)
XLA Modules:
  0.0 73.1 jit_solution(105765371422032750)
XLA Ops:
  0.0 0.7 collective-permute-start.3
  0.7 5.9 %collective-permute-start = (bf16[256,896]{1,0:T(8,128)(2,1)}, bf16[256,896]{1,0:T(8,128)(2,1)S(1)}, u32[]{:S(2)}, u32[]{:S(2)}) collective-permute-start(bf16[256,896]{1,0:T(8,128)(2,1)} %refs_0_.3), channel_id=1, source_target_pairs={{0,1},{1,0},{2,3},{3,2},{4,5},{5,4},{6,7},{7,6},{8,9},{9,8},{10,11... | collective-permute-start | bytes 1376264 | tf_op jit(solution)/shard_map/ppermute | solution.py:202
  6.6 0.7 collective-permute-start.5
  7.3 1.1 %copy-done = bf16[1,152,3,896]{3,1,2,0:T(8,128)(2,1)S(1)} copy-done((bf16[1,152,3,896]{3,1,2,0:T(8,128)(2,1)S(1)}, bf16[1,152,3,896]{3,1,2,0:T(8,128)(2,1)}, u32[]{:S(2)}) %copy-start) | copy-done | bytes 817176
  8.4 1.1 %copy-done.2 = bf16[1,152,3,896]{3,1,2,0:T(8,128)(2,1)S(1)} copy-done((bf16[1,152,3,896]{3,1,2,0:T(8,128)(2,1)S(1)}, bf16[1,152,3,896]{3,1,2,0:T(8,128)(2,1)}, u32[]{:S(2)}) %copy-start.2) | copy-done | bytes 817176
  9.5 1.1 %copy-done.4 = bf16[1,152,3,896]{3,1,2,0:T(8,128)(2,1)S(1)} copy-done((bf16[1,152,3,896]{3,1,2,0:T(8,128)(2,1)S(1)}, bf16[1,152,3,896]{3,1,2,0:T(8,128)(2,1)}, u32[]{:S(2)}) %copy-start.4) | copy-done | bytes 817176
  10.7 1.0 %copy-done.6 = bf16[256,896]{1,0:T(8,128)(2,1)S(1)} copy-done((bf16[256,896]{1,0:T(8,128)(2,1)S(1)}, bf16[256,896]{1,0:T(8,128)(2,1)}, u32[]{:S(2)}) %copy-start.6) | copy-done | bytes 458776
  11.7 1.4 %still.1 = (f32[3,152,896]{2,1,0:T(8,128)S(1)}, f32[3,152,896]{2,1,0:T(8,128)S(1)}, bf16[256,896]{1,0:T(8,128)(2,1)S(1)}) custom-call(bf16[3,152,896]{2,1,0:T(8,128)(2,1)S(1)} %bitcast.12, bf16[3,152,896]{2,1,0:T(8,128)(2,1)S(1)} %bitcast.19, bf16[3,152,896]{2,1,0:T(8,128)(2,1)S(1)} %bitcast.24, bf16[256,896]{1,0:T(8,128)(2,1)S(1)} %copy-done.6), custom_call_target="tpu_custom_call" | custom-call | tf_op jit(solution)/shard_map/still/pallas_call | solution.py:324
  13.1 1.8 %collective-permute-start.2 = (bf16[256,896]{1,0:T(8,128)(2,1)S(1)}, bf16[256,896]{1,0:T(8,128)(2,1)S(1)}, u32[]{:S(2)}, u32[]{:S(2)}) collective-permute-start(bf16[256,896]{1,0:T(8,128)(2,1)S(1)} %get-tuple-element.41), channel_id=1, source_target_pairs={{0,1},{1,0},{2,3},{3,2},{4,5},{5,4},{6,7},{7,6},{8,9},{9,8},{10,11... | collective-permute-start | bytes 1376264 | tf_op jit(solution)/shard_map/ppermute | solution.py:202
  14.9 1.0 %collective-permute-start.11 = (f32[3,152,896]{2,1,0:T(8,128)S(1)}, f32[3,152,896]{2,1,0:T(8,128)S(1)}, u32[]{:S(2)}, u32[]{:S(2)}) collective-permute-start(f32[3,152,896]{2,1,0:T(8,128)S(1)} %get-tuple-element.42.refs_3_.refs_1_), channel_id=1, source_target_pairs={{4,8},{12,16},{20,24},{28,0},{8,4},{16,12},{24,20},{0,28},{5,9},{1... | collective-permute-start | bytes 4902920 | tf_op jit(solution)/shard_map/ppermute | solution.py:34
  15.9 0.8 %near_forward.1 = (bf16[152,512]{1,0:T(8,128)(2,1)S(1)}, f32[152,512]{1,0:T(8,128)S(1)}, f32[152,512]{1,0:T(8,128)S(1)}, bf16[2,152,896]{2,1,0:T(8,128)(2,1)S(1)}) custom-call(bf16[256,896]{1,0:T(8,128)(2,1)S(1)} %copy-done.8, bf16[256,896]{1,0:T(8,128)(2,1)S(1)} %collective-permute-done.3.refs_1_.refs_0_, bf16[3,152,896]{2,1,0:T(8,128)(2,1)S(1)} %bitcast.13, ...), custom_call_target="tpu_custom_call" | custom-call | flops 5000000000 | tf_op jit(solution)/shard_map/near_forward/pallas_call | solution.py:82
  16.8 2.7 %collective-permute-start.8 = (bf16[2,152,896]{2,1,0:T(8,128)(2,1)S(1)}, bf16[2,152,896]{2,1,0:T(8,128)(2,1)S(1)}, u32[]{:S(2)}, u32[]{:S(2)}) collective-permute-start(bf16[2,152,896]{2,1,0:T(8,128)(2,1)S(1)} %get-tuple-element.55), channel_id=1, source_target_pairs={{0,1},{1,0},{2,3},{3,2},{4,5},{5,4},{6,7},{7,6},{8,9},{9,8},{10,11... | collective-permute-start | bytes 1634312 | tf_op jit(solution)/shard_map/ppermute | solution.py:202
  19.4 0.7 collective-permute-start.1
  20.1 0.5 pair_forward.1
  20.6 7.4 %collective-permute-done.2.refs_0_.refs_5_.refs_2_ = bf16[256,896]{1,0:T(8,128)(2,1)S(1)} collective-permute-done((bf16[256,896]{1,0:T(8,128)(2,1)S(1)}, bf16[256,896]{1,0:T(8,128)(2,1)S(1)}, u32[]{:S(2)}, u32[]{:S(2)}) %collective-permute-start.2) | collective-permute-done | bytes 458784 | tf_op jit(solution)/shard_map/ppermute | solution.py:202
  28.0 2.1 %collective-permute-start.7 = (bf16[152,896]{1,0:T(8,128)(2,1)S(1)}, bf16[152,896]{1,0:T(8,128)(2,1)S(1)}, u32[]{:S(2)}, u32[]{:S(2)}) collective-permute-start(bf16[152,896]{1,0:T(8,128)(2,1)S(1)} %get-tuple-element.54), channel_id=1, source_target_pairs={{0,1},{1,0},{2,3},{3,2},{4,5},{5,4},{6,7},{7,6},{8,9},{9,8},{10,11... | collective-permute-start | bytes 817160 | tf_op jit(solution)/shard_map/ppermute | solution.py:202
  30.2 0.7 collective-permute-start.4
  30.9 1.8 %near_backward.1.refs_3_.refs_7_ = f32[3,152,896]{2,1,0:T(8,128)S(1)} custom-call(bf16[256,896]{1,0:T(8,128)(2,1)S(1)} %copy-done.8, bf16[256,896]{1,0:T(8,128)(2,1)S(1)} %collective-permute-done.3.refs_1_.refs_0_, bf16[256,896]{1,0:T(8,128)(2,1)S(1)} %collective-permute-done.refs_0_.refs_2_, bf16[256,896]{1,0:T(8,128)(2,1)S(1)} %copy-done.7, ...), custom_call_target="tpu_custom_call" | custom-call | tf_op jit(solution)/shard_map/near_backward/pallas_call | solution.py:82
  32.7 0.5 far_forward.1
  33.2 0.7 collective-permute-start.6
  33.9 5.8 %collective-permute-done.8.refs_2_ = bf16[2,152,896]{2,1,0:T(8,128)(2,1)S(1)} collective-permute-done((bf16[2,152,896]{2,1,0:T(8,128)(2,1)S(1)}, bf16[2,152,896]{2,1,0:T(8,128)(2,1)S(1)}, u32[]{:S(2)}, u32[]{:S(2)}) %collective-permute-start.8) | collective-permute-done | bytes 544800 | tf_op jit(solution)/shard_map/ppermute | solution.py:202
  39.7 0.8 %ahead_forward.1 = (bf16[152,512]{1,0:T(8,128)(2,1)S(1)}, f32[152,512]{1,0:T(8,128)S(1)}, f32[152,512]{1,0:T(8,128)S(1)}) custom-call(bf16[256,896]{1,0:T(8,128)(2,1)S(1)} %collective-permute-done.3.refs_1_.refs_0_, bf16[256,896]{1,0:T(8,128)(2,1)S(1)} %collective-permute-done.1.refs_0_.refs_1_, bf16[2,152,896]{2,1,0:T(8,128)(2,1)S(1)} %collective-permute-done.8.refs_2_, ...), custom_call_target="tpu_custom_call" | custom-call | flops 20000000000 | tf_op jit(solution)/shard_map/ahead_forward/pallas_call | solution.py:82
  40.5 0.3 pair_first.1.refs_4_
  40.8 4.8 %collective-permute-start.10 = (bf16[152,640]{1,0:T(8,128)(2,1)S(1)}, bf16[152,640]{1,0:T(8,128)(2,1)S(1)}, u32[]{:S(2)}, u32[]{:S(2)}) collective-permute-start(bf16[152,640]{1,0:T(8,128)(2,1)S(1)} %pair_first.1.refs_4_), channel_id=1, source_target_pairs={{0,1},{1,0},{2,3},{3,2},{4,5},{5,4},{6,7},{7,6},{8,9},{9,8},{10,11... | collective-permute-start | bytes 583688 | tf_op jit(solution)/shard_map/ppermute | solution.py:202
  45.6 0.3 ahead_backward.1
  45.9 0.9 %far_backward.1.refs_11_.refs_0_ = f32[3,152,896]{2,1,0:T(8,128)S(1)} custom-call(bf16[256,896]{1,0:T(8,128)(2,1)S(1)} %collective-permute-done.1.refs_0_.refs_1_, bf16[256,640]{1,0:T(8,128)(2,1)S(1)} %collective-permute-done.4.refs_2_.refs_1_.refs_3_, bf16[256,256]{1,0:T(8,128)(2,1)S(1)} %collective-permute-done.6.refs_2_.refs_4_, ...), custom_call_target="tpu_custom_call" | custom-call | tf_op jit(solution)/shard_map/far_backward/pallas_call | solution.py:82
  46.9 1.0 %pair_rest.1 = (bf16[152,640]{1,0:T(8,128)(2,1)S(1)}, bf16[152,768]{1,0:T(8,128)(2,1)S(1)}, bf16[152,640]{1,0:T(8,128)(2,1)S(1)}) custom-call(bf16[256,896]{1,0:T(8,128)(2,1)S(1)} %collective-permute-done.3.refs_1_.refs_0_, bf16[256,896]{1,0:T(8,128)(2,1)S(1)} %collective-permute-done.1.refs_0_.refs_1_, ...), custom_call_target="tpu_custom_call" | custom-call | tf_op jit(solution)/shard_map/pair_rest/pallas_call | solution.py:82
  47.8 1.0 %collective-permute-start.9 = (bf16[152,640]{1,0:T(8,128)(2,1)S(1)}, bf16[152,640]{1,0:T(8,128)(2,1)S(1)}, u32[]{:S(2)}, u32[]{:S(2)}) collective-permute-start(bf16[152,640]{1,0:T(8,128)(2,1)S(1)} %get-tuple-element.62), channel_id=1, source_target_pairs={{0,1},{1,0},{2,3},{3,2},{4,5},{5,4},{6,7},{7,6},{8,9},{9,8},{10,11... | collective-permute-start | bytes 583688 | tf_op jit(solution)/shard_map/ppermute | solution.py:202
  48.8 0.8 %collective-permute-done.10.refs_5_ = bf16[152,640]{1,0:T(8,128)(2,1)S(1)} collective-permute-done((bf16[152,640]{1,0:T(8,128)(2,1)S(1)}, bf16[152,640]{1,0:T(8,128)(2,1)S(1)}, u32[]{:S(2)}, u32[]{:S(2)}) %collective-permute-start.10) | collective-permute-done | bytes 194592 | tf_op jit(solution)/shard_map/ppermute | solution.py:202
  49.7 0.4 change.4
  50.2 2.4 %collective-permute-start.13 = (bf16[152,768]{1,0:T(8,128)(2,1)S(1)}, bf16[152,768]{1,0:T(8,128)(2,1)S(1)}, u32[]{:S(2)}, u32[]{:S(2)}) collective-permute-start(bf16[152,768]{1,0:T(8,128)(2,1)S(1)} %get-tuple-element.67), channel_id=1, source_target_pairs={{0,1},{1,0},{2,3},{3,2},{4,5},{5,4},{6,7},{7,6},{8,9},{9,8},{10,11... | collective-permute-start | bytes 700424 | tf_op jit(solution)/shard_map/ppermute | solution.py:202
  52.6 1.0 %collective-permute-done.9.refs_5_ = bf16[152,640]{1,0:T(8,128)(2,1)S(1)} collective-permute-done((bf16[152,640]{1,0:T(8,128)(2,1)S(1)}, bf16[152,640]{1,0:T(8,128)(2,1)S(1)}, u32[]{:S(2)}, u32[]{:S(2)}) %collective-permute-start.9) | collective-permute-done | bytes 194592 | tf_op jit(solution)/shard_map/ppermute | solution.py:202
  53.5 0.1 collective-permute-done.11.refs_8_.refs_1_
  53.7 0.4 change.5
  54.1 1.8 %collective-permute-start.12 = (bf16[152,640]{1,0:T(8,128)(2,1)S(1)}, bf16[152,640]{1,0:T(8,128)(2,1)S(1)}, u32[]{:S(2)}, u32[]{:S(2)}) collective-permute-start(bf16[152,640]{1,0:T(8,128)(2,1)S(1)} %get-tuple-element.66), channel_id=1, source_target_pairs={{0,1},{1,0},{2,3},{3,2},{4,5},{5,4},{6,7},{7,6},{8,9},{9,8},{10,11... | collective-permute-start | bytes 583688 | tf_op jit(solution)/shard_map/ppermute | solution.py:202
  55.9 0.6 collective-permute-start.16
  56.5 1.8 %collective-permute-done.13.refs_5_ = bf16[152,768]{1,0:T(8,128)(2,1)S(1)} collective-permute-done((bf16[152,768]{1,0:T(8,128)(2,1)S(1)}, bf16[152,768]{1,0:T(8,128)(2,1)S(1)}, u32[]{:S(2)}, u32[]{:S(2)}) %collective-permute-start.13) | collective-permute-done | bytes 233504 | tf_op jit(solution)/shard_map/ppermute | solution.py:202
  58.3 0.4 change.6
  58.7 2.7 %collective-permute-start.17 = (bf16[152,768]{1,0:T(8,128)(2,1)S(1)}, bf16[152,768]{1,0:T(8,128)(2,1)S(1)}, u32[]{:S(2)}, u32[]{:S(2)}) collective-permute-start(bf16[152,768]{1,0:T(8,128)(2,1)S(1)} %get-tuple-element.69.refs_3_.refs_6_), channel_id=1, source_target_pairs={{4,8},{12,16},{20,24},{28,0},{8,4},{16,12},{24,20},{0,28},{5,9},{1... | collective-permute-start | bytes 700424 | tf_op jit(solution)/shard_map/ppermute | solution.py:34
  61.4 0.1 join.1.refs_3_
  61.7 0.8 %collective-permute-done.12.refs_5_ = bf16[152,640]{1,0:T(8,128)(2,1)S(1)} collective-permute-done((bf16[152,640]{1,0:T(8,128)(2,1)S(1)}, bf16[152,640]{1,0:T(8,128)(2,1)S(1)}, u32[]{:S(2)}, u32[]{:S(2)}) %collective-permute-start.12) | collective-permute-done | bytes 194592 | tf_op jit(solution)/shard_map/ppermute | solution.py:202
  62.5 0.4 change.7
  62.9 2.7 %collective-permute-start.15 = (bf16[152,640]{1,0:T(8,128)(2,1)S(1)}, bf16[152,640]{1,0:T(8,128)(2,1)S(1)}, u32[]{:S(2)}, u32[]{:S(2)}) collective-permute-start(bf16[152,640]{1,0:T(8,128)(2,1)S(1)} %get-tuple-element.72), channel_id=1, source_target_pairs={{4,8},{12,16},{20,24},{28,0},{8,4},{16,12},{24,20},{0,28},{5,9},{1... | collective-permute-start | bytes 583688 | tf_op jit(solution)/shard_map/ppermute | solution.py:34
  65.6 2.5 %collective-permute-done.17.refs_2_ = bf16[152,768]{1,0:T(8,128)(2,1)S(1)} collective-permute-done((bf16[152,768]{1,0:T(8,128)(2,1)S(1)}, bf16[152,768]{1,0:T(8,128)(2,1)S(1)}, u32[]{:S(2)}, u32[]{:S(2)}) %collective-permute-start.17) | collective-permute-done | bytes 233504 | tf_op jit(solution)/shard_map/ppermute | solution.py:34
  68.1 0.1 across.6.refs_2_
  68.2 1.1 %finish.2 = (f32[3,152,896]{2,1,0:T(8,128)}, f32[8,128]{1,0:T(8,128)S(1)}) custom-call(f32[152,640]{1,0:T(8,128)S(1)} %across.4.refs_7_.refs_4_.refs_0_, f32[152,640]{1,0:T(8,128)S(1)} %across.5.refs_4_.refs_1_, f32[152,768]{1,0:T(8,128)S(1)} %across.6.refs_2_, f32[152,2048]{1,0:T(8,128)S(1)} %collective-permute-done.18.refs_3_), custom_call_target="tpu_custom_call" | custom-call | tf_op jit(solution)/shard_map/finish/pallas_call | solution.py:428
  69.4 2.9 %collective-permute-done.15.refs_2_ = bf16[152,640]{1,0:T(8,128)(2,1)S(1)} collective-permute-done((bf16[152,640]{1,0:T(8,128)(2,1)S(1)}, bf16[152,640]{1,0:T(8,128)(2,1)S(1)}, u32[]{:S(2)}, u32[]{:S(2)}) %collective-permute-start.15) | collective-permute-done | bytes 194592 | tf_op jit(solution)/shard_map/ppermute | solution.py:34
  72.4 0.8 %finish.3 = f32[3,152,896]{2,1,0:T(8,128)} custom-call(f32[152,640]{1,0:T(8,128)S(1)} %across.7.refs_0_, f32[152,640]{1,0:T(8,128)S(1)} %collective-permute-done.19.refs_1_, f32[3,152,896]{2,1,0:T(8,128)} %get-tuple-element.76.refs_2_), custom_call_target="tpu_custom_call", output_to_operand_aliasing={{}: (2, {})} | custom-call | tf_op jit(solution)/shard_map/finish/pallas_call | solution.py:428
  (32 shorter events, 0.5 us)
Async XLA Ops:
  0.0 15.9 %collective-permute-start.3 = (bf16[256,896]{1,0:T(8,128)(2,1)}, bf16[256,896]{1,0:T(8,128)(2,1)S(1)}, u32[]{:S(2)}, u32[]{:S(2)}) collective-permute-start(bf16[256,896]{1,0:T(8,128)(2,1)} %refs_0_.3), channel_id=1, source_target_pairs={{1,2},{2,1},{5,6},{6,5},{9,10},{10,9},{13,14},{14,13},{17,18},{18,... | collective-permute-start | bytes 1376264 | tf_op jit(solution)/shard_map/ppermute | solution.py:202
  0.7 18.7 %collective-permute-start = (bf16[256,896]{1,0:T(8,128)(2,1)}, bf16[256,896]{1,0:T(8,128)(2,1)S(1)}, u32[]{:S(2)}, u32[]{:S(2)}) collective-permute-start(bf16[256,896]{1,0:T(8,128)(2,1)} %refs_0_.3), channel_id=1, source_target_pairs={{0,1},{1,0},{2,3},{3,2},{4,5},{5,4},{6,7},{7,6},{8,9},{9,8},{10,11... | collective-permute-start | bytes 1376264 | tf_op jit(solution)/shard_map/ppermute | solution.py:202
  6.6 23.6 %collective-permute-start.5 = (bf16[256,896]{1,0:T(8,128)(2,1)}, bf16[256,896]{1,0:T(8,128)(2,1)S(1)}, u32[]{:S(2)}, u32[]{:S(2)}) collective-permute-start(bf16[256,896]{1,0:T(8,128)(2,1)} %refs_3_.1), channel_id=1, source_target_pairs={{1,2},{2,1},{5,6},{6,5},{9,10},{10,9},{13,14},{14,13},{17,18},{18,... | collective-permute-start | bytes 1376264 | tf_op jit(solution)/shard_map/ppermute | solution.py:202
  7.3 1.1 %copy-start = (bf16[1,152,3,896]{3,1,2,0:T(8,128)(2,1)S(1)}, bf16[1,152,3,896]{3,1,2,0:T(8,128)(2,1)}, u32[]{:S(2)}) copy-start(bf16[1,152,3,896]{3,1,2,0:T(8,128)(2,1)} %param.7) | copy-start | bytes 2451460
  8.4 1.1 %copy-start.2 = (bf16[1,152,3,896]{3,1,2,0:T(8,128)(2,1)S(1)}, bf16[1,152,3,896]{3,1,2,0:T(8,128)(2,1)}, u32[]{:S(2)}) copy-start(bf16[1,152,3,896]{3,1,2,0:T(8,128)(2,1)} %param.8) | copy-start | bytes 2451460
  9.5 1.1 %copy-start.4 = (bf16[1,152,3,896]{3,1,2,0:T(8,128)(2,1)S(1)}, bf16[1,152,3,896]{3,1,2,0:T(8,128)(2,1)}, u32[]{:S(2)}) copy-start(bf16[1,152,3,896]{3,1,2,0:T(8,128)(2,1)} %param.9) | copy-start | bytes 2451460
  10.7 1.0 %copy-start.6 = (bf16[256,896]{1,0:T(8,128)(2,1)S(1)}, bf16[256,896]{1,0:T(8,128)(2,1)}, u32[]{:S(2)}) copy-start(bf16[256,896]{1,0:T(8,128)(2,1)} %refs_3_.1) | copy-start | bytes 1376260
  11.7 4.2 %copy-start.8 = (bf16[256,896]{1,0:T(8,128)(2,1)S(1)}, bf16[256,896]{1,0:T(8,128)(2,1)}, u32[]{:S(2)}) copy-start(bf16[256,896]{1,0:T(8,128)(2,1)} %refs_0_.3) | copy-start | bytes 1376260
  13.1 14.9 %collective-permute-start.2 = (bf16[256,896]{1,0:T(8,128)(2,1)S(1)}, bf16[256,896]{1,0:T(8,128)(2,1)S(1)}, u32[]{:S(2)}, u32[]{:S(2)}) collective-permute-start(bf16[256,896]{1,0:T(8,128)(2,1)S(1)} %get-tuple-element.41), channel_id=1, source_target_pairs={{0,1},{1,0},{2,3},{3,2},{4,5},{5,4},{6,7},{7,6},{8,9},{9,8},{10,11... | collective-permute-start | bytes 1376264 | tf_op jit(solution)/shard_map/ppermute | solution.py:202
  14.9 38.8 %collective-permute-start.11 = (f32[3,152,896]{2,1,0:T(8,128)S(1)}, f32[3,152,896]{2,1,0:T(8,128)S(1)}, u32[]{:S(2)}, u32[]{:S(2)}) collective-permute-start(f32[3,152,896]{2,1,0:T(8,128)S(1)} %get-tuple-element.42.refs_3_.refs_1_), channel_id=1, source_target_pairs={{4,8},{12,16},{20,24},{28,0},{8,4},{16,12},{24,20},{0,28},{5,9},{1... | collective-permute-start | bytes 4902920 | tf_op jit(solution)/shard_map/ppermute | solution.py:34
  16.8 22.9 %collective-permute-start.8 = (bf16[2,152,896]{2,1,0:T(8,128)(2,1)S(1)}, bf16[2,152,896]{2,1,0:T(8,128)(2,1)S(1)}, u32[]{:S(2)}, u32[]{:S(2)}) collective-permute-start(bf16[2,152,896]{2,1,0:T(8,128)(2,1)S(1)} %get-tuple-element.55), channel_id=1, source_target_pairs={{0,1},{1,0},{2,3},{3,2},{4,5},{5,4},{6,7},{7,6},{8,9},{9,8},{10,11... | collective-permute-start | bytes 1634312 | tf_op jit(solution)/shard_map/ppermute | solution.py:202
  19.4 13.3 %collective-permute-start.1 = (bf16[256,896]{1,0:T(8,128)(2,1)S(1)}, bf16[256,896]{1,0:T(8,128)(2,1)S(1)}, u32[]{:S(2)}, u32[]{:S(2)}) collective-permute-start(bf16[256,896]{1,0:T(8,128)(2,1)S(1)} %collective-permute-done.refs_0_.refs_2_), channel_id=1, source_target_pairs={{1,2},{2,1},{5,6},{6,5},{9,10},{10,9},{13,14},{14,13},{17,18},{18,... | collective-permute-start | bytes 1376264 | tf_op jit(solution)/shard_map/ppermute | solution.py:202
  20.6 10.2 %copy-start.7 = (bf16[256,896]{1,0:T(8,128)(2,1)S(1)}, bf16[256,896]{1,0:T(8,128)(2,1)}, u32[]{:S(2)}) copy-start(bf16[256,896]{1,0:T(8,128)(2,1)} %refs_3_.1) | copy-start | bytes 1376260
  28.0 17.5 %collective-permute-start.7 = (bf16[152,896]{1,0:T(8,128)(2,1)S(1)}, bf16[152,896]{1,0:T(8,128)(2,1)S(1)}, u32[]{:S(2)}, u32[]{:S(2)}) collective-permute-start(bf16[152,896]{1,0:T(8,128)(2,1)S(1)} %get-tuple-element.54), channel_id=1, source_target_pairs={{0,1},{1,0},{2,3},{3,2},{4,5},{5,4},{6,7},{7,6},{8,9},{9,8},{10,11... | collective-permute-start | bytes 817160 | tf_op jit(solution)/shard_map/ppermute | solution.py:202
  30.2 10.3 %collective-permute-start.4 = (bf16[256,640]{1,0:T(8,128)(2,1)S(1)}, bf16[256,640]{1,0:T(8,128)(2,1)S(1)}, u32[]{:S(2)}, u32[]{:S(2)}) collective-permute-start(bf16[256,640]{1,0:T(8,128)(2,1)S(1)} %get-tuple-element.45.refs_13_), channel_id=1, source_target_pairs={{1,2},{2,1},{5,6},{6,5},{9,10},{10,9},{13,14},{14,13},{17,18},{18,... | collective-permute-start | bytes 983048 | tf_op jit(solution)/shard_map/ppermute | solution.py:202
  33.2 12.7 %collective-permute-start.6 = (bf16[256,256]{1,0:T(8,128)(2,1)S(1)}, bf16[256,256]{1,0:T(8,128)(2,1)S(1)}, u32[]{:S(2)}, u32[]{:S(2)}) collective-permute-start(bf16[256,256]{1,0:T(8,128)(2,1)S(1)} %get-tuple-element.50.refs_3_), channel_id=1, source_target_pairs={{1,2},{2,1},{5,6},{6,5},{9,10},{10,9},{13,14},{14,13},{17,18},{18,... | collective-permute-start | bytes 393224 | tf_op jit(solution)/shard_map/ppermute | solution.py:202
  40.5 5.4 %copy-start.1 = (bf16[1,152,3,896]{3,1,2,0:T(8,128)(2,1)S(1)}, bf16[1,152,3,896]{3,1,2,0:T(8,128)(2,1)}, u32[]{:S(2)}) copy-start(bf16[1,152,3,896]{3,1,2,0:T(8,128)(2,1)} %param.7) | copy-start | bytes 2451460
  40.8 8.9 %collective-permute-start.10 = (bf16[152,640]{1,0:T(8,128)(2,1)S(1)}, bf16[152,640]{1,0:T(8,128)(2,1)S(1)}, u32[]{:S(2)}, u32[]{:S(2)}) collective-permute-start(bf16[152,640]{1,0:T(8,128)(2,1)S(1)} %pair_first.1.refs_4_), channel_id=1, source_target_pairs={{0,1},{1,0},{2,3},{3,2},{4,5},{5,4},{6,7},{7,6},{8,9},{9,8},{10,11... | collective-permute-start | bytes 583688 | tf_op jit(solution)/shard_map/ppermute | solution.py:202
  46.8 2.8 %copy-start.3 = (bf16[1,152,3,896]{3,1,2,0:T(8,128)(2,1)S(1)}, bf16[1,152,3,896]{3,1,2,0:T(8,128)(2,1)}, u32[]{:S(2)}) copy-start(bf16[1,152,3,896]{3,1,2,0:T(8,128)(2,1)} %param.8) | copy-start | bytes 2451460
  46.9 2.8 %copy-start.5 = (bf16[1,152,3,896]{3,1,2,0:T(8,128)(2,1)S(1)}, bf16[1,152,3,896]{3,1,2,0:T(8,128)(2,1)}, u32[]{:S(2)}) copy-start(bf16[1,152,3,896]{3,1,2,0:T(8,128)(2,1)} %param.9) | copy-start | bytes 2451460
  47.8 5.7 %collective-permute-start.9 = (bf16[152,640]{1,0:T(8,128)(2,1)S(1)}, bf16[152,640]{1,0:T(8,128)(2,1)S(1)}, u32[]{:S(2)}, u32[]{:S(2)}) collective-permute-start(bf16[152,640]{1,0:T(8,128)(2,1)S(1)} %get-tuple-element.62), channel_id=1, source_target_pairs={{0,1},{1,0},{2,3},{3,2},{4,5},{5,4},{6,7},{7,6},{8,9},{9,8},{10,11... | collective-permute-start | bytes 583688 | tf_op jit(solution)/shard_map/ppermute | solution.py:202
  50.1 11.5 %collective-permute-start.14 = (bf16[152,640]{1,0:T(8,128)(2,1)S(1)}, bf16[152,640]{1,0:T(8,128)(2,1)S(1)}, u32[]{:S(2)}, u32[]{:S(2)}) collective-permute-start(bf16[152,640]{1,0:T(8,128)(2,1)S(1)} %get-tuple-element.65.refs_7_), channel_id=1, source_target_pairs={{4,8},{12,16},{20,24},{28,0},{8,4},{16,12},{24,20},{0,28},{5,9},{1... | collective-permute-start | bytes 583688 | tf_op jit(solution)/shard_map/ppermute | solution.py:34
  50.2 8.1 %collective-permute-start.13 = (bf16[152,768]{1,0:T(8,128)(2,1)S(1)}, bf16[152,768]{1,0:T(8,128)(2,1)S(1)}, u32[]{:S(2)}, u32[]{:S(2)}) collective-permute-start(bf16[152,768]{1,0:T(8,128)(2,1)S(1)} %get-tuple-element.67), channel_id=1, source_target_pairs={{0,1},{1,0},{2,3},{3,2},{4,5},{5,4},{6,7},{7,6},{8,9},{9,8},{10,11... | collective-permute-start | bytes 700424 | tf_op jit(solution)/shard_map/ppermute | solution.py:202
  54.1 8.4 %collective-permute-start.12 = (bf16[152,640]{1,0:T(8,128)(2,1)S(1)}, bf16[152,640]{1,0:T(8,128)(2,1)S(1)}, u32[]{:S(2)}, u32[]{:S(2)}) collective-permute-start(bf16[152,640]{1,0:T(8,128)(2,1)S(1)} %get-tuple-element.66), channel_id=1, source_target_pairs={{0,1},{1,0},{2,3},{3,2},{4,5},{5,4},{6,7},{7,6},{8,9},{9,8},{10,11... | collective-permute-start | bytes 583688 | tf_op jit(solution)/shard_map/ppermute | solution.py:202
  55.9 9.7 %collective-permute-start.16 = (bf16[152,640]{1,0:T(8,128)(2,1)S(1)}, bf16[152,640]{1,0:T(8,128)(2,1)S(1)}, u32[]{:S(2)}, u32[]{:S(2)}) collective-permute-start(bf16[152,640]{1,0:T(8,128)(2,1)S(1)} %get-tuple-element.68.refs_6_), channel_id=1, source_target_pairs={{4,8},{12,16},{20,24},{28,0},{8,4},{16,12},{24,20},{0,28},{5,9},{1... | collective-permute-start | bytes 583688 | tf_op jit(solution)/shard_map/ppermute | solution.py:34
  58.7 9.4 %collective-permute-start.17 = (bf16[152,768]{1,0:T(8,128)(2,1)S(1)}, bf16[152,768]{1,0:T(8,128)(2,1)S(1)}, u32[]{:S(2)}, u32[]{:S(2)}) collective-permute-start(bf16[152,768]{1,0:T(8,128)(2,1)S(1)} %get-tuple-element.69.refs_3_.refs_6_), channel_id=1, source_target_pairs={{4,8},{12,16},{20,24},{28,0},{8,4},{16,12},{24,20},{0,28},{5,9},{1... | collective-permute-start | bytes 700424 | tf_op jit(solution)/shard_map/ppermute | solution.py:34
  61.5 6.7 %collective-permute-start.18 = (f32[152,2048]{1,0:T(8,128)S(1)}, f32[152,2048]{1,0:T(8,128)S(1)}, u32[]{:S(2)}, u32[]{:S(2)}) collective-permute-start(f32[152,2048]{1,0:T(8,128)S(1)} %join.1.refs_3_), channel_id=1, source_target_pairs={{0,4},{8,12},{16,20},{24,28},{4,0},{12,8},{20,16},{28,24},{1,5},{9... | collective-permute-start | bytes 3735560 | tf_op jit(solution)/shard_map/ppermute | solution.py:34
  62.9 9.4 %collective-permute-start.15 = (bf16[152,640]{1,0:T(8,128)(2,1)S(1)}, bf16[152,640]{1,0:T(8,128)(2,1)S(1)}, u32[]{:S(2)}, u32[]{:S(2)}) collective-permute-start(bf16[152,640]{1,0:T(8,128)(2,1)S(1)} %get-tuple-element.72), channel_id=1, source_target_pairs={{4,8},{12,16},{20,24},{28,0},{8,4},{16,12},{24,20},{0,28},{5,9},{1... | collective-permute-start | bytes 583688 | tf_op jit(solution)/shard_map/ppermute | solution.py:34
  65.5 6.8 %collective-permute-start.19 = (f32[152,640]{1,0:T(8,128)S(1)}, f32[152,640]{1,0:T(8,128)S(1)}, u32[]{:S(2)}, u32[]{:S(2)}) collective-permute-start(f32[152,640]{1,0:T(8,128)S(1)} %get-tuple-element.71.refs_0_), channel_id=1, source_target_pairs={{0,4},{8,12},{16,20},{24,28},{4,0},{12,8},{20,16},{28,24},{1,5},{9... | collective-permute-start | bytes 1167368 | tf_op jit(solution)/shard_map/ppermute | solution.py:34

commit v8 on v7

--- a/solution.py
+++ b/solution.py
@@ -148,11 +148,15 @@
     )
 
 
-def pair_first(inner_x, inner_g, far_g, hidden, sent, *, scale):
-    size = inner_x.shape[0]
-    cut = sent.shape[1]
-    total = over_tokens(hidden[:, :size], inner_g[:, :cut])
-    total += over_tokens(hidden[:, size:], far_g[...])
+def ahead_forward(inner_x, far_x, pair_top, inner_g, hidden, swish, slope, down):
+    near_forward(inner_x, far_x, pair_top, hidden, swish, slope)
+    size, cut = inner_x.shape[0], down.shape[1]
+    down[...] = over_tokens(hidden[:, :size], inner_g[:, :cut])
+
+
+def pair_first(far_g, hidden, down, sent, *, scale):
+    size = far_g.shape[0]
+    total = down[...] + over_tokens(hidden[:, size:], far_g[...])
     sent[...] = (total * scale).astype(HALF)
 
 
@@ -248,10 +252,11 @@
         name="far_forward",
     )
     far_gs = [send(v, middle) for v in (pair_part, pair_more)]
-    hidden, swish, slope = call(
-        near_forward,
-        [array((units, 2 * size), t) for t in (HALF, FULL, FULL)],
-        (inner_x, far_x, pair_top),
+    hidden, swish, slope, down = call(
+        ahead_forward,
+        [array((units, 2 * size), t) for t in (HALF, FULL, FULL)]
+        + [array((units, cuts[0]), FULL)],
+        (inner_x, far_x, pair_top, inner_g),
         after=(pair_more,),
         flops=AHEAD_WORK,
         name="ahead_forward",
@@ -263,7 +268,7 @@
     first = call(
         functools.partial(pair_first, scale=scale),
         [array((units, sizes[0]), HALF)],
-        (inner_x, inner_g, far_gs[0], hidden),
+        (far_gs[0], hidden, down),
         name="pair_first",
     )[0]
     dgate, dupper = call(

time: 73.5 us -> 73.6 us (level)
  no operation moved by 1% of the time
where the time goes in v8:
time: 73.6 us; the launch traced here: 73.2 us
  starting transfers between devices  32.9 us (45%)
  waiting for transfers between devices  23.3 us (32%)
  Pallas kernels  12.2 us (17%)
  local copies, waits for them, and re-layouts  4.47 us (6%)
    ppermute x13, starting transfers between devices, send(): return lax.ppermute(block, 'tp', route)  25.7 us
    ppermute x13, waiting for transfers between devices, send(): return lax.ppermute(block, 'tp', route)  17.5 us
    pallas_call x19, Pallas kernels, call(): pl.pallas_call(body, out_shape=outs, in_specs=[pl.BlockSpec(memory_space=...  8.9 us
    ppermute x7, starting transfers between devices, neighbour(): return lax.ppermute(block, 'blk', route)  7.19 us
    ppermute x7, waiting for transfers between devices, neighbour(): return lax.ppermute(block, 'blk', route)  5.78 us
    unnamed x18, local copies, waits for them, and re-layouts  4.47 us
    pallas_call x2, Pallas kernels, finish(): pl.pallas_call(functools.partial(finish_kernel, pieces=pieces, bands=band...  1.92 us
  transfers between devices with their start and end apart: 20, of which 9 were waited for; matrix products, arithmetic and copies ran while one was open for 0% of the time, Pallas kernels for 16%

profile of v8, /device:TPU:0, one launch (start us, length us, event | category | flops | bytes accessed | tf_op | source)
XLA Modules:
  0.0 73.2 jit_solution(6367544203850648707)
XLA Ops:
  0.0 0.7 collective-permute-start.3
  0.7 5.9 %collective-permute-start = (bf16[256,896]{1,0:T(8,128)(2,1)}, bf16[256,896]{1,0:T(8,128)(2,1)S(1)}, u32[]{:S(2)}, u32[]{:S(2)}) collective-permute-start(bf16[256,896]{1,0:T(8,128)(2,1)} %refs_0_.3), channel_id=1, source_target_pairs={{0,1},{1,0},{2,3},{3,2},{4,5},{5,4},{6,7},{7,6},{8,9},{9,8},{10,11... | collective-permute-start | bytes 1376264 | tf_op jit(solution)/shard_map/ppermute | solution.py:206
  6.6 0.7 collective-permute-start.5
  7.3 1.1 %copy-done = bf16[1,152,3,896]{3,1,2,0:T(8,128)(2,1)S(1)} copy-done((bf16[1,152,3,896]{3,1,2,0:T(8,128)(2,1)S(1)}, bf16[1,152,3,896]{3,1,2,0:T(8,128)(2,1)}, u32[]{:S(2)}) %copy-start) | copy-done | bytes 817176
  8.4 1.1 %copy-done.2 = bf16[1,152,3,896]{3,1,2,0:T(8,128)(2,1)S(1)} copy-done((bf16[1,152,3,896]{3,1,2,0:T(8,128)(2,1)S(1)}, bf16[1,152,3,896]{3,1,2,0:T(8,128)(2,1)}, u32[]{:S(2)}) %copy-start.2) | copy-done | bytes 817176
  9.5 1.1 %copy-done.4 = bf16[1,152,3,896]{3,1,2,0:T(8,128)(2,1)S(1)} copy-done((bf16[1,152,3,896]{3,1,2,0:T(8,128)(2,1)S(1)}, bf16[1,152,3,896]{3,1,2,0:T(8,128)(2,1)}, u32[]{:S(2)}) %copy-start.4) | copy-done | bytes 817176
  10.7 1.0 %copy-done.6 = bf16[256,896]{1,0:T(8,128)(2,1)S(1)} copy-done((bf16[256,896]{1,0:T(8,128)(2,1)S(1)}, bf16[256,896]{1,0:T(8,128)(2,1)}, u32[]{:S(2)}) %copy-start.6) | copy-done | bytes 458776
  11.7 1.4 %still.1 = (f32[3,152,896]{2,1,0:T(8,128)S(1)}, f32[3,152,896]{2,1,0:T(8,128)S(1)}, bf16[256,896]{1,0:T(8,128)(2,1)S(1)}) custom-call(bf16[3,152,896]{2,1,0:T(8,128)(2,1)S(1)} %bitcast.12, bf16[3,152,896]{2,1,0:T(8,128)(2,1)S(1)} %bitcast.19, bf16[3,152,896]{2,1,0:T(8,128)(2,1)S(1)} %bitcast.24, bf16[256,896]{1,0:T(8,128)(2,1)S(1)} %copy-done.6), custom_call_target="tpu_custom_call" | custom-call | tf_op jit(solution)/shard_map/still/pallas_call | solution.py:329
  13.1 1.8 %collective-permute-start.2 = (bf16[256,896]{1,0:T(8,128)(2,1)S(1)}, bf16[256,896]{1,0:T(8,128)(2,1)S(1)}, u32[]{:S(2)}, u32[]{:S(2)}) collective-permute-start(bf16[256,896]{1,0:T(8,128)(2,1)S(1)} %get-tuple-element.42), channel_id=1, source_target_pairs={{0,1},{1,0},{2,3},{3,2},{4,5},{5,4},{6,7},{7,6},{8,9},{9,8},{10,11... | collective-permute-start | bytes 1376264 | tf_op jit(solution)/shard_map/ppermute | solution.py:206
  14.9 1.0 %collective-permute-start.11 = (f32[3,152,896]{2,1,0:T(8,128)S(1)}, f32[3,152,896]{2,1,0:T(8,128)S(1)}, u32[]{:S(2)}, u32[]{:S(2)}) collective-permute-start(f32[3,152,896]{2,1,0:T(8,128)S(1)} %get-tuple-element.43.refs_3_.refs_1_), channel_id=1, source_target_pairs={{4,8},{12,16},{20,24},{28,0},{8,4},{16,12},{24,20},{0,28},{5,9},{1... | collective-permute-start | bytes 4902920 | tf_op jit(solution)/shard_map/ppermute | solution.py:34
  15.9 0.8 %near_forward.1 = (bf16[152,512]{1,0:T(8,128)(2,1)S(1)}, f32[152,512]{1,0:T(8,128)S(1)}, f32[152,512]{1,0:T(8,128)S(1)}, bf16[2,152,896]{2,1,0:T(8,128)(2,1)S(1)}) custom-call(bf16[256,896]{1,0:T(8,128)(2,1)S(1)} %copy-done.8, bf16[256,896]{1,0:T(8,128)(2,1)S(1)} %collective-permute-done.3.refs_1_.refs_0_, bf16[3,152,896]{2,1,0:T(8,128)(2,1)S(1)} %bitcast.13, ...), custom_call_target="tpu_custom_call" | custom-call | flops 5000000000 | tf_op jit(solution)/shard_map/near_forward/pallas_call | solution.py:82
  16.8 2.7 %collective-permute-start.8 = (bf16[2,152,896]{2,1,0:T(8,128)(2,1)S(1)}, bf16[2,152,896]{2,1,0:T(8,128)(2,1)S(1)}, u32[]{:S(2)}, u32[]{:S(2)}) collective-permute-start(bf16[2,152,896]{2,1,0:T(8,128)(2,1)S(1)} %get-tuple-element.56), channel_id=1, source_target_pairs={{0,1},{1,0},{2,3},{3,2},{4,5},{5,4},{6,7},{7,6},{8,9},{9,8},{10,11... | collective-permute-start | bytes 1634312 | tf_op jit(solution)/shard_map/ppermute | solution.py:206
  19.4 0.7 collective-permute-start.1
  20.1 0.5 pair_forward.1
  20.6 7.4 %collective-permute-done.2.refs_0_.refs_5_.refs_2_ = bf16[256,896]{1,0:T(8,128)(2,1)S(1)} collective-permute-done((bf16[256,896]{1,0:T(8,128)(2,1)S(1)}, bf16[256,896]{1,0:T(8,128)(2,1)S(1)}, u32[]{:S(2)}, u32[]{:S(2)}) %collective-permute-start.2) | collective-permute-done | bytes 458784 | tf_op jit(solution)/shard_map/ppermute | solution.py:206
  28.0 2.1 %collective-permute-start.7 = (bf16[152,896]{1,0:T(8,128)(2,1)S(1)}, bf16[152,896]{1,0:T(8,128)(2,1)S(1)}, u32[]{:S(2)}, u32[]{:S(2)}) collective-permute-start(bf16[152,896]{1,0:T(8,128)(2,1)S(1)} %get-tuple-element.55), channel_id=1, source_target_pairs={{0,1},{1,0},{2,3},{3,2},{4,5},{5,4},{6,7},{7,6},{8,9},{9,8},{10,11... | collective-permute-start | bytes 817160 | tf_op jit(solution)/shard_map/ppermute | solution.py:206
  30.2 0.7 collective-permute-start.4
  30.9 1.8 %near_backward.1.refs_3_.refs_7_ = f32[3,152,896]{2,1,0:T(8,128)S(1)} custom-call(bf16[256,896]{1,0:T(8,128)(2,1)S(1)} %copy-done.8, bf16[256,896]{1,0:T(8,128)(2,1)S(1)} %collective-permute-done.3.refs_1_.refs_0_, bf16[256,896]{1,0:T(8,128)(2,1)S(1)} %collective-permute-done.refs_0_.refs_2_, bf16[256,896]{1,0:T(8,128)(2,1)S(1)} %copy-done.7, ...), custom_call_target="tpu_custom_call" | custom-call | tf_op jit(solution)/shard_map/near_backward/pallas_call | solution.py:82
  32.7 0.5 far_forward.1
  33.2 0.7 collective-permute-start.6
  33.9 5.8 %collective-permute-done.8.refs_2_ = bf16[2,152,896]{2,1,0:T(8,128)(2,1)S(1)} collective-permute-done((bf16[2,152,896]{2,1,0:T(8,128)(2,1)S(1)}, bf16[2,152,896]{2,1,0:T(8,128)(2,1)S(1)}, u32[]{:S(2)}, u32[]{:S(2)}) %collective-permute-start.8) | collective-permute-done | bytes 544800 | tf_op jit(solution)/shard_map/ppermute | solution.py:206
  39.7 0.8 %ahead_forward.1 = (bf16[152,512]{1,0:T(8,128)(2,1)S(1)}, f32[152,512]{1,0:T(8,128)S(1)}, f32[152,512]{1,0:T(8,128)S(1)}, f32[152,640]{1,0:T(8,128)S(1)}) custom-call(bf16[256,896]{1,0:T(8,128)(2,1)S(1)} %collective-permute-done.3.refs_1_.refs_0_, bf16[256,896]{1,0:T(8,128)(2,1)S(1)} %collective-permute-done.1.refs_0_.refs_1_, ...), custom_call_target="tpu_custom_call" | custom-call | flops 20000000000 | tf_op jit(solution)/shard_map/ahead_forward/pallas_call | solution.py:82
  40.5 0.2 pair_first.1.refs_4_
  40.7 4.8 %collective-permute-start.10 = (bf16[152,640]{1,0:T(8,128)(2,1)S(1)}, bf16[152,640]{1,0:T(8,128)(2,1)S(1)}, u32[]{:S(2)}, u32[]{:S(2)}) collective-permute-start(bf16[152,640]{1,0:T(8,128)(2,1)S(1)} %pair_first.1.refs_4_), channel_id=1, source_target_pairs={{0,1},{1,0},{2,3},{3,2},{4,5},{5,4},{6,7},{7,6},{8,9},{9,8},{10,11... | collective-permute-start | bytes 583688 | tf_op jit(solution)/shard_map/ppermute | solution.py:206
  45.5 0.3 ahead_backward.1
  45.9 0.9 %far_backward.1.refs_11_.refs_0_ = f32[3,152,896]{2,1,0:T(8,128)S(1)} custom-call(bf16[256,896]{1,0:T(8,128)(2,1)S(1)} %collective-permute-done.1.refs_0_.refs_1_, bf16[256,640]{1,0:T(8,128)(2,1)S(1)} %collective-permute-done.4.refs_0_.refs_1_.refs_3_, bf16[256,256]{1,0:T(8,128)(2,1)S(1)} %collective-permute-done.6.refs_2_.refs_4_, ...), custom_call_target="tpu_custom_call" | custom-call | tf_op jit(solution)/shard_map/far_backward/pallas_call | solution.py:82
  46.8 0.9 %pair_rest.1 = (bf16[152,640]{1,0:T(8,128)(2,1)S(1)}, bf16[152,768]{1,0:T(8,128)(2,1)S(1)}, bf16[152,640]{1,0:T(8,128)(2,1)S(1)}) custom-call(bf16[256,896]{1,0:T(8,128)(2,1)S(1)} %collective-permute-done.3.refs_1_.refs_0_, bf16[256,896]{1,0:T(8,128)(2,1)S(1)} %collective-permute-done.1.refs_0_.refs_1_, ...), custom_call_target="tpu_custom_call" | custom-call | tf_op jit(solution)/shard_map/pair_rest/pallas_call | solution.py:82
  47.8 1.1 %collective-permute-start.9 = (bf16[152,640]{1,0:T(8,128)(2,1)S(1)}, bf16[152,640]{1,0:T(8,128)(2,1)S(1)}, u32[]{:S(2)}, u32[]{:S(2)}) collective-permute-start(bf16[152,640]{1,0:T(8,128)(2,1)S(1)} %get-tuple-element.64), channel_id=1, source_target_pairs={{0,1},{1,0},{2,3},{3,2},{4,5},{5,4},{6,7},{7,6},{8,9},{9,8},{10,11... | collective-permute-start | bytes 583688 | tf_op jit(solution)/shard_map/ppermute | solution.py:206
  48.8 0.7 collective-permute-done.10.refs_5_
  49.6 0.4 change.4
  50.0 0.1 collective-permute-start.14
  50.1 2.4 %collective-permute-start.13 = (bf16[152,768]{1,0:T(8,128)(2,1)S(1)}, bf16[152,768]{1,0:T(8,128)(2,1)S(1)}, u32[]{:S(2)}, u32[]{:S(2)}) collective-permute-start(bf16[152,768]{1,0:T(8,128)(2,1)S(1)} %get-tuple-element.69), channel_id=1, source_target_pairs={{0,1},{1,0},{2,3},{3,2},{4,5},{5,4},{6,7},{7,6},{8,9},{9,8},{10,11... | collective-permute-start | bytes 700424 | tf_op jit(solution)/shard_map/ppermute | solution.py:206
  52.4 1.1 %collective-permute-done.9.refs_5_ = bf16[152,640]{1,0:T(8,128)(2,1)S(1)} collective-permute-done((bf16[152,640]{1,0:T(8,128)(2,1)S(1)}, bf16[152,640]{1,0:T(8,128)(2,1)S(1)}, u32[]{:S(2)}, u32[]{:S(2)}) %collective-permute-start.9) | collective-permute-done | bytes 194592 | tf_op jit(solution)/shard_map/ppermute | solution.py:206
  53.5 0.2 collective-permute-done.11.refs_8_.refs_1_
  53.7 0.4 change.5
  54.1 1.7 %collective-permute-start.12 = (bf16[152,640]{1,0:T(8,128)(2,1)S(1)}, bf16[152,640]{1,0:T(8,128)(2,1)S(1)}, u32[]{:S(2)}, u32[]{:S(2)}) collective-permute-start(bf16[152,640]{1,0:T(8,128)(2,1)S(1)} %get-tuple-element.68), channel_id=1, source_target_pairs={{0,1},{1,0},{2,3},{3,2},{4,5},{5,4},{6,7},{7,6},{8,9},{9,8},{10,11... | collective-permute-start | bytes 583688 | tf_op jit(solution)/shard_map/ppermute | solution.py:206
  55.8 0.6 collective-permute-start.16
  56.3 1.8 %collective-permute-done.13.refs_5_ = bf16[152,768]{1,0:T(8,128)(2,1)S(1)} collective-permute-done((bf16[152,768]{1,0:T(8,128)(2,1)S(1)}, bf16[152,768]{1,0:T(8,128)(2,1)S(1)}, u32[]{:S(2)}, u32[]{:S(2)}) %collective-permute-start.13) | collective-permute-done | bytes 233504 | tf_op jit(solution)/shard_map/ppermute | solution.py:206
  58.2 0.4 change.6
  58.6 2.7 %collective-permute-start.17 = (bf16[152,768]{1,0:T(8,128)(2,1)S(1)}, bf16[152,768]{1,0:T(8,128)(2,1)S(1)}, u32[]{:S(2)}, u32[]{:S(2)}) collective-permute-start(bf16[152,768]{1,0:T(8,128)(2,1)S(1)} %get-tuple-element.71.refs_3_.refs_6_), channel_id=1, source_target_pairs={{4,8},{12,16},{20,24},{28,0},{8,4},{16,12},{24,20},{0,28},{5,9},{1... | collective-permute-start | bytes 700424 | tf_op jit(solution)/shard_map/ppermute | solution.py:34
  61.6 0.8 %collective-permute-done.12.refs_5_ = bf16[152,640]{1,0:T(8,128)(2,1)S(1)} collective-permute-done((bf16[152,640]{1,0:T(8,128)(2,1)S(1)}, bf16[152,640]{1,0:T(8,128)(2,1)S(1)}, u32[]{:S(2)}, u32[]{:S(2)}) %collective-permute-start.12) | collective-permute-done | bytes 194592 | tf_op jit(solution)/shard_map/ppermute | solution.py:206
  62.3 0.4 change.7
  62.7 2.7 %collective-permute-start.15 = (bf16[152,640]{1,0:T(8,128)(2,1)S(1)}, bf16[152,640]{1,0:T(8,128)(2,1)S(1)}, u32[]{:S(2)}, u32[]{:S(2)}) collective-permute-start(bf16[152,640]{1,0:T(8,128)(2,1)S(1)} %get-tuple-element.74), channel_id=1, source_target_pairs={{4,8},{12,16},{20,24},{28,0},{8,4},{16,12},{24,20},{0,28},{5,9},{1... | collective-permute-start | bytes 583688 | tf_op jit(solution)/shard_map/ppermute | solution.py:34
  65.5 2.6 %collective-permute-done.17.refs_2_ = bf16[152,768]{1,0:T(8,128)(2,1)S(1)} collective-permute-done((bf16[152,768]{1,0:T(8,128)(2,1)S(1)}, bf16[152,768]{1,0:T(8,128)(2,1)S(1)}, u32[]{:S(2)}, u32[]{:S(2)}) %collective-permute-start.17) | collective-permute-done | bytes 233504 | tf_op jit(solution)/shard_map/ppermute | solution.py:34
  68.1 0.1 across.6.refs_2_
  68.2 1.1 %finish.2 = (f32[3,152,896]{2,1,0:T(8,128)}, f32[8,128]{1,0:T(8,128)S(1)}) custom-call(f32[152,640]{1,0:T(8,128)S(1)} %across.4.refs_7_.refs_4_.refs_0_, f32[152,640]{1,0:T(8,128)S(1)} %across.5.refs_4_.refs_1_, f32[152,768]{1,0:T(8,128)S(1)} %across.6.refs_2_, f32[152,2048]{1,0:T(8,128)S(1)} %collective-permute-done.18.refs_3_), custom_call_target="tpu_custom_call" | custom-call | tf_op jit(solution)/shard_map/finish/pallas_call | solution.py:433
  69.4 2.9 %collective-permute-done.15.refs_2_ = bf16[152,640]{1,0:T(8,128)(2,1)S(1)} collective-permute-done((bf16[152,640]{1,0:T(8,128)(2,1)S(1)}, bf16[152,640]{1,0:T(8,128)(2,1)S(1)}, u32[]{:S(2)}, u32[]{:S(2)}) %collective-permute-start.15) | collective-permute-done | bytes 194592 | tf_op jit(solution)/shard_map/ppermute | solution.py:34
  72.4 0.8 %finish.3 = f32[3,152,896]{2,1,0:T(8,128)} custom-call(f32[152,640]{1,0:T(8,128)S(1)} %across.7.refs_0_, f32[152,640]{1,0:T(8,128)S(1)} %collective-permute-done.19.refs_1_, f32[3,152,896]{2,1,0:T(8,128)} %get-tuple-element.78.refs_2_), custom_call_target="tpu_custom_call", output_to_operand_aliasing={{}: (2, {})} | custom-call | tf_op jit(solution)/shard_map/finish/pallas_call | solution.py:433
  (32 shorter events, 0.5 us)
Async XLA Ops:
  0.0 15.9 %collective-permute-start.3 = (bf16[256,896]{1,0:T(8,128)(2,1)}, bf16[256,896]{1,0:T(8,128)(2,1)S(1)}, u32[]{:S(2)}, u32[]{:S(2)}) collective-permute-start(bf16[256,896]{1,0:T(8,128)(2,1)} %refs_0_.3), channel_id=1, source_target_pairs={{1,2},{2,1},{5,6},{6,5},{9,10},{10,9},{13,14},{14,13},{17,18},{18,... | collective-permute-start | bytes 1376264 | tf_op jit(solution)/shard_map/ppermute | solution.py:206
  0.7 18.7 %collective-permute-start = (bf16[256,896]{1,0:T(8,128)(2,1)}, bf16[256,896]{1,0:T(8,128)(2,1)S(1)}, u32[]{:S(2)}, u32[]{:S(2)}) collective-permute-start(bf16[256,896]{1,0:T(8,128)(2,1)} %refs_0_.3), channel_id=1, source_target_pairs={{0,1},{1,0},{2,3},{3,2},{4,5},{5,4},{6,7},{7,6},{8,9},{9,8},{10,11... | collective-permute-start | bytes 1376264 | tf_op jit(solution)/shard_map/ppermute | solution.py:206
  6.6 23.6 %collective-permute-start.5 = (bf16[256,896]{1,0:T(8,128)(2,1)}, bf16[256,896]{1,0:T(8,128)(2,1)S(1)}, u32[]{:S(2)}, u32[]{:S(2)}) collective-permute-start(bf16[256,896]{1,0:T(8,128)(2,1)} %refs_3_.1), channel_id=1, source_target_pairs={{1,2},{2,1},{5,6},{6,5},{9,10},{10,9},{13,14},{14,13},{17,18},{18,... | collective-permute-start | bytes 1376264 | tf_op jit(solution)/shard_map/ppermute | solution.py:206
  7.3 1.1 %copy-start = (bf16[1,152,3,896]{3,1,2,0:T(8,128)(2,1)S(1)}, bf16[1,152,3,896]{3,1,2,0:T(8,128)(2,1)}, u32[]{:S(2)}) copy-start(bf16[1,152,3,896]{3,1,2,0:T(8,128)(2,1)} %param.7) | copy-start | bytes 2451460
  8.4 1.1 %copy-start.2 = (bf16[1,152,3,896]{3,1,2,0:T(8,128)(2,1)S(1)}, bf16[1,152,3,896]{3,1,2,0:T(8,128)(2,1)}, u32[]{:S(2)}) copy-start(bf16[1,152,3,896]{3,1,2,0:T(8,128)(2,1)} %param.8) | copy-start | bytes 2451460
  9.5 1.1 %copy-start.4 = (bf16[1,152,3,896]{3,1,2,0:T(8,128)(2,1)S(1)}, bf16[1,152,3,896]{3,1,2,0:T(8,128)(2,1)}, u32[]{:S(2)}) copy-start(bf16[1,152,3,896]{3,1,2,0:T(8,128)(2,1)} %param.9) | copy-start | bytes 2451460
  10.7 1.0 %copy-start.6 = (bf16[256,896]{1,0:T(8,128)(2,1)S(1)}, bf16[256,896]{1,0:T(8,128)(2,1)}, u32[]{:S(2)}) copy-start(bf16[256,896]{1,0:T(8,128)(2,1)} %refs_3_.1) | copy-start | bytes 1376260
  11.7 4.2 %copy-start.8 = (bf16[256,896]{1,0:T(8,128)(2,1)S(1)}, bf16[256,896]{1,0:T(8,128)(2,1)}, u32[]{:S(2)}) copy-start(bf16[256,896]{1,0:T(8,128)(2,1)} %refs_0_.3) | copy-start | bytes 1376260
  13.1 14.9 %collective-permute-start.2 = (bf16[256,896]{1,0:T(8,128)(2,1)S(1)}, bf16[256,896]{1,0:T(8,128)(2,1)S(1)}, u32[]{:S(2)}, u32[]{:S(2)}) collective-permute-start(bf16[256,896]{1,0:T(8,128)(2,1)S(1)} %get-tuple-element.42), channel_id=1, source_target_pairs={{0,1},{1,0},{2,3},{3,2},{4,5},{5,4},{6,7},{7,6},{8,9},{9,8},{10,11... | collective-permute-start | bytes 1376264 | tf_op jit(solution)/shard_map/ppermute | solution.py:206
  14.9 38.8 %collective-permute-start.11 = (f32[3,152,896]{2,1,0:T(8,128)S(1)}, f32[3,152,896]{2,1,0:T(8,128)S(1)}, u32[]{:S(2)}, u32[]{:S(2)}) collective-permute-start(f32[3,152,896]{2,1,0:T(8,128)S(1)} %get-tuple-element.43.refs_3_.refs_1_), channel_id=1, source_target_pairs={{4,8},{12,16},{20,24},{28,0},{8,4},{16,12},{24,20},{0,28},{5,9},{1... | collective-permute-start | bytes 4902920 | tf_op jit(solution)/shard_map/ppermute | solution.py:34
  16.8 22.9 %collective-permute-start.8 = (bf16[2,152,896]{2,1,0:T(8,128)(2,1)S(1)}, bf16[2,152,896]{2,1,0:T(8,128)(2,1)S(1)}, u32[]{:S(2)}, u32[]{:S(2)}) collective-permute-start(bf16[2,152,896]{2,1,0:T(8,128)(2,1)S(1)} %get-tuple-element.56), channel_id=1, source_target_pairs={{0,1},{1,0},{2,3},{3,2},{4,5},{5,4},{6,7},{7,6},{8,9},{9,8},{10,11... | collective-permute-start | bytes 1634312 | tf_op jit(solution)/shard_map/ppermute | solution.py:206
  19.4 13.3 %collective-permute-start.1 = (bf16[256,896]{1,0:T(8,128)(2,1)S(1)}, bf16[256,896]{1,0:T(8,128)(2,1)S(1)}, u32[]{:S(2)}, u32[]{:S(2)}) collective-permute-start(bf16[256,896]{1,0:T(8,128)(2,1)S(1)} %collective-permute-done.refs_0_.refs_2_), channel_id=1, source_target_pairs={{1,2},{2,1},{5,6},{6,5},{9,10},{10,9},{13,14},{14,13},{17,18},{18,... | collective-permute-start | bytes 1376264 | tf_op jit(solution)/shard_map/ppermute | solution.py:206
  20.6 10.2 %copy-start.7 = (bf16[256,896]{1,0:T(8,128)(2,1)S(1)}, bf16[256,896]{1,0:T(8,128)(2,1)}, u32[]{:S(2)}) copy-start(bf16[256,896]{1,0:T(8,128)(2,1)} %refs_3_.1) | copy-start | bytes 1376260
  28.0 17.5 %collective-permute-start.7 = (bf16[152,896]{1,0:T(8,128)(2,1)S(1)}, bf16[152,896]{1,0:T(8,128)(2,1)S(1)}, u32[]{:S(2)}, u32[]{:S(2)}) collective-permute-start(bf16[152,896]{1,0:T(8,128)(2,1)S(1)} %get-tuple-element.55), channel_id=1, source_target_pairs={{0,1},{1,0},{2,3},{3,2},{4,5},{5,4},{6,7},{7,6},{8,9},{9,8},{10,11... | collective-permute-start | bytes 817160 | tf_op jit(solution)/shard_map/ppermute | solution.py:206
  30.2 10.3 %collective-permute-start.4 = (bf16[256,640]{1,0:T(8,128)(2,1)S(1)}, bf16[256,640]{1,0:T(8,128)(2,1)S(1)}, u32[]{:S(2)}, u32[]{:S(2)}) collective-permute-start(bf16[256,640]{1,0:T(8,128)(2,1)S(1)} %get-tuple-element.46.refs_13_), channel_id=1, source_target_pairs={{1,2},{2,1},{5,6},{6,5},{9,10},{10,9},{13,14},{14,13},{17,18},{18,... | collective-permute-start | bytes 983048 | tf_op jit(solution)/shard_map/ppermute | solution.py:206
  33.2 12.6 %collective-permute-start.6 = (bf16[256,256]{1,0:T(8,128)(2,1)S(1)}, bf16[256,256]{1,0:T(8,128)(2,1)S(1)}, u32[]{:S(2)}, u32[]{:S(2)}) collective-permute-start(bf16[256,256]{1,0:T(8,128)(2,1)S(1)} %get-tuple-element.51.refs_4_), channel_id=1, source_target_pairs={{1,2},{2,1},{5,6},{6,5},{9,10},{10,9},{13,14},{14,13},{17,18},{18,... | collective-permute-start | bytes 393224 | tf_op jit(solution)/shard_map/ppermute | solution.py:206
  40.5 5.3 %copy-start.1 = (bf16[1,152,3,896]{3,1,2,0:T(8,128)(2,1)S(1)}, bf16[1,152,3,896]{3,1,2,0:T(8,128)(2,1)}, u32[]{:S(2)}) copy-start(bf16[1,152,3,896]{3,1,2,0:T(8,128)(2,1)} %param.7) | copy-start | bytes 2451460
  40.7 8.8 %collective-permute-start.10 = (bf16[152,640]{1,0:T(8,128)(2,1)S(1)}, bf16[152,640]{1,0:T(8,128)(2,1)S(1)}, u32[]{:S(2)}, u32[]{:S(2)}) collective-permute-start(bf16[152,640]{1,0:T(8,128)(2,1)S(1)} %pair_first.1.refs_4_), channel_id=1, source_target_pairs={{0,1},{1,0},{2,3},{3,2},{4,5},{5,4},{6,7},{7,6},{8,9},{9,8},{10,11... | collective-permute-start | bytes 583688 | tf_op jit(solution)/shard_map/ppermute | solution.py:206
  46.8 2.8 %copy-start.3 = (bf16[1,152,3,896]{3,1,2,0:T(8,128)(2,1)S(1)}, bf16[1,152,3,896]{3,1,2,0:T(8,128)(2,1)}, u32[]{:S(2)}) copy-start(bf16[1,152,3,896]{3,1,2,0:T(8,128)(2,1)} %param.8) | copy-start | bytes 2451460
  46.8 2.8 %copy-start.5 = (bf16[1,152,3,896]{3,1,2,0:T(8,128)(2,1)S(1)}, bf16[1,152,3,896]{3,1,2,0:T(8,128)(2,1)}, u32[]{:S(2)}) copy-start(bf16[1,152,3,896]{3,1,2,0:T(8,128)(2,1)} %param.9) | copy-start | bytes 2451460
  47.8 5.7 %collective-permute-start.9 = (bf16[152,640]{1,0:T(8,128)(2,1)S(1)}, bf16[152,640]{1,0:T(8,128)(2,1)S(1)}, u32[]{:S(2)}, u32[]{:S(2)}) collective-permute-start(bf16[152,640]{1,0:T(8,128)(2,1)S(1)} %get-tuple-element.64), channel_id=1, source_target_pairs={{0,1},{1,0},{2,3},{3,2},{4,5},{5,4},{6,7},{7,6},{8,9},{9,8},{10,11... | collective-permute-start | bytes 583688 | tf_op jit(solution)/shard_map/ppermute | solution.py:206
  50.0 11.5 %collective-permute-start.14 = (bf16[152,640]{1,0:T(8,128)(2,1)S(1)}, bf16[152,640]{1,0:T(8,128)(2,1)S(1)}, u32[]{:S(2)}, u32[]{:S(2)}) collective-permute-start(bf16[152,640]{1,0:T(8,128)(2,1)S(1)} %get-tuple-element.67.refs_7_), channel_id=1, source_target_pairs={{4,8},{12,16},{20,24},{28,0},{8,4},{16,12},{24,20},{0,28},{5,9},{1... | collective-permute-start | bytes 583688 | tf_op jit(solution)/shard_map/ppermute | solution.py:34
  50.1 8.1 %collective-permute-start.13 = (bf16[152,768]{1,0:T(8,128)(2,1)S(1)}, bf16[152,768]{1,0:T(8,128)(2,1)S(1)}, u32[]{:S(2)}, u32[]{:S(2)}) collective-permute-start(bf16[152,768]{1,0:T(8,128)(2,1)S(1)} %get-tuple-element.69), channel_id=1, source_target_pairs={{0,1},{1,0},{2,3},{3,2},{4,5},{5,4},{6,7},{7,6},{8,9},{9,8},{10,11... | collective-permute-start | bytes 700424 | tf_op jit(solution)/shard_map/ppermute | solution.py:206
  54.1 8.3 %collective-permute-start.12 = (bf16[152,640]{1,0:T(8,128)(2,1)S(1)}, bf16[152,640]{1,0:T(8,128)(2,1)S(1)}, u32[]{:S(2)}, u32[]{:S(2)}) collective-permute-start(bf16[152,640]{1,0:T(8,128)(2,1)S(1)} %get-tuple-element.68), channel_id=1, source_target_pairs={{0,1},{1,0},{2,3},{3,2},{4,5},{5,4},{6,7},{7,6},{8,9},{9,8},{10,11... | collective-permute-start | bytes 583688 | tf_op jit(solution)/shard_map/ppermute | solution.py:206
  55.8 9.6 %collective-permute-start.16 = (bf16[152,640]{1,0:T(8,128)(2,1)S(1)}, bf16[152,640]{1,0:T(8,128)(2,1)S(1)}, u32[]{:S(2)}, u32[]{:S(2)}) collective-permute-start(bf16[152,640]{1,0:T(8,128)(2,1)S(1)} %get-tuple-element.70.refs_6_), channel_id=1, source_target_pairs={{4,8},{12,16},{20,24},{28,0},{8,4},{16,12},{24,20},{0,28},{5,9},{1... | collective-permute-start | bytes 583688 | tf_op jit(solution)/shard_map/ppermute | solution.py:34
  58.6 9.5 %collective-permute-start.17 = (bf16[152,768]{1,0:T(8,128)(2,1)S(1)}, bf16[152,768]{1,0:T(8,128)(2,1)S(1)}, u32[]{:S(2)}, u32[]{:S(2)}) collective-permute-start(bf16[152,768]{1,0:T(8,128)(2,1)S(1)} %get-tuple-element.71.refs_3_.refs_6_), channel_id=1, source_target_pairs={{4,8},{12,16},{20,24},{28,0},{8,4},{16,12},{24,20},{0,28},{5,9},{1... | collective-permute-start | bytes 700424 | tf_op jit(solution)/shard_map/ppermute | solution.py:34
  61.4 6.8 %collective-permute-start.18 = (f32[152,2048]{1,0:T(8,128)S(1)}, f32[152,2048]{1,0:T(8,128)S(1)}, u32[]{:S(2)}, u32[]{:S(2)}) collective-permute-start(f32[152,2048]{1,0:T(8,128)S(1)} %join.1.refs_3_), channel_id=1, source_target_pairs={{0,4},{8,12},{16,20},{24,28},{4,0},{12,8},{20,16},{28,24},{1,5},{9... | collective-permute-start | bytes 3735560 | tf_op jit(solution)/shard_map/ppermute | solution.py:34
  62.7 9.6 %collective-permute-start.15 = (bf16[152,640]{1,0:T(8,128)(2,1)S(1)}, bf16[152,640]{1,0:T(8,128)(2,1)S(1)}, u32[]{:S(2)}, u32[]{:S(2)}) collective-permute-start(bf16[152,640]{1,0:T(8,128)(2,1)S(1)} %get-tuple-element.74), channel_id=1, source_target_pairs={{4,8},{12,16},{20,24},{28,0},{8,4},{16,12},{24,20},{0,28},{5,9},{1... | collective-permute-start | bytes 583688 | tf_op jit(solution)/shard_map/ppermute | solution.py:34
  65.4 7.0 %collective-permute-start.19 = (f32[152,640]{1,0:T(8,128)S(1)}, f32[152,640]{1,0:T(8,128)S(1)}, u32[]{:S(2)}, u32[]{:S(2)}) collective-permute-start(f32[152,640]{1,0:T(8,128)S(1)} %get-tuple-element.73.refs_0_), channel_id=1, source_target_pairs={{0,4},{8,12},{16,20},{24,28},{4,0},{12,8},{20,16},{28,24},{1,5},{9... | collective-permute-start | bytes 1167368 | tf_op jit(solution)/shard_map/ppermute | solution.py:34
